TPU v7x, 32 devices: a whole 2x2x4 slice. The times are simulated.
32 devices in a mesh: lon: 8 (over y, x, core), lev: 4 (over z).
Axes of the slice: x: 2, y: 2, z: 4, core: 2. Of those that a mesh axis runs over, the one named last changes fastest.
Arguments:
- thickness: float32 [4, 128, 2048], P('lev', 'lon'), may hold values from 0.5 to 1.5
- wind_field: float32 [2, 4, 128, 2048], P(None, 'lev', 'lon'), may hold values from -3 to 3
Outputs:
- new_thickness: float32 [4, 128, 2048], P('lev', 'lon')
- new_winds: float32 [2, 4, 128, 2048], P(None, 'lev', 'lon')
All inputs are finite; a program needn't handle non-finite values.
Results may differ from a plain program's by a relative error of at most 0.0001.
Values sent between devices are 32-bit elements; how exact they have to be, the bound alone decides.
No kernel may reach another device: no remote copies, remote signals or barrier semaphores. Data moves between devices by JAX's collectives and lax.ppermute only.
A program may use at most 64 MiB of HBM per device.

v0:
```python
import math

import jax
import jax.numpy as jnp
from jax import lax
from jax.sharding import PartitionSpec as P

STEPS = 2


courant = 0.2
mixing = 0.25
coriolis = 0.5
cos_floor = 0.25
highest = lax.Precision.HIGHEST


def with_halo(value, sides, width, wrap):
    for axis, dim in sides:
        size, length = (lax.axis_size(axis), value.shape[dim])
        up = [(i, (i + 1) % size) for i in range(size if wrap else size - 1)]
        down = [(j, i) for i, j in up]
        last = lax.slice_in_dim(value, length - width, length, axis=dim)
        initial = lax.slice_in_dim(value, 0, width, axis=dim)
        before = lax.ppermute(last, axis, up)
        after = lax.ppermute(initial, axis, down)
        value = jnp.concatenate([before, value, after], axis=dim)
    return value


def from_partner(value, axis, bit):
    return lax.ppermute(value, axis, [(i, i ^ 1 << bit) for i in range(lax.axis_size(axis))])


def angle_tables(count_first, count_second, modulus):
    products = (
        jnp.arange(count_first, dtype=jnp.int32)[:, None]
        * jnp.arange(count_second, dtype=jnp.int32)[None, :]
        % modulus
    )
    angles = products.astype(jnp.float32) * (2.0 * math.pi / modulus)
    return (jnp.cos(angles), jnp.sin(angles))


def small_product(table, values):
    return jnp.einsum(
        "kn,bnp->bkp", table, values, precision=highest, preferred_element_type=jnp.float32
    )


def circle_transform(circles, kept_blocks):
    batch_size, length = circles.shape
    radix_size = 128
    blocks = length // radix_size
    cos_small, sin_small = angle_tables(blocks, blocks, blocks)
    cos_twist, sin_twist = angle_tables(blocks, radix_size, length)
    cos_radix, sin_radix = angle_tables(radix_size, radix_size, radix_size)
    shaped = circles.reshape(batch_size, blocks, radix_size)
    first_real = small_product(cos_small, shaped)
    first_imag = -small_product(sin_small, shaped)
    twist_real = first_real * cos_twist + first_imag * sin_twist
    twist_imag = first_imag * cos_twist - first_real * sin_twist
    forward_table = jnp.concatenate(
        [jnp.concatenate([cos_radix, -sin_radix], 1), jnp.concatenate([sin_radix, cos_radix], 1)], 0
    )
    joined = jnp.concatenate([twist_real, twist_imag], 2).reshape(
        batch_size * blocks, 2 * radix_size
    )
    spectrum = jnp.dot(joined, forward_table, precision=highest, preferred_element_type=jnp.float32)
    index_grid = (
        blocks * jnp.arange(radix_size, dtype=jnp.int32)[None, :]
        + jnp.arange(blocks, dtype=jnp.int32)[:, None]
    )
    signed = jnp.where(index_grid > length // 2, index_grid - length, index_grid)
    retained = (jnp.abs(signed) <= length // 3).astype(jnp.float32)
    factor = retained * (1.0 - 2.0 * math.pi / length * signed.astype(jnp.float32)) / length
    factor_pair = jnp.concatenate([factor, factor], 1)
    weighted = spectrum.reshape(batch_size, blocks, 2 * radix_size) * factor_pair
    inverse_table = jnp.concatenate(
        [jnp.concatenate([cos_radix, sin_radix], 1), jnp.concatenate([-sin_radix, cos_radix], 1)], 0
    )
    inverse_first = jnp.dot(
        weighted.reshape(batch_size * blocks, 2 * radix_size),
        inverse_table,
        precision=highest,
        preferred_element_type=jnp.float32,
    )
    inverse_first = inverse_first.reshape(batch_size, blocks, 2 * radix_size)
    first_half = inverse_first[:, :, :radix_size]
    second_half = inverse_first[:, :, radix_size:]
    turn_real = first_half * cos_twist - second_half * sin_twist
    turn_imag = first_half * sin_twist + second_half * cos_twist
    out_real = small_product(cos_small, turn_real) - small_product(sin_small, turn_imag)
    out_imag = small_product(sin_small, turn_real) + small_product(cos_small, turn_imag)
    return (
        out_real.reshape(batch_size, kept_blocks * radix_size),
        out_imag.reshape(batch_size, kept_blocks * radix_size),
    )


def body(thickness, wind_field):
    fields_now = jnp.concatenate([thickness[None], wind_field], 0)
    level_count, lon_count, lat_count = thickness.shape
    circle_blocks = 2 * lat_count // 128
    latitude = (jnp.arange(lat_count).astype(jnp.float32) + 0.5) * (
        math.pi / lat_count
    ) - 0.5 * math.pi
    secant = 1.0 / jnp.maximum(jnp.cos(latitude), cos_floor)
    coriolis_term = coriolis * jnp.sin(latitude)
    sign_column = jnp.array([1.0, -1.0, -1.0], jnp.float32).reshape(3, 1, 1, 1)
    partner_bit = lax.axis_size("lon").bit_length() - 2
    for step_index in range(STEPS):
        widened = with_halo(fields_now, (("lon", 2),), 3, True)
        zonal_slope = (
            45.0 * (widened[:, :, 4 : lon_count + 4] - widened[:, :, 2 : lon_count + 2])
            - 9.0 * (widened[:, :, 5 : lon_count + 5] - widened[:, :, 1 : lon_count + 1])
            + (widened[:, :, 6 : lon_count + 6] - widened[:, :, 0:lon_count])
        ) / 60.0
        stacked_levels = with_halo(fields_now[0], (("lev", 0),), 1, False)
        vertical = stacked_levels[2:] + stacked_levels[:-2] - 2.0 * fields_now[0]
        half_count = lon_count // 2
        upper_side = lax.axis_index("lon") // (lax.axis_size("lon") // 2)
        own_start = upper_side * half_count
        other_start = (1 - upper_side) * half_count
        own_part = lax.dynamic_slice_in_dim(fields_now, own_start, half_count, 2)
        other_part = lax.dynamic_slice_in_dim(fields_now, other_start, half_count, 2)
        arrived = from_partner(other_part, "lon", partner_bit)
        circle = jnp.concatenate([own_part, sign_column * arrived[..., ::-1]], 3).reshape(
            -1, 2 * lat_count
        )
        full_real, full_imag = circle_transform(circle, circle_blocks)
        full_real = full_real.reshape(3, level_count, half_count, 2 * lat_count)
        full_imag = full_imag.reshape(3, level_count, half_count, 2 * lat_count)
        own_smooth = full_real[..., :lat_count]
        own_slope = full_imag[..., :lat_count]
        away_smooth = sign_column * full_real[..., lat_count:][..., ::-1]
        away_slope = -sign_column * full_imag[..., lat_count:][..., ::-1]
        came_smooth, came_slope = from_partner((away_smooth, away_slope), "lon", partner_bit)
        smooth = jnp.zeros_like(fields_now)
        smooth = lax.dynamic_update_slice_in_dim(smooth, own_smooth, own_start, 2)
        smooth = lax.dynamic_update_slice_in_dim(smooth, came_smooth, other_start, 2)
        meridional_slope = jnp.zeros_like(fields_now)
        meridional_slope = lax.dynamic_update_slice_in_dim(
            meridional_slope, own_slope, own_start, 2
        )
        meridional_slope = lax.dynamic_update_slice_in_dim(
            meridional_slope, came_slope, other_start, 2
        )
        thickness_now = fields_now[0]
        eastward = fields_now[1]
        northward = fields_now[2]
        advect = eastward * secant * zonal_slope + northward * meridional_slope
        height_tendency = (
            -advect[0]
            - thickness_now * (secant * zonal_slope[1] + meridional_slope[2])
            + mixing * vertical
        )
        east_tendency = -advect[1] - secant * zonal_slope[0] + coriolis_term * northward
        north_tendency = -advect[2] - meridional_slope[0] - coriolis_term * eastward
        fields_now = smooth + courant * jnp.stack([height_tendency, east_tendency, north_tendency])
    return (fields_now[0], fields_now[1:])


def solution(mesh):
    in_specs = (P("lev", "lon", None), P(None, "lev", "lon", None))
    out_specs = (P("lev", "lon", None), P(None, "lev", "lon", None))
    return jax.shard_map(body, mesh=mesh, in_specs=in_specs, out_specs=out_specs, check_vma=False)
```

profile of v0, /device:TPU:8, one launch (start us, length us, event | category | flops | bytes accessed | tf_op | source)
XLA Modules:
  0.0 70.6 jit_solution(1946147930065391579)
XLA Ops:
  0.6 1.9 %collective-permute-start.5 = (f32[1,16,2048]{2,1,0:T(8,128)}, f32[1,16,2048]{2,1,0:T(8,128)}, u32[]{:S(2)}, u32[]{:S(2)}) collective-permute-start(f32[1,16,2048]{2,1,0:T(8,128)} %param.3), channel_id=1, source_target_pairs={{1,0},{2,1},{3,2},{5,4},{6,5},{7,6},{9,8},{10,9},{11,10},{13,12},{... | collective-permute-start | bytes 393224 | tf_op jit(solution)/shard_map/ppermute | solution.py:26
  2.6 3.9 %collective-permute-start.6 = (f32[1,16,2048]{2,1,0:T(8,128)}, f32[1,16,2048]{2,1,0:T(8,128)}, u32[]{:S(2)}, u32[]{:S(2)}) collective-permute-start(f32[1,16,2048]{2,1,0:T(8,128)} %param.3), channel_id=1, source_target_pairs={{0,1},{1,2},{2,3},{4,5},{5,6},{6,7},{8,9},{9,10},{10,11},{12,13},{... | collective-permute-start | bytes 393224 | tf_op jit(solution)/shard_map/ppermute | solution.py:25
  6.5 1.1 %fusion.39 = (f32[3,1,8,2048]{3,2,1,0:T(8,128)S(1)}, f32[3,1,8,2048]{3,2,1,0:T(8,128)S(1)}) fusion(s32[]{:T(128)S(6)} %select_n.127, f32[2,1,16,2048]{3,2,1,0:T(8,128)} %param.4, f32[1,1,16,2048]{3,2,1,0:T(8,128)} %bitcast.145, s32[]{:T(128)S(6)} %select_n.128), kind=kLoop, calls=%fused_computation.84 | loop fusion | flops 98304 | bytes 786440 | tf_op jit(solution)/shard_map/concatenate | solution.py:102
  7.6 1.6 %collective-permute-start = (f32[3,1,8,2048]{3,2,1,0:T(8,128)S(1)}, f32[3,1,8,2048]{3,2,1,0:T(8,128)S(1)}, u32[]{:S(2)}, u32[]{:S(2)}) collective-permute-start(f32[3,1,8,2048]{3,2,1,0:T(8,128)S(1)} %get-tuple-element.34), channel_id=1, source_target_pairs={{0,16},{4,20},{8,24},{12,28},{16,0},{20,4},{24,8},{28,12},{1,17},{... | collective-permute-start | bytes 589832 | tf_op jit(solution)/shard_map/ppermute | solution.py:32
  11.6 2.8 %collective-permute-done.3 = f32[3,1,3,2048]{3,2,1,0:T(4,128)S(1)} collective-permute-done((f32[3,1,3,2048]{3,2,1,0:T(4,128)S(1)}, f32[3,1,3,2048]{3,2,1,0:T(4,128)S(1)}, u32[]{:S(2)}, u32[]{:S(2)}) %collective-permute-start.3) | collective-permute-done | bytes 73760 | tf_op jit(solution)/shard_map/ppermute | solution.py:25
  14.5 1.0 %broadcast_multiply_fusion.1 = (f32[3,1,16,2048]{3,2,1,0:T(8,128)}, f32[3,1,16,2048]{3,2,1,0:T(8,128)S(1)}) fusion(f32[3,1,19,2048]{3,2,1,0:T(8,128)S(1)} %get-tuple-element.26, f32[3,1,19,2048]{3,2,1,0:T(8,128)S(1)} %get-tuple-element.25), kind=kLoop, calls=%fused_computation.91 | loop fusion | flops 786432 | bytes 3145728 | tf_op jit(solution)/shard_map/div | solution.py:114
  15.5 1.2 %rev.18 = f32[3,1,8,2048]{3,2,1,0:T(8,128)S(1)} reverse(f32[3,1,8,2048]{3,2,1,0:T(8,128)S(1)} %collective-permute-done), dimensions={3} | reverse | bytes 393216 | tf_op jit(solution)/shard_map/rev | solution.py:128
  18.1 0.8 %convolution_multiply_fusion.1 = f32[24,32,256]{2,1,0:T(8,128)S(1)} fusion(f32[24,32,128]{2,1,0:T(8,128)S(1)} %get-tuple-element.9, f32[24,32,128]{2,1,0:T(8,128)S(1)} %get-tuple-element.8, f32[32,256]{1,0:T(8,128)S(1)} %pad_maximum_fusion.8, f32[128,128]{1,0:T(8,128)S(1)} %get-tuple-element.40, f32[128,128]{1,0:T(8,128)S(1)} %get-tuple-element.39, ...), kind=kOutput, calls=%fused_computation.1 | convolution fusion | flops 604569600 | bytes 1802240 | tf_op jit(solution)/shard_map/dot_general | solution.py:69
  21.6 1.2 %rev.20 = f32[3,1,8,2048]{3,2,1,0:T(8,128)S(1)} reverse(f32[3,1,8,2048]{3,2,1,0:T(8,128)S(1)} %get-tuple-element.29), dimensions={3} | reverse | bytes 393216 | tf_op jit(solution)/shard_map/rev | solution.py:137
  22.9 1.6 %collective-permute-start.4 = (f32[3,1,8,2048]{3,2,1,0:T(8,128)S(1)}, f32[3,1,8,2048]{3,2,1,0:T(8,128)S(1)}, u32[]{:S(2)}, u32[]{:S(2)}) collective-permute-start(f32[3,1,8,2048]{3,2,1,0:T(8,128)S(1)} %broadcast_multiply_fusion.3), channel_id=1, source_target_pairs={{0,16},{4,20},{8,24},{12,28},{16,0},{20,4},{24,8},{28,12},{1,17},{... | collective-permute-start | bytes 589832 | tf_op jit(solution)/shard_map/ppermute | solution.py:32
  25.2 1.2 %rev.19 = f32[3,1,8,2048]{3,2,1,0:T(8,128)S(1)} reverse(f32[3,1,8,2048]{3,2,1,0:T(8,128)S(1)} %get-tuple-element.31), dimensions={3} | reverse | bytes 393216 | tf_op jit(solution)/shard_map/rev | solution.py:136
  27.1 3.7 %collective-permute-done.4 = f32[3,1,8,2048]{3,2,1,0:T(8,128)S(1)} collective-permute-done((f32[3,1,8,2048]{3,2,1,0:T(8,128)S(1)}, f32[3,1,8,2048]{3,2,1,0:T(8,128)S(1)}, u32[]{:S(2)}, u32[]{:S(2)}) %collective-permute-start.4) | collective-permute-done | bytes 196640 | tf_op jit(solution)/shard_map/ppermute | solution.py:32
  30.8 0.9 %copy-done.4 = f32[16,2048]{1,0:T(8,128)S(1)} copy-done((f32[16,2048]{1,0:T(8,128)S(1)}, f32[16,2048]{1,0:T(8,128)}, u32[]{:S(2)}) %copy-start.4) | copy-done | bytes 131096
  31.8 0.9 %copy-done.2 = f32[3,1,16,2048]{3,2,1,0:T(8,128)S(1)} copy-done((f32[3,1,16,2048]{3,2,1,0:T(8,128)S(1)}, f32[3,1,16,2048]{3,2,1,0:T(8,128)}, u32[]{:S(2)}) %copy-start.2) | copy-done | bytes 393240
  32.7 1.0 %fusion.58 = f32[1,1,16,2048]{3,2,1,0:T(8,128)S(1)} fusion(f32[1,16,2048]{2,1,0:T(8,128)S(1)} %copy-done.1, f32[3,1,16,2048]{3,2,1,0:T(8,128)S(1)} %constant_dynamic-update-slice_fusion.2, f32[3,1,16,2048]{3,2,1,0:T(8,128)S(1)} %copy-done.2, f32[3,1,16,2048]{3,2,1,0:T(8,128)S(1)} %multiply_add_fusion.3, f32[1,16,2048]{2,1,0:T(8,128)} %collective-permute-done.5, ...), kind=kLoop, calls=%fused_computation.123 | loop fusion | flops 327680 | bytes 925696 | tf_op jit(solution)/shard_map/stack | solution.py:160
  34.0 2.6 %collective-permute-start.9 = (f32[3,1,3,2048]{3,2,1,0:T(4,128)S(1)}, f32[3,1,3,2048]{3,2,1,0:T(4,128)S(1)}, u32[]{:S(2)}, u32[]{:S(2)}) collective-permute-start(f32[3,1,3,2048]{3,2,1,0:T(4,128)S(1)} %get-tuple-element.17), channel_id=1, source_target_pairs={{4,0},{8,4},{12,8},{16,12},{20,16},{24,20},{28,24},{0,28},{5,1},{9... | collective-permute-start | bytes 221192 | tf_op jit(solution)/shard_map/ppermute | solution.py:26
  36.7 1.0 %collective-permute-start.7 = (f32[3,1,8,2048]{3,2,1,0:T(8,128)S(1)}, f32[3,1,8,2048]{3,2,1,0:T(8,128)S(1)}, u32[]{:S(2)}, u32[]{:S(2)}) collective-permute-start(f32[3,1,8,2048]{3,2,1,0:T(8,128)S(1)} %get-tuple-element.24), channel_id=1, source_target_pairs={{0,16},{4,20},{8,24},{12,28},{16,0},{20,4},{24,8},{28,12},{1,17},{... | collective-permute-start | bytes 589832 | tf_op jit(solution)/shard_map/ppermute | solution.py:32
  37.7 1.7 %collective-permute-done.10 = f32[3,1,3,2048]{3,2,1,0:T(4,128)S(1)} collective-permute-done((f32[3,1,3,2048]{3,2,1,0:T(4,128)S(1)}, f32[3,1,3,2048]{3,2,1,0:T(4,128)S(1)}, u32[]{:S(2)}, u32[]{:S(2)}) %collective-permute-start.10) | collective-permute-done | bytes 73760 | tf_op jit(solution)/shard_map/ppermute | solution.py:25
  39.4 1.1 %broadcast_multiply_fusion = (f32[3,1,16,2048]{3,2,1,0:T(8,128)}, f32[3,1,16,2048]{3,2,1,0:T(8,128)S(1)}) fusion(f32[3,1,16,2048]{3,2,1,0:T(8,128)S(1)} %fusion.27, f32[3,1,3,2048]{3,2,1,0:T(4,128)S(1)} %collective-permute-done.10, f32[3,1,3,2048]{3,2,1,0:T(4,128)S(1)} %collective-permute-done.9), kind=kLoop, calls=%fused_computation.90 | loop fusion | flops 1376256 | bytes 1327104 | tf_op jit(solution)/shard_map/div | solution.py:114
  40.5 2.7 %collective-permute-done.7 = f32[3,1,8,2048]{3,2,1,0:T(8,128)S(1)} collective-permute-done((f32[3,1,8,2048]{3,2,1,0:T(8,128)S(1)}, f32[3,1,8,2048]{3,2,1,0:T(8,128)S(1)}, u32[]{:S(2)}, u32[]{:S(2)}) %collective-permute-start.7) | collective-permute-done | bytes 196640 | tf_op jit(solution)/shard_map/ppermute | solution.py:32
  43.2 1.2 %rev.21 = f32[3,1,8,2048]{3,2,1,0:T(8,128)S(1)} reverse(f32[3,1,8,2048]{3,2,1,0:T(8,128)S(1)} %collective-permute-done.7), dimensions={3} | reverse | bytes 393216 | tf_op jit(solution)/shard_map/rev | solution.py:128
  45.7 0.8 %convolution_multiply_fusion = f32[24,32,256]{2,1,0:T(8,128)S(1)} fusion(f32[24,32,128]{2,1,0:T(8,128)S(1)} %get-tuple-element.7, f32[24,32,128]{2,1,0:T(8,128)S(1)} %get-tuple-element.6, f32[32,256]{1,0:T(8,128)S(1)} %pad_maximum_fusion.8, f32[128,128]{1,0:T(8,128)S(1)} %get-tuple-element.40, f32[128,128]{1,0:T(8,128)S(1)} %get-tuple-element.39, ...), kind=kOutput, calls=%fused_computation | convolution fusion | flops 604569600 | bytes 1802240 | tf_op jit(solution)/shard_map/dot_general | solution.py:69
  49.3 1.2 %rev.23 = f32[3,1,8,2048]{3,2,1,0:T(8,128)S(1)} reverse(f32[3,1,8,2048]{3,2,1,0:T(8,128)S(1)} %get-tuple-element.19), dimensions={3} | reverse | bytes 393216 | tf_op jit(solution)/shard_map/rev | solution.py:137
  50.5 0.8 %collective-permute-start.11 = (f32[3,1,8,2048]{3,2,1,0:T(8,128)S(1)}, f32[3,1,8,2048]{3,2,1,0:T(8,128)S(1)}, u32[]{:S(2)}, u32[]{:S(2)}) collective-permute-start(f32[3,1,8,2048]{3,2,1,0:T(8,128)S(1)} %broadcast_multiply_fusion.2), channel_id=1, source_target_pairs={{0,16},{4,20},{8,24},{12,28},{16,0},{20,4},{24,8},{28,12},{1,17},{... | collective-permute-start | bytes 589832 | tf_op jit(solution)/shard_map/ppermute | solution.py:32
  52.1 1.2 %rev.22 = f32[3,1,8,2048]{3,2,1,0:T(8,128)S(1)} reverse(f32[3,1,8,2048]{3,2,1,0:T(8,128)S(1)} %get-tuple-element.21), dimensions={3} | reverse | bytes 393216 | tf_op jit(solution)/shard_map/rev | solution.py:136
  53.4 1.3 %collective-permute-start.8 = (f32[3,1,8,2048]{3,2,1,0:T(8,128)S(1)}, f32[3,1,8,2048]{3,2,1,0:T(8,128)S(1)}, u32[]{:S(2)}, u32[]{:S(2)}) collective-permute-start(f32[3,1,8,2048]{3,2,1,0:T(8,128)S(1)} %broadcast_multiply_fusion.4), channel_id=1, source_target_pairs={{0,16},{4,20},{8,24},{12,28},{16,0},{20,4},{24,8},{28,12},{1,17},{... | collective-permute-start | bytes 589832 | tf_op jit(solution)/shard_map/ppermute | solution.py:32
  54.7 3.6 %collective-permute-done.11 = f32[3,1,8,2048]{3,2,1,0:T(8,128)S(1)} collective-permute-done((f32[3,1,8,2048]{3,2,1,0:T(8,128)S(1)}, f32[3,1,8,2048]{3,2,1,0:T(8,128)S(1)}, u32[]{:S(2)}, u32[]{:S(2)}) %collective-permute-start.11) | collective-permute-done | bytes 196640 | tf_op jit(solution)/shard_map/ppermute | solution.py:32
  58.4 0.9 %copy-done.3 = f32[3,1,16,2048]{3,2,1,0:T(8,128)S(1)} copy-done((f32[3,1,16,2048]{3,2,1,0:T(8,128)S(1)}, f32[3,1,16,2048]{3,2,1,0:T(8,128)}, u32[]{:S(2)}) %copy-start.3) | copy-done | bytes 393240
  59.4 2.9 %collective-permute-start.12 = (f32[1,16,2048]{2,1,0:T(8,128)S(1)}, f32[1,16,2048]{2,1,0:T(8,128)S(1)}, u32[]{:S(2)}, u32[]{:S(2)}) collective-permute-start(f32[1,16,2048]{2,1,0:T(8,128)S(1)} %get-tuple-element.14), channel_id=1, source_target_pairs={{1,0},{2,1},{3,2},{5,4},{6,5},{7,6},{9,8},{10,9},{11,10},{13,12},{... | collective-permute-start | bytes 393224 | tf_op jit(solution)/shard_map/ppermute | solution.py:26
  62.3 3.2 %collective-permute-start.13 = (f32[1,16,2048]{2,1,0:T(8,128)S(1)}, f32[1,16,2048]{2,1,0:T(8,128)S(1)}, u32[]{:S(2)}, u32[]{:S(2)}) collective-permute-start(f32[1,16,2048]{2,1,0:T(8,128)S(1)} %get-tuple-element.14), channel_id=1, source_target_pairs={{0,1},{1,2},{2,3},{4,5},{5,6},{6,7},{8,9},{9,10},{10,11},{12,13},{... | collective-permute-start | bytes 393224 | tf_op jit(solution)/shard_map/ppermute | solution.py:25
  65.5 1.0 %collective-permute-done.12 = f32[1,16,2048]{2,1,0:T(8,128)S(1)} collective-permute-done((f32[1,16,2048]{2,1,0:T(8,128)S(1)}, f32[1,16,2048]{2,1,0:T(8,128)S(1)}, u32[]{:S(2)}, u32[]{:S(2)}) %collective-permute-start.12) | collective-permute-done | bytes 131104 | tf_op jit(solution)/shard_map/ppermute | solution.py:26
  66.5 2.7 %collective-permute-done.13 = f32[1,16,2048]{2,1,0:T(8,128)S(1)} collective-permute-done((f32[1,16,2048]{2,1,0:T(8,128)S(1)}, f32[1,16,2048]{2,1,0:T(8,128)S(1)}, u32[]{:S(2)}, u32[]{:S(2)}) %collective-permute-start.13) | collective-permute-done | bytes 131104 | tf_op jit(solution)/shard_map/ppermute | solution.py:25
  (90 shorter events, 15.0 us)
Async XLA Ops:
  0.6 31.1 %collective-permute-start.5 = (f32[1,16,2048]{2,1,0:T(8,128)}, f32[1,16,2048]{2,1,0:T(8,128)}, u32[]{:S(2)}, u32[]{:S(2)}) collective-permute-start(f32[1,16,2048]{2,1,0:T(8,128)} %param.3), channel_id=1, source_target_pairs={{1,0},{2,1},{3,2},{5,4},{6,5},{7,6},{9,8},{10,9},{11,10},{13,12},{... | collective-permute-start | bytes 393224 | tf_op jit(solution)/shard_map/ppermute | solution.py:26
  2.6 29.2 %collective-permute-start.6 = (f32[1,16,2048]{2,1,0:T(8,128)}, f32[1,16,2048]{2,1,0:T(8,128)}, u32[]{:S(2)}, u32[]{:S(2)}) collective-permute-start(f32[1,16,2048]{2,1,0:T(8,128)} %param.3), channel_id=1, source_target_pairs={{0,1},{1,2},{2,3},{4,5},{5,6},{6,7},{8,9},{9,10},{10,11},{12,13},{... | collective-permute-start | bytes 393224 | tf_op jit(solution)/shard_map/ppermute | solution.py:25
  6.5 2.7 %copy-start = (f32[2,1,16,2048]{3,2,1,0:T(8,128)S(1)}, f32[2,1,16,2048]{3,2,1,0:T(8,128)}, u32[]{:S(2)}) copy-start(f32[2,1,16,2048]{3,2,1,0:T(8,128)} %param.4) | copy-start | bytes 786436
  6.5 2.7 %copy-start.1 = (f32[1,16,2048]{2,1,0:T(8,128)S(1)}, f32[1,16,2048]{2,1,0:T(8,128)}, u32[]{:S(2)}) copy-start(f32[1,16,2048]{2,1,0:T(8,128)} %param.3) | copy-start | bytes 393220
  7.6 7.9 %collective-permute-start = (f32[3,1,8,2048]{3,2,1,0:T(8,128)S(1)}, f32[3,1,8,2048]{3,2,1,0:T(8,128)S(1)}, u32[]{:S(2)}, u32[]{:S(2)}) collective-permute-start(f32[3,1,8,2048]{3,2,1,0:T(8,128)S(1)} %get-tuple-element.34), channel_id=1, source_target_pairs={{0,16},{4,20},{8,24},{12,28},{16,0},{20,4},{24,8},{28,12},{1,17},{... | collective-permute-start | bytes 589832 | tf_op jit(solution)/shard_map/ppermute | solution.py:32
  9.2 2.3 %collective-permute-start.2 = (f32[3,1,3,2048]{3,2,1,0:T(4,128)S(1)}, f32[3,1,3,2048]{3,2,1,0:T(4,128)S(1)}, u32[]{:S(2)}, u32[]{:S(2)}) collective-permute-start(f32[3,1,3,2048]{3,2,1,0:T(4,128)S(1)} %get-tuple-element.27), channel_id=1, source_target_pairs={{4,0},{8,4},{12,8},{16,12},{20,16},{24,20},{28,24},{0,28},{5,1},{9... | collective-permute-start | bytes 221192 | tf_op jit(solution)/shard_map/ppermute | solution.py:26
  9.3 5.1 %collective-permute-start.3 = (f32[3,1,3,2048]{3,2,1,0:T(4,128)S(1)}, f32[3,1,3,2048]{3,2,1,0:T(4,128)S(1)}, u32[]{:S(2)}, u32[]{:S(2)}) collective-permute-start(f32[3,1,3,2048]{3,2,1,0:T(4,128)S(1)} %get-tuple-element.28), channel_id=1, source_target_pairs={{0,4},{4,8},{8,12},{12,16},{16,20},{20,24},{24,28},{28,0},{1,5},{5... | collective-permute-start | bytes 221192 | tf_op jit(solution)/shard_map/ppermute | solution.py:25
  15.5 1.2 %copy-start.5 = (f32[3]{0:T(128)S(1)}, f32[3]{0:T(128)}, u32[]{:S(2)}) copy-start(f32[3]{0:T(128)} %constant.127.clone) | copy-start | bytes 40
  21.6 1.2 %copy-start.8 = (f32[3]{0:T(128)S(1)}, f32[3]{0:T(128)}, u32[]{:S(2)}) copy-start(f32[3]{0:T(128)} %constant.130) | copy-start | bytes 40
  22.9 7.9 %collective-permute-start.4 = (f32[3,1,8,2048]{3,2,1,0:T(8,128)S(1)}, f32[3,1,8,2048]{3,2,1,0:T(8,128)S(1)}, u32[]{:S(2)}, u32[]{:S(2)}) collective-permute-start(f32[3,1,8,2048]{3,2,1,0:T(8,128)S(1)} %broadcast_multiply_fusion.3), channel_id=1, source_target_pairs={{0,16},{4,20},{8,24},{12,28},{16,0},{20,4},{24,8},{28,12},{1,17},{... | collective-permute-start | bytes 589832 | tf_op jit(solution)/shard_map/ppermute | solution.py:32
  25.2 1.2 %copy-start.6 = (f32[3]{0:T(128)S(1)}, f32[3]{0:T(128)}, u32[]{:S(2)}) copy-start(f32[3]{0:T(128)} %constant.127.clone) | copy-start | bytes 40
  26.5 7.3 %collective-permute-start.1 = (f32[3,1,8,2048]{3,2,1,0:T(8,128)S(1)}, f32[3,1,8,2048]{3,2,1,0:T(8,128)S(1)}, u32[]{:S(2)}, u32[]{:S(2)}) collective-permute-start(f32[3,1,8,2048]{3,2,1,0:T(8,128)S(1)} %broadcast_multiply_fusion.6), channel_id=1, source_target_pairs={{0,16},{4,20},{8,24},{12,28},{16,0},{20,4},{24,8},{28,12},{1,17},{... | collective-permute-start | bytes 589832 | tf_op jit(solution)/shard_map/ppermute | solution.py:32
  30.8 0.9 %copy-start.4 = (f32[16,2048]{1,0:T(8,128)S(1)}, f32[16,2048]{1,0:T(8,128)}, u32[]{:S(2)}) copy-start(f32[16,2048]{1,0:T(8,128)} %get-tuple-element.36) | copy-start | bytes 393220
  31.7 1.0 %copy-start.2 = (f32[3,1,16,2048]{3,2,1,0:T(8,128)S(1)}, f32[3,1,16,2048]{3,2,1,0:T(8,128)}, u32[]{:S(2)}) copy-start(f32[3,1,16,2048]{3,2,1,0:T(8,128)} %get-tuple-element.4) | copy-start | bytes 1179652
  34.0 5.4 %collective-permute-start.10 = (f32[3,1,3,2048]{3,2,1,0:T(4,128)S(1)}, f32[3,1,3,2048]{3,2,1,0:T(4,128)S(1)}, u32[]{:S(2)}, u32[]{:S(2)}) collective-permute-start(f32[3,1,3,2048]{3,2,1,0:T(4,128)S(1)} %get-tuple-element.18), channel_id=1, source_target_pairs={{0,4},{4,8},{8,12},{12,16},{16,20},{20,24},{24,28},{28,0},{1,5},{5... | collective-permute-start | bytes 221192 | tf_op jit(solution)/shard_map/ppermute | solution.py:25
  34.0 5.4 %collective-permute-start.9 = (f32[3,1,3,2048]{3,2,1,0:T(4,128)S(1)}, f32[3,1,3,2048]{3,2,1,0:T(4,128)S(1)}, u32[]{:S(2)}, u32[]{:S(2)}) collective-permute-start(f32[3,1,3,2048]{3,2,1,0:T(4,128)S(1)} %get-tuple-element.17), channel_id=1, source_target_pairs={{4,0},{8,4},{12,8},{16,12},{20,16},{24,20},{28,24},{0,28},{5,1},{9... | collective-permute-start | bytes 221192 | tf_op jit(solution)/shard_map/ppermute | solution.py:26
  36.7 6.5 %collective-permute-start.7 = (f32[3,1,8,2048]{3,2,1,0:T(8,128)S(1)}, f32[3,1,8,2048]{3,2,1,0:T(8,128)S(1)}, u32[]{:S(2)}, u32[]{:S(2)}) collective-permute-start(f32[3,1,8,2048]{3,2,1,0:T(8,128)S(1)} %get-tuple-element.24), channel_id=1, source_target_pairs={{0,16},{4,20},{8,24},{12,28},{16,0},{20,4},{24,8},{28,12},{1,17},{... | collective-permute-start | bytes 589832 | tf_op jit(solution)/shard_map/ppermute | solution.py:32
  49.2 1.2 %copy-start.9 = (f32[3]{0:T(128)S(1)}, f32[3]{0:T(128)}, u32[]{:S(2)}) copy-start(f32[3]{0:T(128)} %constant.130) | copy-start | bytes 40
  50.5 7.8 %collective-permute-start.11 = (f32[3,1,8,2048]{3,2,1,0:T(8,128)S(1)}, f32[3,1,8,2048]{3,2,1,0:T(8,128)S(1)}, u32[]{:S(2)}, u32[]{:S(2)}) collective-permute-start(f32[3,1,8,2048]{3,2,1,0:T(8,128)S(1)} %broadcast_multiply_fusion.2), channel_id=1, source_target_pairs={{0,16},{4,20},{8,24},{12,28},{16,0},{20,4},{24,8},{28,12},{1,17},{... | collective-permute-start | bytes 589832 | tf_op jit(solution)/shard_map/ppermute | solution.py:32
  52.1 1.2 %copy-start.7 = (f32[3]{0:T(128)S(1)}, f32[3]{0:T(128)}, u32[]{:S(2)}) copy-start(f32[3]{0:T(128)} %constant.127.clone) | copy-start | bytes 40
  53.4 12.1 %collective-permute-start.8 = (f32[3,1,8,2048]{3,2,1,0:T(8,128)S(1)}, f32[3,1,8,2048]{3,2,1,0:T(8,128)S(1)}, u32[]{:S(2)}, u32[]{:S(2)}) collective-permute-start(f32[3,1,8,2048]{3,2,1,0:T(8,128)S(1)} %broadcast_multiply_fusion.4), channel_id=1, source_target_pairs={{0,16},{4,20},{8,24},{12,28},{16,0},{20,4},{24,8},{28,12},{1,17},{... | collective-permute-start | bytes 589832 | tf_op jit(solution)/shard_map/ppermute | solution.py:32
  58.3 1.0 %copy-start.3 = (f32[3,1,16,2048]{3,2,1,0:T(8,128)S(1)}, f32[3,1,16,2048]{3,2,1,0:T(8,128)}, u32[]{:S(2)}) copy-start(f32[3,1,16,2048]{3,2,1,0:T(8,128)} %get-tuple-element.2) | copy-start | bytes 1179652
  59.4 7.1 %collective-permute-start.12 = (f32[1,16,2048]{2,1,0:T(8,128)S(1)}, f32[1,16,2048]{2,1,0:T(8,128)S(1)}, u32[]{:S(2)}, u32[]{:S(2)}) collective-permute-start(f32[1,16,2048]{2,1,0:T(8,128)S(1)} %get-tuple-element.14), channel_id=1, source_target_pairs={{1,0},{2,1},{3,2},{5,4},{6,5},{7,6},{9,8},{10,9},{11,10},{13,12},{... | collective-permute-start | bytes 393224 | tf_op jit(solution)/shard_map/ppermute | solution.py:26
  62.3 6.9 %collective-permute-start.13 = (f32[1,16,2048]{2,1,0:T(8,128)S(1)}, f32[1,16,2048]{2,1,0:T(8,128)S(1)}, u32[]{:S(2)}, u32[]{:S(2)}) collective-permute-start(f32[1,16,2048]{2,1,0:T(8,128)S(1)} %get-tuple-element.14), channel_id=1, source_target_pairs={{0,1},{1,2},{2,3},{4,5},{5,6},{6,7},{8,9},{9,10},{10,11},{12,13},{... | collective-permute-start | bytes 393224 | tf_op jit(solution)/shard_map/ppermute | solution.py:25
where the time goes:
time: 71.5 us; the launch traced here: 70.6 us
  starting transfers between devices  22.1 us (31%)
  waiting for transfers between devices  18.5 us (26%)
  local copies, waits for them, and re-layouts  12 us (17%)
  matrix products  10.1 us (14%)
  other arithmetic  6.8 us (10%)
  between operations  1.21 us (2%)
    ppermute x6, waiting for transfers between devices, from_partner(): lax.ppermute(value, axis, [(i, i ^ 1 << bit) for i in range(lax.axis_size...  9.95 us
    ppermute x4, starting transfers between devices, with_halo(): before = lax.ppermute(last, axis, up)  7.62 us
    ppermute x4, starting transfers between devices, with_halo(): after = lax.ppermute(initial, axis, down)  7.51 us
    ppermute x4, waiting for transfers between devices, with_halo(): before = lax.ppermute(last, axis, up)  7.19 us
    dot_general x12, matrix products, small_product(): jnp.einsum('kn,bnp->bkp', table, values, precision=highest, preferred_ele...  6.96 us
    ppermute x6, starting transfers between devices, from_partner(): lax.ppermute(value, axis, [(i, i ^ 1 << bit) for i in range(lax.axis_size...  6.94 us
    unnamed x22, local copies, waits for them, and re-layouts  2.91 us
    rev x2, local copies, waits for them, and re-layouts, body(): away_slope = -sign_column * full_imag[..., lat_count:][..., ::-1]  2.34 us
  transfers between devices with their start and end apart: 14, of which 8 were waited for; matrix products, arithmetic and copies ran while one was open for 24% of the time, Pallas kernels for 0%

commit v1 on v0

v1 whole, which is shorter than its diff:
```python
import functools
import math

import jax
import jax.numpy as jnp
import numpy as np
from jax import lax
from jax.experimental import pallas as pl
from jax.experimental.pallas import tpu as pltpu
from jax.sharding import PartitionSpec as P

STEPS = 2

courant = 0.2
mixing = 0.25
coriolis = 0.5
cos_floor = 0.25

RADIX = 128
ROWS = 8
HALO = 3
SIGNS = (1.0, -1.0, -1.0)


def split_table(table):
    high = table.astype(np.float32).astype(jnp.bfloat16)
    low = (table - high.astype(np.float64)).astype(np.float32).astype(jnp.bfloat16)
    return jnp.asarray(high), jnp.asarray(low)


@functools.lru_cache(maxsize=None)
def numpy_tables(lat_count):
    length = 2 * lat_count
    blocks = length // RADIX
    kept = blocks // 2 + 1
    centred = np.arange(RADIX) + 0.5
    order = np.arange(RADIX)
    signed = np.where(order < RADIX // 2, order, order - RADIX).astype(np.float64)
    angle = 2.0 * np.pi / RADIX * centred[:, None] * signed[None, :]
    cos, sin = np.cos(angle), np.sin(angle)
    forward = np.block([[cos, -sin], [sin, cos]])
    cos_t, sin_t = cos.T, sin.T
    weight = signed[:, None]
    inverse = np.block(
        [
            [cos_t, sin_t, -weight * sin_t, weight * cos_t],
            [-sin_t, cos_t, -weight * cos_t, -weight * sin_t],
        ]
    )
    first = np.arange(kept)
    turn = 2.0 * np.pi / length * first[:, None] * centred[None, :]
    twist = np.stack([np.cos(turn), -np.sin(turn)], 1)
    share = np.where((first == 0) | (first == blocks // 2), 1.0, 2.0)[:, None] / length
    back = np.stack([np.cos(turn) * share, np.sin(turn) * share], 1)
    slope_scale = 2.0 * np.pi * blocks / length
    back = np.concatenate([back, back * slope_scale], 1)
    wave = first[:, None] + blocks * signed[None, :]
    retained = (np.abs(wave) <= length // 3).astype(np.float64)
    plus = np.concatenate([retained, retained], 1)
    minus = np.concatenate([retained, -retained], 1)
    masks = np.stack([plus, minus, -minus], 1)
    latitude = (np.arange(lat_count) + 0.5) * (np.pi / lat_count) - 0.5 * np.pi
    rows = np.stack(
        [1.0 / np.maximum(np.cos(latitude), cos_floor), coriolis * np.sin(latitude)]
    )
    flat = lambda a: a.reshape(-1, a.shape[-1]).astype(np.float32)
    return forward, inverse, flat(twist), flat(back), flat(masks), rows.astype(np.float32)


def times(value, angle):
    real, imag = value
    cos, sin = math.cos(angle), math.sin(angle)
    quarter = round(angle / (math.pi / 2), 9)
    if quarter == int(quarter):
        turn = int(quarter) % 4
        return [(real, imag), (-imag, real), (-real, -imag), (imag, -real)][turn]
    if abs(abs(cos) - abs(sin)) < 1e-12:
        scale = abs(cos)
        a = real if cos > 0 else -real
        b = imag if cos > 0 else -imag
        c = imag if sin > 0 else -imag
        d = real if sin > 0 else -real
        return (scale * (a - c), scale * (b + d))
    return (real * cos - imag * sin, imag * cos + real * sin)


def add(a, b):
    return (a[0] + b[0], a[1] + b[1])


def sub(a, b):
    return (a[0] - b[0], a[1] - b[1])


def complex_dft(values, sign):
    n = len(values)
    if n == 1:
        return values
    half = n // 2
    even = complex_dft([add(values[m], values[m + half]) for m in range(half)], sign)
    odd = complex_dft(
        [
            times(sub(values[m], values[m + half]), sign * 2 * math.pi * m / n)
            for m in range(half)
        ],
        sign,
    )
    return [even[q // 2] if q % 2 == 0 else odd[q // 2] for q in range(n)]


def odd_outputs(values):
    r = len(values)
    if r == 1:
        return {1: (values[0], None)}
    half = r // 2
    turned = [
        times((values[m], -values[m + half]), -math.pi * m / r) for m in range(half)
    ]
    out = {}
    for q, value in enumerate(complex_dft(turned, -1)):
        j = 4 * q + 1
        out[j if j <= r else 2 * r - j] = value if j <= r else (value[0], -value[1])
    return out


def half_circle_forward(values):
    n = len(values)
    out = {j: value for j, value in odd_outputs(values).items()}
    scale = 2
    while len(values) > 1:
        half = len(values) // 2
        difference = [values[m] - values[m + half] for m in range(half)]
        values = [values[m] + values[m + half] for m in range(half)]
        for j, value in odd_outputs(difference).items():
            out[j * scale] = value
        scale *= 2
    out[0] = (values[0], None)
    return [out[k] for k in range(n + 1)]


def odd_inputs(values, r):
    if r == 1:
        return [values[1][0]]
    half = r // 2
    gathered = []
    for q in range(half):
        j = 4 * q + 1
        if j <= r:
            gathered.append(values[j])
        else:
            real, imag = values[2 * r - j]
            gathered.append((real, -imag))
    turned = [
        times(value, math.pi * m / r) for m, value in enumerate(complex_dft(gathered, 1))
    ]
    return [value[0] for value in turned] + [-value[1] for value in turned]


def half_circle_inverse(values):
    n = len(values) - 1
    result = [values[0][0]]
    size = 1
    while size < n:
        step = n // size
        difference = odd_inputs({j: values[j * step] for j in range(1, size + 1, 2)}, size)
        result = [result[m] + difference[m] for m in range(size)] + [
            result[m] - difference[m] for m in range(size)
        ]
        size *= 2
    last = odd_inputs({j: values[j] for j in range(1, n + 1, 2)}, n)
    return [result[m] + last[m] for m in range(n)]


def tile(index):
    return pl.ds(index * RADIX, RADIX)


def split(value):
    high = value.astype(jnp.bfloat16)
    return high, (value - high.astype(jnp.float32)).astype(jnp.bfloat16)


def triple_product(value, high_table, low_table):
    high, low = split(value)
    dot = functools.partial(jnp.dot, preferred_element_type=jnp.float32)
    return dot(high, high_table) + dot(low, high_table) + dot(high, low_table)


def forward_stage(fields, twist, turned, blocks):
    count = fields.shape[0]
    for field in range(count):
        slabs = [fields[field, :, tile(m)] for m in range(blocks // 2)]
        for k, (real, imag) in enumerate(half_circle_forward(slabs)):
            at = pl.ds((k * count + field) * ROWS, ROWS)
            cos, sin = twist[2 * k : 2 * k + 1, :], twist[2 * k + 1 : 2 * k + 2, :]
            if imag is None:
                turned[at, tile(0)] = real * cos
                turned[at, tile(1)] = real * sin
            else:
                turned[at, tile(0)] = real * cos - imag * sin
                turned[at, tile(1)] = real * sin + imag * cos


def own_kernel(blocks, fields, twist, masks, high, low, spectrum, turned):
    kept = blocks // 2 + 1
    forward_stage(fields, twist, turned, blocks)
    result = triple_product(turned[...], high[...], low[...])
    for k in range(kept):
        at = k * 3 * ROWS
        spectrum[at : at + 3 * ROWS, :] = (
            result[at : at + 3 * ROWS, :] * masks[3 * k : 3 * k + 1, :]
        )


def halo_rows(pack, lat_count, field, index):
    if field < 2:
        return pack[HALO * field : HALO * field + HALO, tile(index)]
    last = pack[index // 2 : index // 2 + 1, pl.ds(lat_count + index % 2 * RADIX, RADIX)]
    return jnp.concatenate([pack[2 * HALO : ROWS, tile(index)], last], 0)


def pack_rows(pack, lat_count, field, index, rows):
    if field < 2:
        pack[HALO * field : HALO * field + HALO, tile(index)] = rows
    else:
        pack[2 * HALO : ROWS, tile(index)] = rows[: ROWS - 2 * HALO]
        pack[index // 2 : index // 2 + 1, pl.ds(lat_count + index % 2 * RADIX, RADIX)] = rows[
            ROWS - 2 * HALO :
        ]


def pack_kernel(first_half, second_half, first_pack, last_pack):
    lat_count = first_half.shape[-1]
    for field in range(3):
        for index in range(lat_count // RADIX):
            pack_rows(first_pack, lat_count, field, index, first_half[field, :HALO, tile(index)])
            pack_rows(
                last_pack, lat_count, field, index, second_half[field, ROWS - HALO :, tile(index)]
            )


def step_kernel(
    blocks,
    half,
    final,
    mine,
    other,
    halo,
    far,
    above,
    below,
    spectrum,
    twist,
    back,
    masks,
    rows,
    forward_high,
    forward_low,
    inverse_high,
    inverse_low,
    *rest,
):
    kept = blocks // 2 + 1
    tiles = blocks // 2
    lat_count = mine.shape[-1]
    outs, (turned, weighted, spread, smooth, slope) = rest[:-5], rest[-5:]
    forward_stage(far, twist, turned, blocks)
    result = triple_product(turned[...], forward_high[...], forward_low[...])
    for k in range(kept):
        for field in range(3):
            at = (k * 3 + field) * ROWS
            row = 3 * k + (1 if SIGNS[field] > 0 else 2)
            weighted[at : at + ROWS, :] = (
                spectrum[at : at + ROWS, :] + result[at : at + ROWS, :] * masks[row : row + 1, :]
            )
    spread[...] = triple_product(weighted[...], inverse_high[...], inverse_low[...])
    for field in range(3):
        smooth_terms, slope_terms = [], []
        for k in range(kept):
            at = pl.ds((k * 3 + field) * ROWS, ROWS)
            real, imag, slope_real, slope_imag = [spread[at, tile(i)] for i in range(4)]
            cos, sin, slope_cos, slope_sin = [back[4 * k + i : 4 * k + i + 1, :] for i in range(4)]
            turn_real = real * cos - imag * sin
            turn_imag = real * sin + imag * cos
            wave = 2.0 * math.pi * k / (2 * lat_count)
            smooth_terms.append((turn_real, turn_imag))
            slope_terms.append(
                (
                    slope_real * slope_cos - slope_imag * slope_sin - wave * turn_imag,
                    slope_real * slope_sin + slope_imag * slope_cos + wave * turn_real,
                )
            )
        for m, value in enumerate(half_circle_inverse(smooth_terms)):
            smooth[field, :, tile(m)] = value
        for m, value in enumerate(half_circle_inverse(slope_terms)):
            slope[field, :, tile(m)] = value
    for index in range(tiles):
        zonal = []
        for field in range(3):
            here = mine[field, :, tile(index)]
            edge = halo_rows(halo, lat_count, field, index)
            there = other[field, :, tile(index)]
            if half == 0:
                line = jnp.concatenate([edge, here, there[:HALO]], 0)
            else:
                line = jnp.concatenate([there[ROWS - HALO :], here, edge], 0)
            at = [line[i : i + ROWS] for i in range(2 * HALO + 1)]
            zonal.append(
                (45.0 / 60.0) * (at[4] - at[2])
                - (9.0 / 60.0) * (at[5] - at[1])
                + (1.0 / 60.0) * (at[6] - at[0])
            )
        height, east, north = [mine[field, :, tile(index)] for field in range(3)]
        secant, turning = rows[0:1, tile(index)], rows[1:2, tile(index)]
        low_row = half * ROWS
        vertical = (
            above[low_row : low_row + ROWS, tile(index)]
            + below[low_row : low_row + ROWS, tile(index)]
            - 2.0 * height
        )
        zonal = [secant * value for value in zonal]
        slopes = [slope[field, :, tile(index)] for field in range(3)]
        advect = [east * zonal[field] + north * slopes[field] for field in range(3)]
        tendency = [
            mixing * vertical - advect[0] - height * (zonal[1] + slopes[2]),
            turning * north - advect[1] - zonal[0],
            -advect[2] - slopes[0] - turning * east,
        ]
        values = [smooth[field, :, tile(index)] + courant * tendency[field] for field in range(3)]
        if final:
            for field in range(3):
                outs[0][field, :, tile(index)] = values[field]
        else:
            for field in range(3):
                outs[0][field, :, tile(index)] = values[field]
                chosen = values[field][:HALO] if half == 0 else values[field][ROWS - HALO :]
                pack_rows(outs[1], lat_count, field, index, chosen)


def vmem(count):
    return [pl.BlockSpec(memory_space=pltpu.VMEM)] * count


def params():
    return pltpu.CompilerParams(vmem_limit_bytes=24 * 1024 * 1024)


def shift(value, axis, step, wrap):
    size = lax.axis_size(axis)
    pairs = [(i, (i + step) % size) for i in range(size) if wrap or 0 <= i + step < size]
    return lax.ppermute(value, axis, pairs)


def from_antipode(value):
    size = lax.axis_size("lon")
    return lax.ppermute(value, "lon", [(i, (i + size // 2) % size) for i in range(size)])


def body(thickness, wind_field):
    level_count, lon_count, lat_count = thickness.shape
    assert level_count == 1 and lon_count == 2 * ROWS
    blocks = 2 * lat_count // RADIX
    kept = blocks // 2 + 1
    spectral_rows = (3 * kept * ROWS + 15) // 16 * 16
    forward, inverse, twist, back, masks, rows = numpy_tables(lat_count)
    forward_tables = split_table(forward)
    inverse_tables = split_table(inverse)
    twist, back, masks, rows = [jnp.asarray(a) for a in (twist, back, masks, rows)]
    f32 = jnp.float32
    half_shape = jax.ShapeDtypeStruct((3, ROWS, lat_count), f32)
    pack_shape = jax.ShapeDtypeStruct((ROWS, lat_count + lat_count // ROWS), f32)
    spectrum_shape = jax.ShapeDtypeStruct((spectral_rows, 2 * RADIX), f32)
    scratch = lambda *shape: pltpu.VMEM(shape, f32)

    own = pl.pallas_call(
        functools.partial(own_kernel, blocks),
        out_shape=spectrum_shape,
        in_specs=vmem(5),
        out_specs=vmem(1)[0],
        scratch_shapes=[scratch(spectral_rows, 2 * RADIX)],
        compiler_params=params(),
        name="own_spectrum",
    )
    pack = pl.pallas_call(
        pack_kernel,
        out_shape=[pack_shape] * 2,
        in_specs=vmem(2),
        out_specs=vmem(2),
        compiler_params=params(),
        name="pack_halo",
    )

    def advance(half, final, *args):
        outs = [half_shape] if final else [half_shape, pack_shape]
        return pl.pallas_call(
            functools.partial(step_kernel, blocks, half, final),
            out_shape=outs,
            in_specs=vmem(len(args)),
            out_specs=vmem(len(outs)),
            scratch_shapes=[
                scratch(spectral_rows, 2 * RADIX),
                scratch(spectral_rows, 2 * RADIX),
                scratch(spectral_rows, 4 * RADIX),
                scratch(3, ROWS, lat_count),
                scratch(3, ROWS, lat_count),
            ],
            compiler_params=params(),
            name=f"advance_half",
        )(*args)

    fields = jnp.concatenate([thickness, wind_field[:, 0]], 0)
    halves = [fields[:, :ROWS], fields[:, ROWS:]]
    packs = None
    height = thickness[0]
    for step in range(STEPS):
        final = step == STEPS - 1
        far = [from_antipode(half) for half in halves]
        spectra = [own(half, twist, masks, *forward_tables) for half in halves]
        if packs is None:
            packs = pack(*halves)
        first_pack, last_pack = packs
        halo_left = shift(last_pack, "lon", 1, True)
        halo_right = shift(first_pack, "lon", -1, True)
        above = shift(height, "lev", -1, False)
        below = shift(height, "lev", 1, False)
        results = []
        for half in range(2):
            results.append(
                advance(
                    half,
                    final,
                    halves[half],
                    halves[1 - half],
                    (halo_left, halo_right)[half],
                    far[half],
                    above,
                    below,
                    spectra[half],
                    twist,
                    back,
                    masks,
                    rows,
                    *forward_tables,
                    *inverse_tables,
                )
            )
        halves = [result[0] for result in results]
        if not final:
            packs = [result[1] for result in results]
            height = jnp.concatenate([half[0] for half in halves], 0)
    fields = jnp.concatenate(halves, 1)
    return fields[:1], fields[1:, None]


def solution(mesh):
    in_specs = (P("lev", "lon", None), P(None, "lev", "lon", None))
    out_specs = (P("lev", "lon", None), P(None, "lev", "lon", None))
    return jax.shard_map(body, mesh=mesh, in_specs=in_specs, out_specs=out_specs, check_vma=False)
```

time: 71.5 us -> 36.7 us (0.51)
  the two profiles are of different devices: /device:TPU:8 before, /device:TPU:0 now
where the time goes in v1:
time: 36.7 us; the launch traced here: 36.5 us
  starting transfers between devices  20.5 us (56%)
  Pallas kernels  7.96 us (22%)
  waiting for transfers between devices  4.54 us (12%)
  other arithmetic  2.49 us (7%)
  between operations  0.88 us (2%)
    ppermute x8, starting transfers between devices, shift(): return lax.ppermute(value, axis, pairs)  15.4 us
    pallas_call x4, Pallas kernels, advance(): pl.pallas_call(functools.partial(step_kernel, blocks, half, final), out_s...  6.36 us
    ppermute x4, starting transfers between devices, from_antipode(): lax.ppermute(value, 'lon', [(i, (i + size // 2) % size) for i in range(si...  5.17 us
    ppermute x8, waiting for transfers between devices, shift(): return lax.ppermute(value, axis, pairs)  3.66 us
    pallas_call x4, Pallas kernels, body(): spectra = [own(half, twist, masks, *forward_tables) for half in halves]  1.55 us
    concatenate x1, other arithmetic, body(): fields = jnp.concatenate([thickness, wind_field[:, 0]], 0)  1.09 us
    ppermute x4, waiting for transfers between devices, from_antipode(): lax.ppermute(value, 'lon', [(i, (i + size // 2) % size) for i in range(si...  0.87 us
  transfers between devices with their start and end apart: 12, of which 5 were waited for; matrix products, arithmetic and copies ran while one was open for 0% of the time, Pallas kernels for 17%

profile of v1, /device:TPU:0, one launch (start us, length us, event | category | flops | bytes accessed | tf_op | source)
XLA Modules:
  0.0 36.5 jit_solution(6566210048194352549)
XLA Ops:
  0.6 1.1 %fusion.1 = (f32[3,8,2048]{2,1,0:T(8,128)S(1)}, f32[3,8,2048]{2,1,0:T(8,128)S(1)}) fusion(f32[1,16,2048]{2,1,0:T(8,128)} %param.10, f32[2,16,2048]{2,1,0:T(8,128)} %bitcast.10), kind=kLoop, calls=%fused_computation.4 | loop fusion | flops 98304 | bytes 786432 | tf_op jit(solution)/shard_map/concatenate | solution.py:411
  1.7 3.0 %collective-permute-start.5 = (f32[3,8,2048]{2,1,0:T(8,128)S(1)}, f32[3,8,2048]{2,1,0:T(8,128)S(1)}, u32[]{:S(2)}, u32[]{:S(2)}) collective-permute-start(f32[3,8,2048]{2,1,0:T(8,128)S(1)} %get-tuple-element.17.second_half.other.fields.mine), channel_id=1, source_target_pairs={{0,16},{4,20},{8,24},{12,28},{16,0},{20,4},{24,8},{28,12},{1,17},{... | collective-permute-start | bytes 589832 | tf_op jit(solution)/shard_map/ppermute | solution.py:356
  4.8 1.3 %collective-permute-start.2 = (f32[16,2048]{1,0:T(8,128)S(1)}, f32[16,2048]{1,0:T(8,128)S(1)}, u32[]{:S(2)}, u32[]{:S(2)}) collective-permute-start(f32[16,2048]{1,0:T(8,128)S(1)} %bitcast.11), channel_id=1, source_target_pairs={{1,0},{2,1},{3,2},{5,4},{6,5},{7,6},{9,8},{10,9},{11,10},{13,12},{... | collective-permute-start | bytes 393224 | tf_op jit(solution)/shard_map/ppermute | solution.py:351
  6.1 4.6 %collective-permute-start.3 = (f32[16,2048]{1,0:T(8,128)S(1)}, f32[16,2048]{1,0:T(8,128)S(1)}, u32[]{:S(2)}, u32[]{:S(2)}) collective-permute-start(f32[16,2048]{1,0:T(8,128)S(1)} %bitcast.12), channel_id=1, source_target_pairs={{0,1},{1,2},{2,3},{4,5},{5,6},{6,7},{8,9},{9,10},{10,11},{12,13},{... | collective-permute-start | bytes 393224 | tf_op jit(solution)/shard_map/ppermute | solution.py:351
  10.6 0.0 copy-start
  10.6 0.0 copy-start.1
  10.6 0.0 copy-start.4
  10.7 0.0 copy-start.5
  10.7 0.1 collective-permute-start.4
  10.8 1.5 %collective-permute-start.1 = (f32[3,8,2048]{2,1,0:T(8,128)S(1)}, f32[3,8,2048]{2,1,0:T(8,128)S(1)}, u32[]{:S(2)}, u32[]{:S(2)}) collective-permute-start(f32[3,8,2048]{2,1,0:T(8,128)S(1)} %get-tuple-element.16.first_half.fields.mine.other), channel_id=1, source_target_pairs={{0,16},{4,20},{8,24},{12,28},{16,0},{20,4},{24,8},{28,12},{1,17},{... | collective-permute-start | bytes 589832 | tf_op jit(solution)/shard_map/ppermute | solution.py:356
  12.3 0.4 %own_spectrum.5.spectrum = f32[416,256]{1,0:T(8,128)S(1)} custom-call(f32[3,8,2048]{2,1,0:T(8,128)S(1)} %get-tuple-element.17.second_half.other.fields.mine, f32[34,128]{1,0:T(8,128)S(1)} %copy-done.5, f32[51,256]{1,0:T(8,128)S(1)} %copy-done.4, bf16[256,256]{1,0:T(8,128)(2,1)S(1)} %copy-done, bf16[256,256]{1,0:T(8,128)(2,1)S(1)} %copy-done.1), custom_call_target="tpu_custom_call" | custom-call | tf_op jit(solution)/shard_map/own_spectrum/pallas_call | solution.py:418
  12.8 0.4 %own_spectrum.4.spectrum = f32[416,256]{1,0:T(8,128)S(1)} custom-call(f32[3,8,2048]{2,1,0:T(8,128)S(1)} %get-tuple-element.16.first_half.fields.mine.other, f32[34,128]{1,0:T(8,128)S(1)} %copy-done.5, f32[51,256]{1,0:T(8,128)S(1)} %copy-done.4, bf16[256,256]{1,0:T(8,128)(2,1)S(1)} %copy-done, bf16[256,256]{1,0:T(8,128)(2,1)S(1)} %copy-done.1), custom_call_target="tpu_custom_call" | custom-call | tf_op jit(solution)/shard_map/own_spectrum/pallas_call | solution.py:418
  13.2 1.5 %collective-permute-start = (f32[8,2304]{1,0:T(8,128)S(1)}, f32[8,2304]{1,0:T(8,128)S(1)}, u32[]{:S(2)}, u32[]{:S(2)}) collective-permute-start(f32[8,2304]{1,0:T(8,128)S(1)} %get-tuple-element.8), channel_id=1, source_target_pairs={{0,4},{4,8},{8,12},{12,16},{16,20},{20,24},{24,28},{28,0},{1,5},{5... | collective-permute-start | bytes 221192 | tf_op jit(solution)/shard_map/ppermute | solution.py:351
  14.8 1.6 %advance_half.5 = (f32[3,8,2048]{2,1,0:T(8,128)S(1)}, f32[8,2304]{1,0:T(8,128)S(1)}) custom-call(f32[3,8,2048]{2,1,0:T(8,128)S(1)} %get-tuple-element.17.second_half.other.fields.mine, f32[3,8,2048]{2,1,0:T(8,128)S(1)} %get-tuple-element.16.first_half.fields.mine.other, f32[8,2304]{1,0:T(8,128)S(1)} %collective-permute-done.4.halo, ...), custom_call_target="tpu_custom_call" | custom-call | tf_op jit(solution)/shard_map/advance_half/pallas_call | solution.py:395
  16.4 0.3 collective-permute-start.11
  16.7 1.4 %collective-permute-done.halo = f32[8,2304]{1,0:T(8,128)S(1)} collective-permute-done((f32[8,2304]{1,0:T(8,128)S(1)}, f32[8,2304]{1,0:T(8,128)S(1)}, u32[]{:S(2)}, u32[]{:S(2)}) %collective-permute-start) | collective-permute-done | bytes 73760 | tf_op jit(solution)/shard_map/ppermute | solution.py:351
  18.0 0.9 %collective-permute-done.1.far = f32[3,8,2048]{2,1,0:T(8,128)S(1)} collective-permute-done((f32[3,8,2048]{2,1,0:T(8,128)S(1)}, f32[3,8,2048]{2,1,0:T(8,128)S(1)}, u32[]{:S(2)}, u32[]{:S(2)}) %collective-permute-start.1) | collective-permute-done | bytes 196640 | tf_op jit(solution)/shard_map/ppermute | solution.py:356
  18.9 1.6 %advance_half.4 = (f32[3,8,2048]{2,1,0:T(8,128)S(1)}, f32[8,2304]{1,0:T(8,128)S(1)}) custom-call(f32[3,8,2048]{2,1,0:T(8,128)S(1)} %get-tuple-element.16.first_half.fields.mine.other, f32[3,8,2048]{2,1,0:T(8,128)S(1)} %get-tuple-element.17.second_half.other.fields.mine, f32[8,2304]{1,0:T(8,128)S(1)} %collective-permute-done.halo, ...), custom_call_target="tpu_custom_call" | custom-call | tf_op jit(solution)/shard_map/advance_half/pallas_call | solution.py:395
  20.5 0.3 collective-permute-start.7
  20.9 2.0 %collective-permute-start.10 = (f32[8,2304]{1,0:T(8,128)S(1)}, f32[8,2304]{1,0:T(8,128)S(1)}, u32[]{:S(2)}, u32[]{:S(2)}) collective-permute-start(f32[8,2304]{1,0:T(8,128)S(1)} %get-tuple-element.13), channel_id=1, source_target_pairs={{0,28},{4,0},{8,4},{12,8},{16,12},{20,16},{24,20},{28,24},{1,29},{... | collective-permute-start | bytes 221192 | tf_op jit(solution)/shard_map/ppermute | solution.py:351
  22.9 1.3 %collective-permute-start.8 = (f32[16,2048]{1,0:T(8,128)S(1)}, f32[16,2048]{1,0:T(8,128)S(1)}, u32[]{:S(2)}, u32[]{:S(2)}) collective-permute-start(f32[16,2048]{1,0:T(8,128)S(1)} %pad_maximum_fusion.3), channel_id=1, source_target_pairs={{1,0},{2,1},{3,2},{5,4},{6,5},{7,6},{9,8},{10,9},{11,10},{13,12},{... | collective-permute-start | bytes 393224 | tf_op jit(solution)/shard_map/ppermute | solution.py:351
  24.2 4.6 %collective-permute-start.9 = (f32[16,2048]{1,0:T(8,128)S(1)}, f32[16,2048]{1,0:T(8,128)S(1)}, u32[]{:S(2)}, u32[]{:S(2)}) collective-permute-start(f32[16,2048]{1,0:T(8,128)S(1)} %pad_maximum_fusion.3), channel_id=1, source_target_pairs={{0,1},{1,2},{2,3},{4,5},{5,6},{6,7},{8,9},{9,10},{10,11},{12,13},{... | collective-permute-start | bytes 393224 | tf_op jit(solution)/shard_map/ppermute | solution.py:351
  28.8 0.1 collective-permute-start.6
  28.8 0.4 %own_spectrum.7.spectrum = f32[416,256]{1,0:T(8,128)S(1)} custom-call(f32[3,8,2048]{2,1,0:T(8,128)S(1)} %get-tuple-element.11.other.fields.mine, f32[34,128]{1,0:T(8,128)S(1)} %copy-done.5, f32[51,256]{1,0:T(8,128)S(1)} %copy-done.4, bf16[256,256]{1,0:T(8,128)(2,1)S(1)} %copy-done, bf16[256,256]{1,0:T(8,128)(2,1)S(1)} %copy-done.1), custom_call_target="tpu_custom_call" | custom-call | tf_op jit(solution)/shard_map/own_spectrum/pallas_call | solution.py:418
  29.2 0.4 %own_spectrum.6.spectrum = f32[416,256]{1,0:T(8,128)S(1)} custom-call(f32[3,8,2048]{2,1,0:T(8,128)S(1)} %get-tuple-element.9.fields.mine.other, f32[34,128]{1,0:T(8,128)S(1)} %copy-done.5, f32[51,256]{1,0:T(8,128)S(1)} %copy-done.4, bf16[256,256]{1,0:T(8,128)(2,1)S(1)} %copy-done, bf16[256,256]{1,0:T(8,128)(2,1)S(1)} %copy-done.1), custom_call_target="tpu_custom_call" | custom-call | tf_op jit(solution)/shard_map/own_spectrum/pallas_call | solution.py:418
  29.6 0.1 collective-permute-done.8.above
  29.7 1.5 %collective-permute-done.9.below = f32[16,2048]{1,0:T(8,128)S(1)} collective-permute-done((f32[16,2048]{1,0:T(8,128)S(1)}, f32[16,2048]{1,0:T(8,128)S(1)}, u32[]{:S(2)}, u32[]{:S(2)}) %collective-permute-start.9) | collective-permute-done | bytes 131104 | tf_op jit(solution)/shard_map/ppermute | solution.py:351
  31.2 1.6 %advance_half.7 = f32[3,8,2048]{2,1,0:T(8,128)S(1)} custom-call(f32[3,8,2048]{2,1,0:T(8,128)S(1)} %get-tuple-element.11.other.fields.mine, f32[3,8,2048]{2,1,0:T(8,128)S(1)} %get-tuple-element.9.fields.mine.other, f32[8,2304]{1,0:T(8,128)S(1)} %collective-permute-done.10.halo, f32[3,8,2048]{2,1,0:T(8,128)S(1)} %collective-permute-done.11.far, ...), custom_call_target="tpu_custom_call" | custom-call | tf_op jit(solution)/shard_map/advance_half/pallas_call | solution.py:395
  32.8 0.6 %collective-permute-done.6.halo = f32[8,2304]{1,0:T(8,128)S(1)} collective-permute-done((f32[8,2304]{1,0:T(8,128)S(1)}, f32[8,2304]{1,0:T(8,128)S(1)}, u32[]{:S(2)}, u32[]{:S(2)}) %collective-permute-start.6) | collective-permute-done | bytes 73760 | tf_op jit(solution)/shard_map/ppermute | solution.py:351
  33.5 1.6 %advance_half.6 = f32[3,8,2048]{2,1,0:T(8,128)S(1)} custom-call(f32[3,8,2048]{2,1,0:T(8,128)S(1)} %get-tuple-element.9.fields.mine.other, f32[3,8,2048]{2,1,0:T(8,128)S(1)} %get-tuple-element.11.other.fields.mine, f32[8,2304]{1,0:T(8,128)S(1)} %collective-permute-done.6.halo, f32[3,8,2048]{2,1,0:T(8,128)S(1)} %collective-permute-done.7.far, ...), custom_call_target="tpu_custom_call" | custom-call | tf_op jit(solution)/shard_map/advance_half/pallas_call | solution.py:395
  35.1 0.7 %pad_maximum_fusion.2 = f32[1,16,2048]{2,1,0:T(8,128)} fusion(f32[3,8,2048]{2,1,0:T(8,128)S(1)} %advance_half.7, f32[3,8,2048]{2,1,0:T(8,128)S(1)} %advance_half.6), kind=kLoop, calls=%fused_computation.6 | loop fusion | flops 32768 | bytes 524288 | tf_op jit(solution)/shard_map/slice | solution.py:452
  35.7 0.7 %fusion = f32[2,1,16,2048]{3,2,1,0:T(8,128)} fusion(f32[3,8,2048]{2,1,0:T(8,128)S(1)} %advance_half.7, f32[3,8,2048]{2,1,0:T(8,128)S(1)} %advance_half.6), kind=kLoop, calls=%fused_computation.3 | loop fusion | flops 65536 | bytes 655360
  (25 shorter events, 0.1 us)
Async XLA Ops:
  0.6 4.1 %copy-start.8 = (f32[1,16,2048]{2,1,0:T(8,128)S(1)}, f32[1,16,2048]{2,1,0:T(8,128)}, u32[]{:S(2)}) copy-start(f32[1,16,2048]{2,1,0:T(8,128)} %param.10) | copy-start | bytes 393220
  1.7 13.0 %collective-permute-start.5 = (f32[3,8,2048]{2,1,0:T(8,128)S(1)}, f32[3,8,2048]{2,1,0:T(8,128)S(1)}, u32[]{:S(2)}, u32[]{:S(2)}) collective-permute-start(f32[3,8,2048]{2,1,0:T(8,128)S(1)} %get-tuple-element.17.second_half.other.fields.mine), channel_id=1, source_target_pairs={{0,16},{4,20},{8,24},{12,28},{16,0},{20,4},{24,8},{28,12},{1,17},{... | collective-permute-start | bytes 589832 | tf_op jit(solution)/shard_map/ppermute | solution.py:356
  4.8 10.0 %collective-permute-start.2 = (f32[16,2048]{1,0:T(8,128)S(1)}, f32[16,2048]{1,0:T(8,128)S(1)}, u32[]{:S(2)}, u32[]{:S(2)}) collective-permute-start(f32[16,2048]{1,0:T(8,128)S(1)} %bitcast.11), channel_id=1, source_target_pairs={{1,0},{2,1},{3,2},{5,4},{6,5},{7,6},{9,8},{10,9},{11,10},{13,12},{... | collective-permute-start | bytes 393224 | tf_op jit(solution)/shard_map/ppermute | solution.py:351
  6.1 8.7 %collective-permute-start.3 = (f32[16,2048]{1,0:T(8,128)S(1)}, f32[16,2048]{1,0:T(8,128)S(1)}, u32[]{:S(2)}, u32[]{:S(2)}) collective-permute-start(f32[16,2048]{1,0:T(8,128)S(1)} %bitcast.12), channel_id=1, source_target_pairs={{0,1},{1,2},{2,3},{4,5},{5,6},{6,7},{8,9},{9,10},{10,11},{12,13},{... | collective-permute-start | bytes 393224 | tf_op jit(solution)/shard_map/ppermute | solution.py:351
  10.6 1.7 %copy-start = (bf16[256,256]{1,0:T(8,128)(2,1)S(1)}, bf16[256,256]{1,0:T(8,128)(2,1)}, u32[]{:S(2)}) copy-start(bf16[256,256]{1,0:T(8,128)(2,1)} %constant.16.clone.high.forward_high) | copy-start | bytes 393220
  10.6 1.7 %copy-start.1 = (bf16[256,256]{1,0:T(8,128)(2,1)S(1)}, bf16[256,256]{1,0:T(8,128)(2,1)}, u32[]{:S(2)}) copy-start(bf16[256,256]{1,0:T(8,128)(2,1)} %constant.17.clone.low.forward_low) | copy-start | bytes 393220
  10.6 1.7 %copy-start.4 = (f32[51,256]{1,0:T(8,128)S(1)}, f32[51,256]{1,0:T(8,128)}, u32[]{:S(2)}) copy-start(f32[51,256]{1,0:T(8,128)} %constant.22.clone.masks) | copy-start | bytes 156676
  10.7 1.7 %copy-start.5 = (f32[34,128]{1,0:T(8,128)S(1)}, f32[34,128]{1,0:T(8,128)}, u32[]{:S(2)}) copy-start(f32[34,128]{1,0:T(8,128)} %constant.20.clone.twist) | copy-start | bytes 52228
  10.7 2.5 %collective-permute-start.4 = (f32[8,2304]{1,0:T(8,128)S(1)}, f32[8,2304]{1,0:T(8,128)S(1)}, u32[]{:S(2)}, u32[]{:S(2)}) collective-permute-start(f32[8,2304]{1,0:T(8,128)S(1)} %get-tuple-element.10), channel_id=1, source_target_pairs={{0,28},{4,0},{8,4},{12,8},{16,12},{20,16},{24,20},{28,24},{1,29},{... | collective-permute-start | bytes 221192 | tf_op jit(solution)/shard_map/ppermute | solution.py:351
  10.8 8.1 %collective-permute-start.1 = (f32[3,8,2048]{2,1,0:T(8,128)S(1)}, f32[3,8,2048]{2,1,0:T(8,128)S(1)}, u32[]{:S(2)}, u32[]{:S(2)}) collective-permute-start(f32[3,8,2048]{2,1,0:T(8,128)S(1)} %get-tuple-element.16.first_half.fields.mine.other), channel_id=1, source_target_pairs={{0,16},{4,20},{8,24},{12,28},{16,0},{20,4},{24,8},{28,12},{1,17},{... | collective-permute-start | bytes 589832 | tf_op jit(solution)/shard_map/ppermute | solution.py:356
  12.7 2.0 %copy-start.2 = (bf16[256,512]{1,0:T(8,128)(2,1)S(1)}, bf16[256,512]{1,0:T(8,128)(2,1)}, u32[]{:S(2)}) copy-start(bf16[256,512]{1,0:T(8,128)(2,1)} %constant.18.clone.inverse_high) | copy-start | bytes 786436
  12.8 2.0 %copy-start.3 = (bf16[256,512]{1,0:T(8,128)(2,1)S(1)}, bf16[256,512]{1,0:T(8,128)(2,1)}, u32[]{:S(2)}) copy-start(bf16[256,512]{1,0:T(8,128)(2,1)} %constant.19.clone.inverse_low) | copy-start | bytes 786436
  12.8 2.0 %copy-start.6 = (f32[68,128]{1,0:T(8,128)S(1)}, f32[68,128]{1,0:T(8,128)}, u32[]{:S(2)}) copy-start(f32[68,128]{1,0:T(8,128)} %constant.21.clone.back) | copy-start | bytes 104452
  12.8 2.0 %copy-start.7 = (f32[2,2048]{1,0:T(2,128)S(1)}, f32[2,2048]{1,0:T(2,128)}, u32[]{:S(2)}) copy-start(f32[2,2048]{1,0:T(2,128)} %constant.23.clone.rows) | copy-start | bytes 49156
  13.2 4.8 %collective-permute-start = (f32[8,2304]{1,0:T(8,128)S(1)}, f32[8,2304]{1,0:T(8,128)S(1)}, u32[]{:S(2)}, u32[]{:S(2)}) collective-permute-start(f32[8,2304]{1,0:T(8,128)S(1)} %get-tuple-element.8), channel_id=1, source_target_pairs={{0,4},{4,8},{8,12},{12,16},{16,20},{20,24},{24,28},{28,0},{1,5},{5... | collective-permute-start | bytes 221192 | tf_op jit(solution)/shard_map/ppermute | solution.py:351
  16.4 14.9 %collective-permute-start.11 = (f32[3,8,2048]{2,1,0:T(8,128)S(1)}, f32[3,8,2048]{2,1,0:T(8,128)S(1)}, u32[]{:S(2)}, u32[]{:S(2)}) collective-permute-start(f32[3,8,2048]{2,1,0:T(8,128)S(1)} %get-tuple-element.11.other.fields.mine), channel_id=1, source_target_pairs={{0,16},{4,20},{8,24},{12,28},{16,0},{20,4},{24,8},{28,12},{1,17},{... | collective-permute-start | bytes 589832 | tf_op jit(solution)/shard_map/ppermute | solution.py:356
  20.5 13.0 %collective-permute-start.7 = (f32[3,8,2048]{2,1,0:T(8,128)S(1)}, f32[3,8,2048]{2,1,0:T(8,128)S(1)}, u32[]{:S(2)}, u32[]{:S(2)}) collective-permute-start(f32[3,8,2048]{2,1,0:T(8,128)S(1)} %get-tuple-element.9.fields.mine.other), channel_id=1, source_target_pairs={{0,16},{4,20},{8,24},{12,28},{16,0},{20,4},{24,8},{28,12},{1,17},{... | collective-permute-start | bytes 589832 | tf_op jit(solution)/shard_map/ppermute | solution.py:356
  20.9 7.9 %collective-permute-start.10 = (f32[8,2304]{1,0:T(8,128)S(1)}, f32[8,2304]{1,0:T(8,128)S(1)}, u32[]{:S(2)}, u32[]{:S(2)}) collective-permute-start(f32[8,2304]{1,0:T(8,128)S(1)} %get-tuple-element.13), channel_id=1, source_target_pairs={{0,28},{4,0},{8,4},{12,8},{16,12},{20,16},{24,20},{28,24},{1,29},{... | collective-permute-start | bytes 221192 | tf_op jit(solution)/shard_map/ppermute | solution.py:351
  22.9 6.9 %collective-permute-start.8 = (f32[16,2048]{1,0:T(8,128)S(1)}, f32[16,2048]{1,0:T(8,128)S(1)}, u32[]{:S(2)}, u32[]{:S(2)}) collective-permute-start(f32[16,2048]{1,0:T(8,128)S(1)} %pad_maximum_fusion.3), channel_id=1, source_target_pairs={{1,0},{2,1},{3,2},{5,4},{6,5},{7,6},{9,8},{10,9},{11,10},{13,12},{... | collective-permute-start | bytes 393224 | tf_op jit(solution)/shard_map/ppermute | solution.py:351
  24.2 7.1 %collective-permute-start.9 = (f32[16,2048]{1,0:T(8,128)S(1)}, f32[16,2048]{1,0:T(8,128)S(1)}, u32[]{:S(2)}, u32[]{:S(2)}) collective-permute-start(f32[16,2048]{1,0:T(8,128)S(1)} %pad_maximum_fusion.3), channel_id=1, source_target_pairs={{0,1},{1,2},{2,3},{4,5},{5,6},{6,7},{8,9},{9,10},{10,11},{12,13},{... | collective-permute-start | bytes 393224 | tf_op jit(solution)/shard_map/ppermute | solution.py:351
  28.8 4.7 %collective-permute-start.6 = (f32[8,2304]{1,0:T(8,128)S(1)}, f32[8,2304]{1,0:T(8,128)S(1)}, u32[]{:S(2)}, u32[]{:S(2)}) collective-permute-start(f32[8,2304]{1,0:T(8,128)S(1)} %get-tuple-element.12), channel_id=1, source_target_pairs={{0,4},{4,8},{8,12},{12,16},{16,20},{20,24},{24,28},{28,0},{1,5},{5... | collective-permute-start | bytes 221192 | tf_op jit(solution)/shard_map/ppermute | solution.py:351

commit v2 on v1

v2 whole, which is shorter than its diff:
```python
import functools
import math

import jax
import jax.numpy as jnp
import numpy as np
from jax import lax
from jax.experimental import pallas as pl
from jax.experimental.pallas import tpu as pltpu
from jax.sharding import PartitionSpec as P

STEPS = 2

courant = 0.2
mixing = 0.25
coriolis = 0.5
cos_floor = 0.25

RADIX = 128
ROWS = 8
TRANSFORM_COST = 10_000_000_000
PIECES = 4
HALO = 3


def split_table(table):
    high = table.astype(np.float32).astype(jnp.bfloat16)
    low = (table - high.astype(np.float64)).astype(np.float32).astype(jnp.bfloat16)
    return jnp.asarray(high), jnp.asarray(low)


@functools.lru_cache(maxsize=None)
def numpy_tables(lat_count):
    length = 2 * lat_count
    blocks = length // RADIX
    kept = blocks // 2 + 1
    centred = np.arange(RADIX) + 0.5
    order = np.arange(RADIX)
    signed = np.where(order < RADIX // 2, order, order - RADIX).astype(np.float64)
    angle = 2.0 * np.pi / RADIX * centred[:, None] * signed[None, :]
    cos, sin = np.cos(angle), np.sin(angle)
    forward = np.block([[cos, -sin], [sin, cos]])
    cos_t, sin_t = cos.T, sin.T
    weight = signed[:, None]
    inverse = np.block(
        [
            [cos_t, sin_t, -weight * sin_t, weight * cos_t],
            [-sin_t, cos_t, -weight * cos_t, -weight * sin_t],
        ]
    )
    first = np.arange(kept)
    turn = 2.0 * np.pi / length * first[:, None] * centred[None, :]
    twist = np.stack([np.cos(turn), -np.sin(turn)], 1)
    share = np.where((first == 0) | (first == blocks // 2), 1.0, 2.0)[:, None] / length
    back = np.stack([np.cos(turn) * share, np.sin(turn) * share], 1)
    slope_scale = 2.0 * np.pi * blocks / length
    back = np.concatenate([back, back * slope_scale], 1)
    wave = first[:, None] + blocks * signed[None, :]
    retained = (np.abs(wave) <= length // 3).astype(np.float64)
    plus = np.concatenate([retained, retained], 1)
    minus = np.concatenate([retained, -retained], 1)
    masks = np.stack([plus, minus, -minus], 1)
    latitude = (np.arange(lat_count) + 0.5) * (np.pi / lat_count) - 0.5 * np.pi
    rows = np.stack(
        [1.0 / np.maximum(np.cos(latitude), cos_floor), coriolis * np.sin(latitude)]
    )
    flat = lambda a: a.reshape(-1, a.shape[-1]).astype(np.float32)
    return forward, inverse, flat(twist), flat(back), flat(masks), rows.astype(np.float32)


def times(value, angle):
    real, imag = value
    cos, sin = math.cos(angle), math.sin(angle)
    quarter = round(angle / (math.pi / 2), 9)
    if quarter == int(quarter):
        turn = int(quarter) % 4
        return [(real, imag), (-imag, real), (-real, -imag), (imag, -real)][turn]
    if abs(abs(cos) - abs(sin)) < 1e-12:
        scale = abs(cos)
        a = real if cos > 0 else -real
        b = imag if cos > 0 else -imag
        c = imag if sin > 0 else -imag
        d = real if sin > 0 else -real
        return (scale * (a - c), scale * (b + d))
    return (real * cos - imag * sin, imag * cos + real * sin)


def add(a, b):
    return (a[0] + b[0], a[1] + b[1])


def sub(a, b):
    return (a[0] - b[0], a[1] - b[1])


def complex_dft(values, sign):
    n = len(values)
    if n == 1:
        return values
    half = n // 2
    even = complex_dft([add(values[m], values[m + half]) for m in range(half)], sign)
    odd = complex_dft(
        [
            times(sub(values[m], values[m + half]), sign * 2 * math.pi * m / n)
            for m in range(half)
        ],
        sign,
    )
    return [even[q // 2] if q % 2 == 0 else odd[q // 2] for q in range(n)]


def odd_outputs(values):
    r = len(values)
    if r == 1:
        return {1: (values[0], None)}
    half = r // 2
    turned = [
        times((values[m], -values[m + half]), -math.pi * m / r) for m in range(half)
    ]
    out = {}
    for q, value in enumerate(complex_dft(turned, -1)):
        j = 4 * q + 1
        out[j if j <= r else 2 * r - j] = value if j <= r else (value[0], -value[1])
    return out


def half_circle_forward(values):
    n = len(values)
    out = {j: value for j, value in odd_outputs(values).items()}
    scale = 2
    while len(values) > 1:
        half = len(values) // 2
        difference = [values[m] - values[m + half] for m in range(half)]
        values = [values[m] + values[m + half] for m in range(half)]
        for j, value in odd_outputs(difference).items():
            out[j * scale] = value
        scale *= 2
    out[0] = (values[0], None)
    return [out[k] for k in range(n + 1)]


def odd_inputs(values, r):
    if r == 1:
        return [values[1][0]]
    half = r // 2
    gathered = []
    for q in range(half):
        j = 4 * q + 1
        if j <= r:
            gathered.append(values[j])
        else:
            real, imag = values[2 * r - j]
            gathered.append((real, -imag))
    turned = [
        times(value, math.pi * m / r) for m, value in enumerate(complex_dft(gathered, 1))
    ]
    return [value[0] for value in turned] + [-value[1] for value in turned]


def half_circle_inverse(values):
    n = len(values) - 1
    result = [values[0][0]]
    size = 1
    while size < n:
        step = n // size
        difference = odd_inputs({j: values[j * step] for j in range(1, size + 1, 2)}, size)
        result = [result[m] + difference[m] for m in range(size)] + [
            result[m] - difference[m] for m in range(size)
        ]
        size *= 2
    last = odd_inputs({j: values[j] for j in range(1, n + 1, 2)}, n)
    return [result[m] + last[m] for m in range(n)]


def tile(index):
    return pl.ds(index * RADIX, RADIX)


def split(value):
    high = value.astype(jnp.bfloat16)
    return high, (value - high.astype(jnp.float32)).astype(jnp.bfloat16)


def triple_product(value, high_table, low_table):
    high, low = split(value)
    dot = functools.partial(jnp.dot, preferred_element_type=jnp.float32)
    return dot(high, high_table) + dot(low, high_table) + dot(high, low_table)


def forward_stage(slabs_of, groups, twist, turned, blocks):
    for group in range(groups):
        slabs = slabs_of(group)
        for k, (real, imag) in enumerate(half_circle_forward(slabs)):
            at = pl.ds((k * groups + group) * ROWS, ROWS)
            cos, sin = twist[2 * k : 2 * k + 1, :], twist[2 * k + 1 : 2 * k + 2, :]
            if imag is None:
                turned[at, tile(0)] = real * cos
                turned[at, tile(1)] = real * sin
            else:
                turned[at, tile(0)] = real * cos - imag * sin
                turned[at, tile(1)] = real * sin + imag * cos


def reader(fields, tiles):
    per_field = fields.shape[1] // ROWS

    def slabs_of(group):
        field, part = divmod(group, per_field)
        return [fields[field, part * ROWS : part * ROWS + ROWS, tile(m)] for m in range(tiles)]

    return slabs_of


def pack_rows(pack, lat_count, field, index, rows):
    if field < 2:
        pack[HALO * field : HALO * field + HALO, tile(index)] = rows
    else:
        pack[2 * HALO : ROWS, tile(index)] = rows[: ROWS - 2 * HALO]
        pack[index // 2 : index // 2 + 1, pl.ds(lat_count + index % 2 * RADIX, RADIX)] = rows[
            ROWS - 2 * HALO :
        ]


def halo_rows(pack, lat_count, field, index):
    if field < 2:
        return pack[HALO * field : HALO * field + HALO, tile(index)]
    last = pack[index // 2 : index // 2 + 1, pl.ds(lat_count + index % 2 * RADIX, RADIX)]
    return jnp.concatenate([pack[2 * HALO : ROWS, tile(index)], last], 0)


def field_of(height, wind, field, index):
    return height[0, :, tile(index)] if field == 0 else wind[field - 1, :, tile(index)]


def odd_device():
    return lax.rem(lax.axis_index("lon"), 2) == 1


def pack_edge(height, wind, pack, first):
    lat_count = height.shape[-1]
    for field in range(3):
        for index in range(lat_count // RADIX):
            rows = field_of(height, wind, field, index)
            chosen = jnp.where(first, rows[:HALO], rows[rows.shape[0] - HALO :])
            pack_rows(pack, lat_count, field, index, chosen)


def gather_kernel(fields, height, wind, near_pack):
    height[...] = fields[:1]
    wind[...] = fields[1:]
    pack_edge(height, wind, near_pack, odd_device())


def own_kernel(blocks, near, height, wind, twist, masks, high, low, *rest):
    spectra, (far_pack, height_copy), turned = rest[:2], rest[2:4], rest[4:]
    pack_edge(height, wind, far_pack, jnp.logical_not(odd_device()))
    height_copy[...] = height[...]
    kept = blocks // 2 + 1
    for fields, spectrum, work in zip((height, wind), spectra, turned):
        span = fields.shape[0] * fields.shape[1]
        forward_stage(reader(fields, blocks // 2), span // ROWS, twist, work, blocks)
        result = triple_product(work[...], high[...], low[...])
        for k in range(kept):
            at = k * span
            spectrum[at : at + span, :] = result[at : at + span, :] * masks[3 * k : 3 * k + 1, :]


def far_kernel(
    blocks,
    parity,
    far,
    spectrum,
    twist,
    back,
    masks,
    forward_high,
    forward_low,
    inverse_high,
    inverse_low,
    *rest,
):
    smooth, slope, turned, weighted, spread = rest[-5:]
    kept = blocks // 2 + 1
    tiles = blocks // 2
    count, lon_count = far.shape[:2]
    per_field = lon_count // ROWS
    groups = count * per_field
    length = blocks * RADIX
    forward_stage(reader(far, tiles), groups, twist, turned, blocks)
    result = triple_product(turned[...], forward_high[...], forward_low[...])
    span = groups * ROWS
    for k in range(kept):
        at = k * span
        row = 3 * k + (1 if parity > 0 else 2)
        weighted[at : at + span, :] = (
            spectrum[at : at + span, :] + result[at : at + span, :] * masks[row : row + 1, :]
        )
    spread[...] = triple_product(weighted[...], inverse_high[...], inverse_low[...])
    for group in range(groups):
        field, part = divmod(group, per_field)
        out = slice(part * ROWS, part * ROWS + ROWS)
        smooth_terms, slope_terms = [], []
        for k in range(kept):
            at = pl.ds((k * groups + group) * ROWS, ROWS)
            real, imag, slope_real, slope_imag = [spread[at, tile(i)] for i in range(4)]
            cos, sin, slope_cos, slope_sin = [back[4 * k + i : 4 * k + i + 1, :] for i in range(4)]
            turn_real = real * cos - imag * sin
            turn_imag = real * sin + imag * cos
            wave = 2.0 * math.pi * k / length
            smooth_terms.append((turn_real, turn_imag))
            slope_terms.append(
                (
                    slope_real * slope_cos - slope_imag * slope_sin - wave * turn_imag,
                    slope_real * slope_sin + slope_imag * slope_cos + wave * turn_real,
                )
            )
        for m, value in enumerate(half_circle_inverse(smooth_terms)):
            smooth[field, out, tile(m)] = value
        for m, value in enumerate(half_circle_inverse(slope_terms)):
            slope[field, out, tile(m)] = value


def update_kernel(
    final,
    height,
    wind,
    near,
    far,
    first_level,
    second_level,
    height_smooth,
    height_slope,
    wind_smooth,
    wind_slope,
    rows,
    *outs,
):
    lon_count, lat_count = height.shape[1:]
    tiles = lat_count // RADIX
    odd = odd_device()
    if final:
        height_out, wind_out, staged, sems = outs
    copies = []
    for index in range(tiles):
        here = [field_of(height, wind, field, index) for field in range(3)]
        zonal = []
        for field in range(3):
            close = halo_rows(near, lat_count, field, index)
            away = halo_rows(far, lat_count, field, index)
            line = jnp.concatenate(
                [jnp.where(odd, close, away), here[field], jnp.where(odd, away, close)], 0
            )
            at = [line[i : i + lon_count] for i in range(2 * HALO + 1)]
            zonal.append(
                (45.0 / 60.0) * (at[4] - at[2])
                - (9.0 / 60.0) * (at[5] - at[1])
                + (1.0 / 60.0) * (at[6] - at[0])
            )
        thick, east, north = here
        secant, turning = rows[0:1, tile(index)], rows[1:2, tile(index)]
        vertical = first_level[0, :, tile(index)] + second_level[0, :, tile(index)] - 2.0 * thick
        zonal = [secant * value for value in zonal]
        slopes = [
            height_slope[0, :, tile(index)],
            wind_slope[0, :, tile(index)],
            wind_slope[1, :, tile(index)],
        ]
        smooths = [
            height_smooth[0, :, tile(index)],
            wind_smooth[0, :, tile(index)],
            wind_smooth[1, :, tile(index)],
        ]
        advect = [east * zonal[field] + north * slopes[field] for field in range(3)]
        tendency = [
            mixing * vertical - advect[0] - thick * (zonal[1] + slopes[2]),
            turning * north - advect[1] - zonal[0],
            -advect[2] - slopes[0] - turning * east,
        ]
        values = [smooths[field] + courant * tendency[field] for field in range(3)]
        if final:
            for field in range(3):
                staged[field, :, tile(index)] = values[field]
            if (index + 1) % (tiles // PIECES) == 0:
                piece = (index + 1) // (tiles // PIECES) - 1
                at = pl.ds(piece * (lat_count // PIECES), lat_count // PIECES)
                for field in range(3):
                    target = (
                        height_out.at[0, :, at] if field == 0 else wind_out.at[field - 1, :, at]
                    )
                    copy = pltpu.make_async_copy(
                        staged.at[field, :, at], target, sems.at[piece * 3 + field]
                    )
                    copy.start()
                    copies.append(copy)
        else:
            height_next, wind_next, near_pack = outs
            height_next[0, :, tile(index)] = values[0]
            for field in range(1, 3):
                wind_next[field - 1, :, tile(index)] = values[field]
            for field in range(3):
                first, last = values[field][:HALO], values[field][lon_count - HALO :]
                pack_rows(near_pack, lat_count, field, index, jnp.where(odd, first, last))
    for copy in copies:
        copy.wait()


def vmem(count):
    return [pl.BlockSpec(memory_space=pltpu.VMEM)] * count


def anywhere(count):
    return [pl.BlockSpec(memory_space=pl.ANY)] * count


def params():
    return pltpu.CompilerParams(vmem_limit_bytes=24 * 1024 * 1024)


def exchange(value, axis, first):
    size = lax.axis_size(axis)
    wrap = axis == "lon"
    pairs = [(i, (i + 1) % size) for i in range(first, size if wrap else size - 1, 2)]
    return lax.ppermute(value, axis, pairs + [(j, i) for i, j in pairs])


def from_antipode(value):
    size = lax.axis_size("lon")
    return lax.ppermute(value, "lon", [(i, (i + size // 2) % size) for i in range(size)])


def body(thickness, wind_field):
    level_count, lon_count, lat_count = thickness.shape
    assert level_count == 1 and lon_count % ROWS == 0
    blocks = 2 * lat_count // RADIX
    kept = blocks // 2 + 1
    forward, inverse, twist, back, masks, rows = numpy_tables(lat_count)
    forward_tables = split_table(forward)
    inverse_tables = split_table(inverse)
    twist, back, masks, rows = [jnp.asarray(a) for a in (twist, back, masks, rows)]
    f32 = jnp.float32
    array = lambda *shape: jax.ShapeDtypeStruct(shape, f32)
    scratch = lambda *shape: pltpu.VMEM(shape, f32)
    height_shape, wind_shape = array(1, lon_count, lat_count), array(2, lon_count, lat_count)
    pack_shape = array(ROWS, lat_count + lat_count // ROWS)
    spectral = lambda count, width: (count * kept * lon_count, width * RADIX)

    def call(kernel, name, outs, scratches, *args, in_specs=None, out_specs=None, cost=None):
        return pl.pallas_call(
            kernel,
            out_shape=outs,
            in_specs=in_specs or vmem(len(args)),
            out_specs=out_specs or vmem(len(outs)),
            scratch_shapes=scratches,
            compiler_params=params(),
            cost_estimate=cost
            and pl.CostEstimate(flops=cost, bytes_accessed=cost // 300, transcendentals=0),
            name=name,
        )(*args)

    def transform(count, parity, far, spectrum, *after):
        return call(
            functools.partial(far_kernel, blocks, parity),
            "antipode_transform",
            [array(count, lon_count, lat_count)] * 2,
            [scratch(*spectral(count, 2))] * 2 + [scratch(*spectral(count, 4))],
            far,
            spectrum,
            twist,
            back,
            masks,
            *forward_tables,
            *inverse_tables,
            *after,
            in_specs=vmem(9) + anywhere(len(after)),
            cost=TRANSFORM_COST,
        )

    far_wind = from_antipode(wind_field.reshape(wind_shape.shape))
    far_height = from_antipode(thickness)
    moving = [height_shape, wind_shape, pack_shape]
    fields = jnp.concatenate([thickness, wind_field.reshape(wind_shape.shape)], 0)
    height, wind, near_pack = call(gather_kernel, "gather_fields", moving, [], fields)
    for step in range(STEPS):
        near = exchange(near_pack, "lon", 0)
        height_spectrum, wind_spectrum, far_pack, height_copy = call(
            functools.partial(own_kernel, blocks),
            "own_spectra",
            [array(*spectral(1, 2)), array(*spectral(2, 2)), pack_shape, height_shape],
            [scratch(*spectral(1, 2)), scratch(*spectral(2, 2))],
            near,
            height,
            wind,
            twist,
            masks,
            *forward_tables,
            in_specs=anywhere(1) + vmem(6),
        )
        levels = [exchange(height_copy, "lev", first) for first in (0, 1)]
        far = exchange(far_pack, "lon", 1)
        wind_terms = transform(2, -1, far_wind, wind_spectrum)
        height_terms = transform(1, 1, far_height, height_spectrum, wind_terms[0])
        args = (height, wind, near, far, *levels, *height_terms, *wind_terms, rows)
        if step == STEPS - 1:
            height, wind = call(
                functools.partial(update_kernel, True),
                "update_fields",
                [height_shape, wind_shape],
                [scratch(3, lon_count, lat_count), pltpu.SemaphoreType.DMA((3 * PIECES,))],
                *args,
                out_specs=anywhere(2),
            )
            return height, wind.reshape(wind_field.shape)
        height, wind, near_pack = call(
            functools.partial(update_kernel, False),
            "update_fields",
            moving,
            [],
            *args,
        )
        far_wind, far_height = from_antipode(wind), from_antipode(height)


def solution(mesh):
    in_specs = (P("lev", "lon", None), P(None, "lev", "lon", None))
    out_specs = (P("lev", "lon", None), P(None, "lev", "lon", None))
    return jax.shard_map(body, mesh=mesh, in_specs=in_specs, out_specs=out_specs, check_vma=False)
```

time: 36.7 us -> 30.3 us (0.83)
  the two profiles are of different devices: /device:TPU:0 before, /device:TPU:10 now
where the time goes in v2:
time: 30.3 us; the launch traced here: 30.1 us
  starting transfers between devices  13.8 us (46%)
  Pallas kernels  8.3 us (27%)
  waiting for transfers between devices  6.03 us (20%)
  other arithmetic  1.05 us (3%)
  between operations  0.9 us (3%)
    ppermute x8, starting transfers between devices, exchange(): return lax.ppermute(value, axis, pairs + [(j, i) for i, j in pairs])  9.96 us
    pallas_call x9, Pallas kernels, call(): pl.pallas_call(kernel, out_shape=outs, in_specs=in_specs or vmem(len(args...  8.3 us
    ppermute x4, starting transfers between devices, from_antipode(): lax.ppermute(value, 'lon', [(i, (i + size // 2) % size) for i in range(si...  3.81 us
    ppermute x4, waiting for transfers between devices, from_antipode(): lax.ppermute(value, 'lon', [(i, (i + size // 2) % size) for i in range(si...  3.42 us
    ppermute x8, waiting for transfers between devices, exchange(): return lax.ppermute(value, axis, pairs + [(j, i) for i, j in pairs])  2.61 us
    concatenate x1, other arithmetic, body(): jnp.concatenate([thickness, wind_field.reshape(wind_shape.shape)], 0)  1.05 us
  transfers between devices with their start and end apart: 12, of which 4 were waited for; matrix products, arithmetic and copies ran while one was open for 3% of the time, Pallas kernels for 21%

profile of v2, /device:TPU:10, one launch (start us, length us, event | category | flops | bytes accessed | tf_op | source)
XLA Modules:
  0.0 30.1 jit_solution(5815105106490105008)
XLA Ops:
  0.6 1.6 %collective-permute-start.5 = (f32[2,16,2048]{2,1,0:T(8,128)}, f32[2,16,2048]{2,1,0:T(8,128)S(1)}, u32[]{:S(2)}, u32[]{:S(2)}) collective-permute-start(f32[2,16,2048]{2,1,0:T(8,128)} %bitcast.4), channel_id=1, source_target_pairs={{0,16},{4,20},{8,24},{12,28},{16,0},{20,4},{24,8},{28,12},{1,17},{... | collective-permute-start | bytes 786440 | tf_op jit(solution)/shard_map/ppermute | solution.py:428
  2.2 1.0 %pad_maximum_fusion.fields = f32[3,16,2048]{2,1,0:T(8,128)S(1)} fusion(f32[2,16,2048]{2,1,0:T(8,128)} %bitcast.5, f32[1,16,2048]{2,1,0:T(8,128)} %param.10), kind=kLoop, calls=%fused_computation | loop fusion | flops 98304 | bytes 786432 | tf_op jit(solution)/shard_map/concatenate | solution.py:481
  3.3 0.0 copy-start
  3.3 0.0 copy-start.1
  3.3 0.0 copy-start.3
  3.3 0.1 gather_fields.1
  3.4 0.1 collective-permute-start
  3.5 0.6 %collective-permute-start.4 = (f32[1,16,2048]{2,1,0:T(8,128)S(1)}, f32[1,16,2048]{2,1,0:T(8,128)S(1)}, u32[]{:S(2)}, u32[]{:S(2)}) collective-permute-start(f32[1,16,2048]{2,1,0:T(8,128)S(1)} %copy-done.8), channel_id=1, source_target_pairs={{0,16},{4,20},{8,24},{12,28},{16,0},{20,4},{24,8},{28,12},{1,17},{... | collective-permute-start | bytes 393224 | tf_op jit(solution)/shard_map/ppermute | solution.py:428
  4.0 0.7 %collective-permute-done.near = f32[8,2304]{1,0:T(8,128)S(1)} collective-permute-done((f32[8,2304]{1,0:T(8,128)S(1)}, f32[8,2304]{1,0:T(8,128)S(1)}, u32[]{:S(2)}, u32[]{:S(2)}) %collective-permute-start) | collective-permute-done | bytes 73760 | tf_op jit(solution)/shard_map/ppermute | solution.py:423
  4.7 0.0 copy-start.5
  4.8 0.0 copy-start.6
  4.8 0.0 copy-start.7
  4.8 0.7 %own_spectra.2 = (f32[272,256]{1,0:T(8,128)S(1)}, f32[544,256]{1,0:T(8,128)S(1)}, f32[8,2304]{1,0:T(8,128)S(1)}, f32[1,16,2048]{2,1,0:T(8,128)S(1)}) custom-call(f32[8,2304]{1,0:T(8,128)S(1)} %collective-permute-done.near, f32[1,16,2048]{2,1,0:T(8,128)S(1)} %get-tuple-element.26.height, f32[2,16,2048]{2,1,0:T(8,128)S(1)} %get-tuple-element.27.wind, ...), custom_call_target="tpu_custom_call" | custom-call | tf_op jit(solution)/shard_map/own_spectra/pallas_call | solution.py:448
  5.5 0.5 %collective-permute-start.2 = (f32[1,16,2048]{2,1,0:T(8,128)S(1)}, f32[1,16,2048]{2,1,0:T(8,128)S(1)}, u32[]{:S(2)}, u32[]{:S(2)}) collective-permute-start(f32[1,16,2048]{2,1,0:T(8,128)S(1)} %get-tuple-element.30), channel_id=1, source_target_pairs={{0,1},{2,3},{1,0},{3,2},{4,5},{6,7},{5,4},{7,6},{8,9},{10,11},{9,8... | collective-permute-start | bytes 393224 | tf_op jit(solution)/shard_map/ppermute | solution.py:423
  6.0 4.6 %collective-permute-start.3 = (f32[1,16,2048]{2,1,0:T(8,128)S(1)}, f32[1,16,2048]{2,1,0:T(8,128)S(1)}, u32[]{:S(2)}, u32[]{:S(2)}) collective-permute-start(f32[1,16,2048]{2,1,0:T(8,128)S(1)} %get-tuple-element.30), channel_id=1, source_target_pairs={{1,2},{2,1},{5,6},{6,5},{9,10},{10,9},{13,14},{14,13},{17,18},{18,... | collective-permute-start | bytes 393224 | tf_op jit(solution)/shard_map/ppermute | solution.py:423
  10.6 0.1 collective-permute-start.1
  10.7 1.6 %antipode_transform.4 = (f32[2,16,2048]{2,1,0:T(8,128)S(1)}, f32[2,16,2048]{2,1,0:T(8,128)S(1)}) custom-call(f32[2,16,2048]{2,1,0:T(8,128)S(1)} %collective-permute-done.5.far, f32[544,256]{1,0:T(8,128)S(1)} %get-tuple-element.32.spectrum, f32[34,128]{1,0:T(8,128)S(1)} %copy-done.3, f32[68,128]{1,0:T(8,128)S(1)} %copy-done.7, f32[51,256]{1,0:T(8,128)S(1)} %copy-done.2, ...), custom_call_target="tpu_custom_call" | custom-call | flops 10000000000 | bytes 33333332 | tf_op jit(solution)/shard_map/antipode_transform/pallas_call | solution.py:448
  12.3 0.9 %antipode_transform.5 = (f32[1,16,2048]{2,1,0:T(8,128)S(1)}, f32[1,16,2048]{2,1,0:T(8,128)S(1)}) custom-call(f32[1,16,2048]{2,1,0:T(8,128)S(1)} %collective-permute-done.4.far, f32[272,256]{1,0:T(8,128)S(1)} %get-tuple-element.31.spectrum, f32[34,128]{1,0:T(8,128)S(1)} %copy-done.3, f32[68,128]{1,0:T(8,128)S(1)} %copy-done.7, f32[51,256]{1,0:T(8,128)S(1)} %copy-done.2, ...), custom_call_target="tpu_custom_call" | custom-call | flops 10000000000 | bytes 33333332 | tf_op jit(solution)/shard_map/antipode_transform/pallas_call | solution.py:448
  13.2 1.9 %collective-permute-done.1.far = f32[8,2304]{1,0:T(8,128)S(1)} collective-permute-done((f32[8,2304]{1,0:T(8,128)S(1)}, f32[8,2304]{1,0:T(8,128)S(1)}, u32[]{:S(2)}, u32[]{:S(2)}) %collective-permute-start.1) | collective-permute-done | bytes 73760 | tf_op jit(solution)/shard_map/ppermute | solution.py:423
  15.2 0.6 %update_fields.2 = (f32[1,16,2048]{2,1,0:T(8,128)S(1)}, f32[2,16,2048]{2,1,0:T(8,128)S(1)}, f32[8,2304]{1,0:T(8,128)S(1)}) custom-call(f32[1,16,2048]{2,1,0:T(8,128)S(1)} %get-tuple-element.26.height, f32[2,16,2048]{2,1,0:T(8,128)S(1)} %get-tuple-element.27.wind, f32[8,2304]{1,0:T(8,128)S(1)} %collective-permute-done.near, ...), custom_call_target="tpu_custom_call" | custom-call | tf_op jit(solution)/shard_map/update_fields/pallas_call | solution.py:448
  15.8 0.7 %collective-permute-start.11 = (f32[2,16,2048]{2,1,0:T(8,128)S(1)}, f32[2,16,2048]{2,1,0:T(8,128)S(1)}, u32[]{:S(2)}, u32[]{:S(2)}) collective-permute-start(f32[2,16,2048]{2,1,0:T(8,128)S(1)} %get-tuple-element.38.wind), channel_id=1, source_target_pairs={{0,16},{4,20},{8,24},{12,28},{16,0},{20,4},{24,8},{28,12},{1,17},{... | collective-permute-start | bytes 786440 | tf_op jit(solution)/shard_map/ppermute | solution.py:428
  16.5 0.4 %collective-permute-start.6 = (f32[8,2304]{1,0:T(8,128)S(1)}, f32[8,2304]{1,0:T(8,128)S(1)}, u32[]{:S(2)}, u32[]{:S(2)}) collective-permute-start(f32[8,2304]{1,0:T(8,128)S(1)} %get-tuple-element.39), channel_id=1, source_target_pairs={{0,4},{8,12},{16,20},{24,28},{4,0},{12,8},{20,16},{28,24},{1,5},{9... | collective-permute-start | bytes 221192 | tf_op jit(solution)/shard_map/ppermute | solution.py:423
  16.9 0.9 %collective-permute-start.10 = (f32[1,16,2048]{2,1,0:T(8,128)S(1)}, f32[1,16,2048]{2,1,0:T(8,128)S(1)}, u32[]{:S(2)}, u32[]{:S(2)}) collective-permute-start(f32[1,16,2048]{2,1,0:T(8,128)S(1)} %get-tuple-element.37.height), channel_id=1, source_target_pairs={{0,16},{4,20},{8,24},{12,28},{16,0},{20,4},{24,8},{28,12},{1,17},{... | collective-permute-start | bytes 393224 | tf_op jit(solution)/shard_map/ppermute | solution.py:428
  17.9 0.7 %own_spectra.3 = (f32[272,256]{1,0:T(8,128)S(1)}, f32[544,256]{1,0:T(8,128)S(1)}, f32[8,2304]{1,0:T(8,128)S(1)}, f32[1,16,2048]{2,1,0:T(8,128)S(1)}) custom-call(f32[8,2304]{1,0:T(8,128)S(1)} %collective-permute-done.6.near, f32[1,16,2048]{2,1,0:T(8,128)S(1)} %get-tuple-element.37.height, f32[2,16,2048]{2,1,0:T(8,128)S(1)} %get-tuple-element.38.wind, ...), custom_call_target="tpu_custom_call" | custom-call | tf_op jit(solution)/shard_map/own_spectra/pallas_call | solution.py:448
  18.6 0.1 collective-permute-start.8
  18.6 4.1 %collective-permute-start.9 = (f32[1,16,2048]{2,1,0:T(8,128)S(1)}, f32[1,16,2048]{2,1,0:T(8,128)S(1)}, u32[]{:S(2)}, u32[]{:S(2)}) collective-permute-start(f32[1,16,2048]{2,1,0:T(8,128)S(1)} %get-tuple-element.41), channel_id=1, source_target_pairs={{1,2},{2,1},{5,6},{6,5},{9,10},{10,9},{13,14},{14,13},{17,18},{18,... | collective-permute-start | bytes 393224 | tf_op jit(solution)/shard_map/ppermute | solution.py:423
  22.8 0.1 collective-permute-start.7
  22.9 2.1 %collective-permute-done.11.far = f32[2,16,2048]{2,1,0:T(8,128)S(1)} collective-permute-done((f32[2,16,2048]{2,1,0:T(8,128)S(1)}, f32[2,16,2048]{2,1,0:T(8,128)S(1)}, u32[]{:S(2)}, u32[]{:S(2)}) %collective-permute-start.11) | collective-permute-done | bytes 262176 | tf_op jit(solution)/shard_map/ppermute | solution.py:428
  25.0 1.6 %antipode_transform.6 = (f32[2,16,2048]{2,1,0:T(8,128)S(1)}, f32[2,16,2048]{2,1,0:T(8,128)S(1)}) custom-call(f32[2,16,2048]{2,1,0:T(8,128)S(1)} %collective-permute-done.11.far, f32[544,256]{1,0:T(8,128)S(1)} %get-tuple-element.43.spectrum, f32[34,128]{1,0:T(8,128)S(1)} %copy-done.3, f32[68,128]{1,0:T(8,128)S(1)} %copy-done.7, f32[51,256]{1,0:T(8,128)S(1)} %copy-done.2, ...), custom_call_target="tpu_custom_call" | custom-call | flops 10000000000 | bytes 33333332 | tf_op jit(solution)/shard_map/antipode_transform/pallas_call | solution.py:448
  26.5 1.3 %collective-permute-done.10.far = f32[1,16,2048]{2,1,0:T(8,128)S(1)} collective-permute-done((f32[1,16,2048]{2,1,0:T(8,128)S(1)}, f32[1,16,2048]{2,1,0:T(8,128)S(1)}, u32[]{:S(2)}, u32[]{:S(2)}) %collective-permute-start.10) | collective-permute-done | bytes 131104 | tf_op jit(solution)/shard_map/ppermute | solution.py:428
  27.8 0.9 %antipode_transform.7 = (f32[1,16,2048]{2,1,0:T(8,128)S(1)}, f32[1,16,2048]{2,1,0:T(8,128)S(1)}) custom-call(f32[1,16,2048]{2,1,0:T(8,128)S(1)} %collective-permute-done.10.far, f32[272,256]{1,0:T(8,128)S(1)} %get-tuple-element.42.spectrum, f32[34,128]{1,0:T(8,128)S(1)} %copy-done.3, f32[68,128]{1,0:T(8,128)S(1)} %copy-done.7, f32[51,256]{1,0:T(8,128)S(1)} %copy-done.2, ...), custom_call_target="tpu_custom_call" | custom-call | flops 10000000000 | bytes 33333332 | tf_op jit(solution)/shard_map/antipode_transform/pallas_call | solution.py:448
  28.8 1.3 %update_fields.3 = (f32[1,16,2048]{2,1,0:T(8,128)}, f32[2,16,2048]{2,1,0:T(8,128)}) custom-call(f32[1,16,2048]{2,1,0:T(8,128)S(1)} %get-tuple-element.37.height, f32[2,16,2048]{2,1,0:T(8,128)S(1)} %get-tuple-element.38.wind, f32[8,2304]{1,0:T(8,128)S(1)} %collective-permute-done.6.near, f32[8,2304]{1,0:T(8,128)S(1)} %collective-permute-done.7.far, ...), custom_call_target="tpu_custom_call" | custom-call | tf_op jit(solution)/shard_map/update_fields/pallas_call | solution.py:448
  (20 shorter events, 0.1 us)
Async XLA Ops:
  0.6 10.1 %collective-permute-start.5 = (f32[2,16,2048]{2,1,0:T(8,128)}, f32[2,16,2048]{2,1,0:T(8,128)S(1)}, u32[]{:S(2)}, u32[]{:S(2)}) collective-permute-start(f32[2,16,2048]{2,1,0:T(8,128)} %bitcast.4), channel_id=1, source_target_pairs={{0,16},{4,20},{8,24},{12,28},{16,0},{20,4},{24,8},{28,12},{1,17},{... | collective-permute-start | bytes 786440 | tf_op jit(solution)/shard_map/ppermute | solution.py:428
  2.2 1.3 %copy-start.8 = (f32[1,16,2048]{2,1,0:T(8,128)S(1)}, f32[1,16,2048]{2,1,0:T(8,128)}, u32[]{:S(2)}) copy-start(f32[1,16,2048]{2,1,0:T(8,128)} %param.10) | copy-start | bytes 393220
  3.3 1.5 %copy-start = (bf16[256,256]{1,0:T(8,128)(2,1)S(1)}, bf16[256,256]{1,0:T(8,128)(2,1)}, u32[]{:S(2)}) copy-start(bf16[256,256]{1,0:T(8,128)(2,1)} %constant.16.clone.high.forward_high) | copy-start | bytes 393220
  3.3 1.4 %copy-start.1 = (bf16[256,256]{1,0:T(8,128)(2,1)S(1)}, bf16[256,256]{1,0:T(8,128)(2,1)}, u32[]{:S(2)}) copy-start(bf16[256,256]{1,0:T(8,128)(2,1)} %constant.17.clone.low.forward_low) | copy-start | bytes 393220
  3.3 1.4 %copy-start.2 = (f32[51,256]{1,0:T(8,128)S(1)}, f32[51,256]{1,0:T(8,128)}, u32[]{:S(2)}) copy-start(f32[51,256]{1,0:T(8,128)} %constant.22.clone.masks) | copy-start | bytes 156676
  3.3 1.4 %copy-start.3 = (f32[34,128]{1,0:T(8,128)S(1)}, f32[34,128]{1,0:T(8,128)}, u32[]{:S(2)}) copy-start(f32[34,128]{1,0:T(8,128)} %constant.20.clone.twist) | copy-start | bytes 52228
  3.4 1.3 %collective-permute-start = (f32[8,2304]{1,0:T(8,128)S(1)}, f32[8,2304]{1,0:T(8,128)S(1)}, u32[]{:S(2)}, u32[]{:S(2)}) collective-permute-start(f32[8,2304]{1,0:T(8,128)S(1)} %get-tuple-element.28), channel_id=1, source_target_pairs={{0,4},{8,12},{16,20},{24,28},{4,0},{12,8},{20,16},{28,24},{1,5},{9... | collective-permute-start | bytes 221192 | tf_op jit(solution)/shard_map/ppermute | solution.py:423
  3.5 8.8 %collective-permute-start.4 = (f32[1,16,2048]{2,1,0:T(8,128)S(1)}, f32[1,16,2048]{2,1,0:T(8,128)S(1)}, u32[]{:S(2)}, u32[]{:S(2)}) collective-permute-start(f32[1,16,2048]{2,1,0:T(8,128)S(1)} %copy-done.8), channel_id=1, source_target_pairs={{0,16},{4,20},{8,24},{12,28},{16,0},{20,4},{24,8},{28,12},{1,17},{... | collective-permute-start | bytes 393224 | tf_op jit(solution)/shard_map/ppermute | solution.py:428
  4.7 6.0 %copy-start.5 = (bf16[256,512]{1,0:T(8,128)(2,1)S(1)}, bf16[256,512]{1,0:T(8,128)(2,1)}, u32[]{:S(2)}) copy-start(bf16[256,512]{1,0:T(8,128)(2,1)} %constant.18.clone.inverse_high) | copy-start | bytes 786436
  4.8 6.0 %copy-start.6 = (bf16[256,512]{1,0:T(8,128)(2,1)S(1)}, bf16[256,512]{1,0:T(8,128)(2,1)}, u32[]{:S(2)}) copy-start(bf16[256,512]{1,0:T(8,128)(2,1)} %constant.19.clone.inverse_low) | copy-start | bytes 786436
  4.8 5.9 %copy-start.7 = (f32[68,128]{1,0:T(8,128)S(1)}, f32[68,128]{1,0:T(8,128)}, u32[]{:S(2)}) copy-start(f32[68,128]{1,0:T(8,128)} %constant.21.clone.back) | copy-start | bytes 104452
  5.5 9.7 %collective-permute-start.2 = (f32[1,16,2048]{2,1,0:T(8,128)S(1)}, f32[1,16,2048]{2,1,0:T(8,128)S(1)}, u32[]{:S(2)}, u32[]{:S(2)}) collective-permute-start(f32[1,16,2048]{2,1,0:T(8,128)S(1)} %get-tuple-element.30), channel_id=1, source_target_pairs={{0,1},{2,3},{1,0},{3,2},{4,5},{6,7},{5,4},{7,6},{8,9},{10,11},{9,8... | collective-permute-start | bytes 393224 | tf_op jit(solution)/shard_map/ppermute | solution.py:423
  6.0 9.2 %collective-permute-start.3 = (f32[1,16,2048]{2,1,0:T(8,128)S(1)}, f32[1,16,2048]{2,1,0:T(8,128)S(1)}, u32[]{:S(2)}, u32[]{:S(2)}) collective-permute-start(f32[1,16,2048]{2,1,0:T(8,128)S(1)} %get-tuple-element.30), channel_id=1, source_target_pairs={{1,2},{2,1},{5,6},{6,5},{9,10},{10,9},{13,14},{14,13},{17,18},{18,... | collective-permute-start | bytes 393224 | tf_op jit(solution)/shard_map/ppermute | solution.py:423
  10.6 4.6 %collective-permute-start.1 = (f32[8,2304]{1,0:T(8,128)S(1)}, f32[8,2304]{1,0:T(8,128)S(1)}, u32[]{:S(2)}, u32[]{:S(2)}) collective-permute-start(f32[8,2304]{1,0:T(8,128)S(1)} %get-tuple-element.29), channel_id=1, source_target_pairs={{4,8},{12,16},{20,24},{28,0},{8,4},{16,12},{24,20},{0,28},{5,9},{1... | collective-permute-start | bytes 221192 | tf_op jit(solution)/shard_map/ppermute | solution.py:423
  12.3 2.9 %copy-start.4 = (f32[2,2048]{1,0:T(2,128)S(1)}, f32[2,2048]{1,0:T(2,128)}, u32[]{:S(2)}) copy-start(f32[2,2048]{1,0:T(2,128)} %constant.23.clone.rows) | copy-start | bytes 49156
  15.8 9.2 %collective-permute-start.11 = (f32[2,16,2048]{2,1,0:T(8,128)S(1)}, f32[2,16,2048]{2,1,0:T(8,128)S(1)}, u32[]{:S(2)}, u32[]{:S(2)}) collective-permute-start(f32[2,16,2048]{2,1,0:T(8,128)S(1)} %get-tuple-element.38.wind), channel_id=1, source_target_pairs={{0,16},{4,20},{8,24},{12,28},{16,0},{20,4},{24,8},{28,12},{1,17},{... | collective-permute-start | bytes 786440 | tf_op jit(solution)/shard_map/ppermute | solution.py:428
  16.5 1.4 %collective-permute-start.6 = (f32[8,2304]{1,0:T(8,128)S(1)}, f32[8,2304]{1,0:T(8,128)S(1)}, u32[]{:S(2)}, u32[]{:S(2)}) collective-permute-start(f32[8,2304]{1,0:T(8,128)S(1)} %get-tuple-element.39), channel_id=1, source_target_pairs={{0,4},{8,12},{16,20},{24,28},{4,0},{12,8},{20,16},{28,24},{1,5},{9... | collective-permute-start | bytes 221192 | tf_op jit(solution)/shard_map/ppermute | solution.py:423
  16.9 10.9 %collective-permute-start.10 = (f32[1,16,2048]{2,1,0:T(8,128)S(1)}, f32[1,16,2048]{2,1,0:T(8,128)S(1)}, u32[]{:S(2)}, u32[]{:S(2)}) collective-permute-start(f32[1,16,2048]{2,1,0:T(8,128)S(1)} %get-tuple-element.37.height), channel_id=1, source_target_pairs={{0,16},{4,20},{8,24},{12,28},{16,0},{20,4},{24,8},{28,12},{1,17},{... | collective-permute-start | bytes 393224 | tf_op jit(solution)/shard_map/ppermute | solution.py:428
  18.6 10.2 %collective-permute-start.8 = (f32[1,16,2048]{2,1,0:T(8,128)S(1)}, f32[1,16,2048]{2,1,0:T(8,128)S(1)}, u32[]{:S(2)}, u32[]{:S(2)}) collective-permute-start(f32[1,16,2048]{2,1,0:T(8,128)S(1)} %get-tuple-element.41), channel_id=1, source_target_pairs={{0,1},{2,3},{1,0},{3,2},{4,5},{6,7},{5,4},{7,6},{8,9},{10,11},{9,8... | collective-permute-start | bytes 393224 | tf_op jit(solution)/shard_map/ppermute | solution.py:423
  18.6 10.1 %collective-permute-start.9 = (f32[1,16,2048]{2,1,0:T(8,128)S(1)}, f32[1,16,2048]{2,1,0:T(8,128)S(1)}, u32[]{:S(2)}, u32[]{:S(2)}) collective-permute-start(f32[1,16,2048]{2,1,0:T(8,128)S(1)} %get-tuple-element.41), channel_id=1, source_target_pairs={{1,2},{2,1},{5,6},{6,5},{9,10},{10,9},{13,14},{14,13},{17,18},{18,... | collective-permute-start | bytes 393224 | tf_op jit(solution)/shard_map/ppermute | solution.py:423
  22.8 6.0 %collective-permute-start.7 = (f32[8,2304]{1,0:T(8,128)S(1)}, f32[8,2304]{1,0:T(8,128)S(1)}, u32[]{:S(2)}, u32[]{:S(2)}) collective-permute-start(f32[8,2304]{1,0:T(8,128)S(1)} %get-tuple-element.40), channel_id=1, source_target_pairs={{4,8},{12,16},{20,24},{28,0},{8,4},{16,12},{24,20},{0,28},{5,9},{1... | collective-permute-start | bytes 221192 | tf_op jit(solution)/shard_map/ppermute | solution.py:423

commit v3 on v2

--- a/solution.py
+++ b/solution.py
@@ -18,7 +18,8 @@
 
 RADIX = 128
 ROWS = 8
-TRANSFORM_COST = 10_000_000_000
+FIRST_COST = 2000000000
+SECOND_COST = 2000000000
 PIECES = 4
 HALO = 3
 
@@ -183,8 +184,9 @@
 
 def triple_product(value, high_table, low_table):
     high, low = split(value)
-    dot = functools.partial(jnp.dot, preferred_element_type=jnp.float32)
-    return dot(high, high_table) + dot(low, high_table) + dot(high, low_table)
+    left = jnp.concatenate([high, low, high], 1)
+    right = jnp.concatenate([high_table, high_table, low_table], 0)
+    return jnp.dot(left, right, preferred_element_type=jnp.float32)
 
 
 def forward_stage(slabs_of, groups, twist, turned, blocks):
@@ -201,14 +203,8 @@
                 turned[at, tile(1)] = real * sin + imag * cos
 
 
-def reader(fields, tiles):
-    per_field = fields.shape[1] // ROWS
-
-    def slabs_of(group):
-        field, part = divmod(group, per_field)
-        return [fields[field, part * ROWS : part * ROWS + ROWS, tile(m)] for m in range(tiles)]
-
-    return slabs_of
+def row_groups(lon_count):
+    return [slice(i, i + ROWS) for i in range(0, lon_count, ROWS)]
 
 
 def pack_rows(pack, lat_count, field, index, rows):
@@ -228,80 +224,80 @@
     return jnp.concatenate([pack[2 * HALO : ROWS, tile(index)], last], 0)
 
 
-def field_of(height, wind, field, index):
-    return height[0, :, tile(index)] if field == 0 else wind[field - 1, :, tile(index)]
+def field_at(east, rest, field, *at):
+    return east[(0, *at)] if field == 0 else rest[(field - 1, *at)]
 
 
 def odd_device():
     return lax.rem(lax.axis_index("lon"), 2) == 1
 
 
-def pack_edge(height, wind, pack, first):
-    lat_count = height.shape[-1]
-    for field in range(3):
-        for index in range(lat_count // RADIX):
-            rows = field_of(height, wind, field, index)
-            chosen = jnp.where(first, rows[:HALO], rows[rows.shape[0] - HALO :])
-            pack_rows(pack, lat_count, field, index, chosen)
-
-
-def gather_kernel(fields, height, wind, near_pack):
-    height[...] = fields[:1]
-    wind[...] = fields[1:]
-    pack_edge(height, wind, near_pack, odd_device())
-
-
-def own_kernel(blocks, near, height, wind, twist, masks, high, low, *rest):
-    spectra, (far_pack, height_copy), turned = rest[:2], rest[2:4], rest[4:]
-    pack_edge(height, wind, far_pack, jnp.logical_not(odd_device()))
-    height_copy[...] = height[...]
+def pack_tile(field, index, rows, near_pack, far_pack, lat_count):
+    first, last = rows[:HALO], rows[rows.shape[0] - HALO :]
+    odd = odd_device()
+    pack_rows(near_pack, lat_count, field, index, jnp.where(odd, first, last))
+    pack_rows(far_pack, lat_count, field, index, jnp.where(odd, last, first))
+
+
+def gather_kernel(fields, east, rest, height, near_pack, far_pack):
+    lat_count = fields.shape[-1]
+    for index in range(lat_count // RADIX):
+        at = tile(index)
+        thickness, eastward, northward = [fields[i, :, at] for i in range(3)]
+        east[0, :, at] = eastward
+        rest[0, :, at] = northward
+        rest[1, :, at] = thickness
+        height[0, :, at] = thickness
+        for field, rows in enumerate((eastward, northward, thickness)):
+            pack_tile(field, index, rows, near_pack, far_pack, lat_count)
+
+
+def own_kernel(blocks, split_at, near, east, rest, twist, masks, high, low, *refs):
+    first, second, turned = refs
     kept = blocks // 2 + 1
-    for fields, spectrum, work in zip((height, wind), spectra, turned):
-        span = fields.shape[0] * fields.shape[1]
-        forward_stage(reader(fields, blocks // 2), span // ROWS, twist, work, blocks)
-        result = triple_product(work[...], high[...], low[...])
-        for k in range(kept):
-            at = k * span
-            spectrum[at : at + span, :] = result[at : at + span, :] * masks[3 * k : 3 * k + 1, :]
-
-
-def far_kernel(
-    blocks,
-    parity,
-    far,
-    spectrum,
-    twist,
-    back,
-    masks,
-    forward_high,
-    forward_low,
-    inverse_high,
-    inverse_low,
-    *rest,
-):
-    smooth, slope, turned, weighted, spread = rest[-5:]
+    lon_count = east.shape[1]
+    groups = [(field, at) for field in range(3) for at in row_groups(lon_count)]
+
+    def slabs_of(group):
+        field, at = groups[group]
+        return [field_at(east, rest, field, at, tile(m)) for m in range(blocks // 2)]
+
+    forward_stage(slabs_of, len(groups), twist, turned, blocks)
+    result = triple_product(turned[...], high[...], low[...])
+    cut, span = split_at * lon_count, 3 * lon_count
+    for k in range(kept):
+        value = result[k * span : k * span + span, :] * masks[3 * k : 3 * k + 1, :]
+        first[k * cut : k * cut + cut, :] = value[:cut]
+        second[k * (span - cut) : (k + 1) * (span - cut), :] = value[cut:]
+
+
+def transform(blocks, parities, far, spectrum, tables, smooth, slope, work):
+    twist, back, masks, forward_high, forward_low, inverse_high, inverse_low = tables
+    turned, weighted, spread = work
     kept = blocks // 2 + 1
-    tiles = blocks // 2
     count, lon_count = far.shape[:2]
-    per_field = lon_count // ROWS
-    groups = count * per_field
     length = blocks * RADIX
-    forward_stage(reader(far, tiles), groups, twist, turned, blocks)
+    groups = [(field, at) for field in range(count) for at in row_groups(lon_count)]
+
+    def slabs_of(group):
+        field, at = groups[group]
+        return [far[field, at, tile(m)] for m in range(blocks // 2)]
+
+    forward_stage(slabs_of, len(groups), twist, turned, blocks)
     result = triple_product(turned[...], forward_high[...], forward_low[...])
-    span = groups * ROWS
     for k in range(kept):
-        at = k * span
-        row = 3 * k + (1 if parity > 0 else 2)
-        weighted[at : at + span, :] = (
-            spectrum[at : at + span, :] + result[at : at + span, :] * masks[row : row + 1, :]
-        )
+        for field, parity in enumerate(parities):
+            at = (k * count + field) * lon_count
+            row = 3 * k + (1 if parity > 0 else 2)
+            weighted[at : at + lon_count, :] = (
+                spectrum[at : at + lon_count, :]
+                + result[at : at + lon_count, :] * masks[row : row + 1, :]
+            )
     spread[...] = triple_product(weighted[...], inverse_high[...], inverse_low[...])
-    for group in range(groups):
-        field, part = divmod(group, per_field)
-        out = slice(part * ROWS, part * ROWS + ROWS)
+    for group, (field, out) in enumerate(groups):
         smooth_terms, slope_terms = [], []
         for k in range(kept):
-            at = pl.ds((k * groups + group) * ROWS, ROWS)
+            at = pl.ds((k * len(groups) + group) * ROWS, ROWS)
             real, imag, slope_real, slope_imag = [spread[at, tile(i)] for i in range(4)]
             cos, sin, slope_cos, slope_sin = [back[4 * k + i : 4 * k + i + 1, :] for i in range(4)]
             turn_real = real * cos - imag * sin
@@ -320,29 +316,24 @@
             slope[field, out, tile(m)] = value
 
 
-def update_kernel(
-    final,
-    height,
-    wind,
-    near,
-    far,
-    first_level,
-    second_level,
-    height_smooth,
-    height_slope,
-    wind_smooth,
-    wind_slope,
-    rows,
-    *outs,
-):
-    lon_count, lat_count = height.shape[1:]
-    tiles = lat_count // RADIX
+def first_kernel(blocks, with_north, far_rows, spectrum, east, rest, near, far, rows, *refs):
+    tables, refs = refs[:7], refs[7:]
+    lon_count, lat_count = east.shape[1:]
     odd = odd_device()
-    if final:
-        height_out, wind_out, staged, sems = outs
-    copies = []
-    for index in range(tiles):
-        here = [field_of(height, wind, field, index) for field in range(3)]
+    east_next, zonal_terms = refs[:2]
+    if with_north:
+        north_terms, refs = refs[2], refs[3:]
+    else:
+        refs = refs[2:]
+    smooth, slope, *work = refs
+    count = far_rows.shape[0]
+    transform(blocks, (-1,) * count, far_rows, spectrum, tables, smooth, slope, work)
+    if with_north:
+        north_terms[0] = smooth[1]
+        north_terms[1] = slope[1]
+    for index in range(lat_count // RADIX):
+        here = [field_at(east, rest, field, slice(None), tile(index)) for field in range(3)]
+        secant, turning = rows[0:1, tile(index)], rows[1:2, tile(index)]
         zonal = []
         for field in range(3):
             close = halo_rows(near, lat_count, field, index)
@@ -351,55 +342,82 @@
                 [jnp.where(odd, close, away), here[field], jnp.where(odd, away, close)], 0
             )
             at = [line[i : i + lon_count] for i in range(2 * HALO + 1)]
-            zonal.append(
+            difference = (
                 (45.0 / 60.0) * (at[4] - at[2])
                 - (9.0 / 60.0) * (at[5] - at[1])
                 + (1.0 / 60.0) * (at[6] - at[0])
             )
-        thick, east, north = here
-        secant, turning = rows[0:1, tile(index)], rows[1:2, tile(index)]
-        vertical = first_level[0, :, tile(index)] + second_level[0, :, tile(index)] - 2.0 * thick
-        zonal = [secant * value for value in zonal]
-        slopes = [
-            height_slope[0, :, tile(index)],
-            wind_slope[0, :, tile(index)],
-            wind_slope[1, :, tile(index)],
-        ]
-        smooths = [
-            height_smooth[0, :, tile(index)],
-            wind_smooth[0, :, tile(index)],
-            wind_smooth[1, :, tile(index)],
-        ]
-        advect = [east * zonal[field] + north * slopes[field] for field in range(3)]
-        tendency = [
-            mixing * vertical - advect[0] - thick * (zonal[1] + slopes[2]),
-            turning * north - advect[1] - zonal[0],
-            -advect[2] - slopes[0] - turning * east,
-        ]
-        values = [smooths[field] + courant * tendency[field] for field in range(3)]
+            zonal.append(secant * difference)
+        eastward, northward, thick = here
+        tendency = (
+            turning * northward
+            - eastward * zonal[0]
+            - northward * slope[0, :, tile(index)]
+            - zonal[2]
+        )
+        east_next[0, :, tile(index)] = smooth[0, :, tile(index)] + courant * tendency
+        zonal_terms[0, :, tile(index)] = -eastward * zonal[1] - turning * eastward
+        zonal_terms[1, :, tile(index)] = -eastward * zonal[2] - thick * zonal[0]
+
+
+def second_kernel(
+    blocks, with_north, final, far_rows, spectrum, rest, zonal_terms, *refs
+):
+    tables, refs = refs[:7], refs[7:]
+    if with_north:
+        north_terms, refs = refs[0], refs[1:]
+    lat_count = rest.shape[-1]
+    if final:
+        rest_next, *refs = refs
+    else:
+        (east_next, levels, others, rest_next, height_next, near_pack, far_pack, *refs) = refs
+    smooth, slope, *work = refs
+    parities = (1,) if with_north else (-1, 1)
+    transform(blocks, parities, far_rows, spectrum, tables, smooth, slope, work)
+    for index in range(lat_count // RADIX):
+        at = tile(index)
+        northward, thick = rest[0, :, at], rest[1, :, at]
+        last = len(parities) - 1
+        thick_smooth, thick_slope = smooth[last, :, at], slope[last, :, at]
+        north_smooth = north_terms[0, :, at] if with_north else smooth[0, :, at]
+        north_slope = north_terms[1, :, at] if with_north else slope[0, :, at]
+        north_tendency = zonal_terms[0, :, at] - northward * north_slope - thick_slope
+        thick_tendency = zonal_terms[1, :, at] - northward * thick_slope - thick * north_slope
         if final:
-            for field in range(3):
-                staged[field, :, tile(index)] = values[field]
-            if (index + 1) % (tiles // PIECES) == 0:
-                piece = (index + 1) // (tiles // PIECES) - 1
-                at = pl.ds(piece * (lat_count // PIECES), lat_count // PIECES)
-                for field in range(3):
-                    target = (
-                        height_out.at[0, :, at] if field == 0 else wind_out.at[field - 1, :, at]
-                    )
-                    copy = pltpu.make_async_copy(
-                        staged.at[field, :, at], target, sems.at[piece * 3 + field]
-                    )
-                    copy.start()
-                    copies.append(copy)
+            thick_tendency -= 2.0 * mixing * thick
         else:
-            height_next, wind_next, near_pack = outs
-            height_next[0, :, tile(index)] = values[0]
-            for field in range(1, 3):
-                wind_next[field - 1, :, tile(index)] = values[field]
-            for field in range(3):
-                first, last = values[field][:HALO], values[field][lon_count - HALO :]
-                pack_rows(near_pack, lat_count, field, index, jnp.where(odd, first, last))
+            thick_tendency += mixing * (levels[0, :, at] + others[0, :, at] - 2.0 * thick)
+        values = (
+            north_smooth + courant * north_tendency,
+            thick_smooth + courant * thick_tendency,
+        )
+        for field in range(2):
+            rest_next[field, :, at] = values[field]
+        if not final:
+            height_next[0, :, at] = values[1]
+            for field, moved in enumerate((east_next[0, :, at], *values)):
+                pack_tile(field, index, moved, near_pack, far_pack, lat_count)
+
+
+def last_kernel(east, rest, levels, others, height_out, wind_out, height, sems):
+    tiles = height.shape[-1] // RADIX
+    copies = [
+        pltpu.make_async_copy(east.at[0], wind_out.at[0], sems.at[0]),
+        pltpu.make_async_copy(rest.at[0], wind_out.at[1], sems.at[1]),
+    ]
+    for copy in copies:
+        copy.start()
+    for piece in range(PIECES):
+        for index in range(piece * tiles // PIECES, (piece + 1) * tiles // PIECES):
+            at = tile(index)
+            height[:, at] = rest[1, :, at] + (courant * mixing) * (
+                levels[0, :, at] + others[0, :, at]
+            )
+        span = pl.ds(piece * tiles // PIECES * RADIX, tiles // PIECES * RADIX)
+        copies.append(
+            pltpu.make_async_copy(height.at[:, span], height_out.at[0, :, span], sems.at[2 + piece])
+        )
+        copies[-1].start()
     for copy in copies:
         copy.wait()
 
@@ -437,12 +455,20 @@
     forward_tables = split_table(forward)
     inverse_tables = split_table(inverse)
     twist, back, masks, rows = [jnp.asarray(a) for a in (twist, back, masks, rows)]
+    tables = (twist, back, masks, *forward_tables, *inverse_tables)
     f32 = jnp.float32
     array = lambda *shape: jax.ShapeDtypeStruct(shape, f32)
     scratch = lambda *shape: pltpu.VMEM(shape, f32)
-    height_shape, wind_shape = array(1, lon_count, lat_count), array(2, lon_count, lat_count)
+    one, two = array(1, lon_count, lat_count), array(2, lon_count, lat_count)
     pack_shape = array(ROWS, lat_count + lat_count // ROWS)
     spectral = lambda count, width: (count * kept * lon_count, width * RADIX)
+    working = lambda count: [
+        scratch(count, lon_count, lat_count),
+        scratch(count, lon_count, lat_count),
+        scratch(*spectral(count, 2)),
+        scratch(*spectral(count, 2)),
+        scratch(*spectral(count, 4)),
+    ]
 
     def call(kernel, name, outs, scratches, *args, in_specs=None, out_specs=None, cost=None):
         return pl.pallas_call(
@@ -457,67 +483,78 @@
             name=name,
         )(*args)
 
-    def transform(count, parity, far, spectrum, *after):
-        return call(
-            functools.partial(far_kernel, blocks, parity),
-            "antipode_transform",
-            [array(count, lon_count, lat_count)] * 2,
-            [scratch(*spectral(count, 2))] * 2 + [scratch(*spectral(count, 4))],
-            far,
-            spectrum,
-            twist,
-            back,
-            masks,
-            *forward_tables,
-            *inverse_tables,
-            *after,
-            in_specs=vmem(9) + anywhere(len(after)),
-            cost=TRANSFORM_COST,
-        )
-
-    far_wind = from_antipode(wind_field.reshape(wind_shape.shape))
-    far_height = from_antipode(thickness)
-    moving = [height_shape, wind_shape, pack_shape]
-    fields = jnp.concatenate([thickness, wind_field.reshape(wind_shape.shape)], 0)
-    height, wind, near_pack = call(gather_kernel, "gather_fields", moving, [], fields)
+    winds = wind_field.reshape(2, lon_count, lat_count)
+    far_first, far_second = from_antipode(winds), from_antipode(thickness)
+    fields = jnp.concatenate([thickness, winds], 0)
+    east, rest, height, near_pack, far_pack = call(
+        gather_kernel, "gather_fields", [one, two, one, pack_shape, pack_shape], [], fields
+    )
     for step in range(STEPS):
+        final = step == STEPS - 1
+        with_north = step == 0
+        counts = (2, 1) if with_north else (1, 2)
         near = exchange(near_pack, "lon", 0)
-        height_spectrum, wind_spectrum, far_pack, height_copy = call(
-            functools.partial(own_kernel, blocks),
+        levels = [exchange(height, "lev", first) for first in (0, 1)]
+        far = exchange(far_pack, "lon", 1)
+        spectra = call(
+            functools.partial(own_kernel, blocks, counts[0]),
             "own_spectra",
-            [array(*spectral(1, 2)), array(*spectral(2, 2)), pack_shape, height_shape],
-            [scratch(*spectral(1, 2)), scratch(*spectral(2, 2))],
+            [array(*spectral(count, 2)) for count in counts],
+            [scratch(*spectral(3, 2))],
             near,
-            height,
-            wind,
+            east,
+            rest,
             twist,
             masks,
             *forward_tables,
             in_specs=anywhere(1) + vmem(6),
         )
-        levels = [exchange(height_copy, "lev", first) for first in (0, 1)]
-        far = exchange(far_pack, "lon", 1)
-        wind_terms = transform(2, -1, far_wind, wind_spectrum)
-        height_terms = transform(1, 1, far_height, height_spectrum, wind_terms[0])
-        args = (height, wind, near, far, *levels, *height_terms, *wind_terms, rows)
-        if step == STEPS - 1:
-            height, wind = call(
-                functools.partial(update_kernel, True),
-                "update_fields",
-                [height_shape, wind_shape],
-                [scratch(3, lon_count, lat_count), pltpu.SemaphoreType.DMA((3 * PIECES,))],
-                *args,
+        east_next, zonal_terms, *north_terms = call(
+            functools.partial(first_kernel, blocks, with_north),
+            "eastward_wind",
+            [one, two] + [two] * with_north,
+            working(counts[0]),
+            far_first,
+            spectra[0],
+            east,
+            rest,
+            near,
+            far,
+            rows,
+            *tables,
+            cost=FIRST_COST,
+        )
+        if not final:
+            far_first = from_antipode(east_next)
+        args = (far_second, spectra[1], rest, zonal_terms, *tables, *north_terms)
+        kernel = functools.partial(second_kernel, blocks, with_north, final)
+        if final:
+            (rest_next,) = call(
+                kernel, "north_and_height", [two], working(counts[1]), *args, cost=SECOND_COST
+            )
+            height, winds = call(
+                last_kernel,
+                "level_term",
+                [one, two],
+                [scratch(lon_count, lat_count), pltpu.SemaphoreType.DMA((2 + PIECES,))],
+                east_next,
+                rest_next,
+                *levels,
                 out_specs=anywhere(2),
             )
-            return height, wind.reshape(wind_field.shape)
-        height, wind, near_pack = call(
-            functools.partial(update_kernel, False),
-            "update_fields",
-            moving,
-            [],
+            return height, winds.reshape(wind_field.shape)
+        rest, height, near_pack, far_pack = call(
+            kernel,
+            "north_and_height",
+            [two, one, pack_shape, pack_shape],
+            working(counts[1]),
             *args,
+            east_next,
+            *levels,
+            cost=SECOND_COST,
         )
-        far_wind, far_height = from_antipode(wind), from_antipode(height)
+        east = east_next
+        far_second = from_antipode(rest)
 
 
 def solution(mesh):

time: 30.3 us -> 27.6 us (0.911)
  the two profiles are of different devices: /device:TPU:10 before, /device:TPU:8 now
where the time goes in v3:
time: 27.6 us; the launch traced here: 27.4 us
  starting transfers between devices  17.2 us (62%)
  Pallas kernels  7.13 us (26%)
  other arithmetic  1.05 us (4%)
  waiting for transfers between devices  0.85 us (3%)
  between operations  0.85 us (3%)
  local copies, waits for them, and re-layouts  0.38 us (1%)
    ppermute x8, starting transfers between devices, exchange(): return lax.ppermute(value, axis, pairs + [(j, i) for i, j in pairs])  11.9 us
    pallas_call x8, Pallas kernels, call(): pl.pallas_call(kernel, out_shape=outs, in_specs=in_specs or vmem(len(args...  7.13 us
    ppermute x4, starting transfers between devices, from_antipode(): lax.ppermute(value, 'lon', [(i, (i + size // 2) % size) for i in range(si...  5.3 us
    concatenate x1, other arithmetic, body(): fields = jnp.concatenate([thickness, winds], 0)  1.05 us
  transfers between devices with their start and end apart: 12, of which 3 were waited for; matrix products, arithmetic and copies ran while one was open for 4% of the time, Pallas kernels for 23%

profile of v3, /device:TPU:8, one launch (start us, length us, event | category | flops | bytes accessed | tf_op | source)
XLA Modules:
  0.0 27.4 jit_solution(13678347620526947770)
XLA Ops:
  0.6 1.6 %collective-permute-start = (f32[2,16,2048]{2,1,0:T(8,128)}, f32[2,16,2048]{2,1,0:T(8,128)S(1)}, u32[]{:S(2)}, u32[]{:S(2)}) collective-permute-start(f32[2,16,2048]{2,1,0:T(8,128)} %bitcast.4), channel_id=1, source_target_pairs={{0,16},{4,20},{8,24},{12,28},{16,0},{20,4},{24,8},{28,12},{1,17},{... | collective-permute-start | bytes 786440 | tf_op jit(solution)/shard_map/ppermute | solution.py:446
  2.2 1.0 %pad_maximum_fusion.fields = f32[3,16,2048]{2,1,0:T(8,128)S(1)} fusion(f32[2,16,2048]{2,1,0:T(8,128)} %bitcast.5, f32[1,16,2048]{2,1,0:T(8,128)} %param.10), kind=kLoop, calls=%fused_computation | loop fusion | flops 98304 | bytes 786432 | tf_op jit(solution)/shard_map/concatenate | solution.py:488
  3.3 0.0 copy-start
  3.3 0.0 copy-start.1
  3.3 0.0 copy-start.2
  3.3 0.0 copy-start.3
  3.3 0.1 gather_fields.1
  3.4 0.1 collective-permute-start.1
  3.5 1.5 %collective-permute-start.2 = (f32[8,2304]{1,0:T(8,128)S(1)}, f32[8,2304]{1,0:T(8,128)S(1)}, u32[]{:S(2)}, u32[]{:S(2)}) collective-permute-start(f32[8,2304]{1,0:T(8,128)S(1)} %get-tuple-element.26), channel_id=1, source_target_pairs={{4,8},{12,16},{20,24},{28,0},{8,4},{16,12},{24,20},{0,28},{5,9},{1... | collective-permute-start | bytes 221192 | tf_op jit(solution)/shard_map/ppermute | solution.py:441
  5.0 0.4 %collective-permute-start.5 = (f32[1,16,2048]{2,1,0:T(8,128)S(1)}, f32[1,16,2048]{2,1,0:T(8,128)S(1)}, u32[]{:S(2)}, u32[]{:S(2)}) collective-permute-start(f32[1,16,2048]{2,1,0:T(8,128)S(1)} %get-tuple-element.31), channel_id=1, source_target_pairs={{0,1},{2,3},{1,0},{3,2},{4,5},{6,7},{5,4},{7,6},{8,9},{10,11},{9,8... | collective-permute-start | bytes 393224 | tf_op jit(solution)/shard_map/ppermute | solution.py:441
  5.5 4.6 %collective-permute-start.6 = (f32[1,16,2048]{2,1,0:T(8,128)S(1)}, f32[1,16,2048]{2,1,0:T(8,128)S(1)}, u32[]{:S(2)}, u32[]{:S(2)}) collective-permute-start(f32[1,16,2048]{2,1,0:T(8,128)S(1)} %get-tuple-element.31), channel_id=1, source_target_pairs={{1,2},{2,1},{5,6},{6,5},{9,10},{10,9},{13,14},{14,13},{17,18},{18,... | collective-permute-start | bytes 393224 | tf_op jit(solution)/shard_map/ppermute | solution.py:441
  10.1 1.6 %collective-permute-start.4 = (f32[1,16,2048]{2,1,0:T(8,128)S(1)}, f32[1,16,2048]{2,1,0:T(8,128)S(1)}, u32[]{:S(2)}, u32[]{:S(2)}) collective-permute-start(f32[1,16,2048]{2,1,0:T(8,128)S(1)} %copy-done.8), channel_id=1, source_target_pairs={{0,16},{4,20},{8,24},{12,28},{16,0},{20,4},{24,8},{28,12},{1,17},{... | collective-permute-start | bytes 393224 | tf_op jit(solution)/shard_map/ppermute | solution.py:446
  11.7 0.0 copy-start.4
  11.7 0.0 copy-start.5
  11.7 0.0 copy-start.7
  11.8 0.6 %own_spectra.2 = (f32[544,256]{1,0:T(8,128)S(1)}, f32[272,256]{1,0:T(8,128)S(1)}) custom-call(f32[8,2304]{1,0:T(8,128)S(1)} %collective-permute-done.1.near, f32[1,16,2048]{2,1,0:T(8,128)S(1)} %get-tuple-element.23.east, f32[2,16,2048]{2,1,0:T(8,128)S(1)} %get-tuple-element.24.rest, f32[34,128]{1,0:T(8,128)S(1)} %copy-done.3, f32[51,256]{1,0:T(8,128)S(1)} %copy-done.2, ...), custom_call_target="tpu_custom_call" | custom-call | tf_op jit(solution)/shard_map/own_spectra/pallas_call | solution.py:474
  12.4 0.2 copy-done.4
  12.7 0.1 copy-done.5
  12.7 1.7 %eastward_wind.2 = (f32[1,16,2048]{2,1,0:T(8,128)S(1)}, f32[2,16,2048]{2,1,0:T(8,128)S(1)}, f32[2,16,2048]{2,1,0:T(8,128)S(1)}) custom-call(f32[2,16,2048]{2,1,0:T(8,128)S(1)} %collective-permute-done.far_rows, f32[544,256]{1,0:T(8,128)S(1)} %get-tuple-element.25.spectrum, f32[1,16,2048]{2,1,0:T(8,128)S(1)} %get-tuple-element.23.east, ...), custom_call_target="tpu_custom_call" | custom-call | flops 2000000000 | bytes 6666666 | tf_op jit(solution)/shard_map/eastward_wind/pallas_call | solution.py:474
  14.4 0.6 %collective-permute-start.3 = (f32[1,16,2048]{2,1,0:T(8,128)S(1)}, f32[1,16,2048]{2,1,0:T(8,128)S(1)}, u32[]{:S(2)}, u32[]{:S(2)}) collective-permute-start(f32[1,16,2048]{2,1,0:T(8,128)S(1)} %get-tuple-element.27.refs_8_.east), channel_id=1, source_target_pairs={{0,16},{4,20},{8,24},{12,28},{16,0},{20,4},{24,8},{28,12},{1,17},{... | collective-permute-start | bytes 393224 | tf_op jit(solution)/shard_map/ppermute | solution.py:446
  15.0 0.1 collective-permute-done.4.far_rows
  15.1 0.9 %north_and_height.2 = (f32[2,16,2048]{2,1,0:T(8,128)S(1)}, f32[1,16,2048]{2,1,0:T(8,128)S(1)}, f32[8,2304]{1,0:T(8,128)S(1)}, f32[8,2304]{1,0:T(8,128)S(1)}) custom-call(f32[1,16,2048]{2,1,0:T(8,128)S(1)} %collective-permute-done.4.far_rows, f32[272,256]{1,0:T(8,128)S(1)} %get-tuple-element.28.spectrum, f32[2,16,2048]{2,1,0:T(8,128)S(1)} %get-tuple-element.24.rest, ...), custom_call_target="tpu_custom_call" | custom-call | flops 2000000000 | bytes 6666666 | tf_op jit(solution)/shard_map/north_and_height/pallas_call | solution.py:474
  16.0 1.6 %collective-permute-start.9 = (f32[2,16,2048]{2,1,0:T(8,128)S(1)}, f32[2,16,2048]{2,1,0:T(8,128)S(1)}, u32[]{:S(2)}, u32[]{:S(2)}) collective-permute-start(f32[2,16,2048]{2,1,0:T(8,128)S(1)} %get-tuple-element.33.rest), channel_id=1, source_target_pairs={{0,16},{4,20},{8,24},{12,28},{16,0},{20,4},{24,8},{28,12},{1,17},{... | collective-permute-start | bytes 786440 | tf_op jit(solution)/shard_map/ppermute | solution.py:446
  17.6 0.6 %collective-permute-start.8 = (f32[8,2304]{1,0:T(8,128)S(1)}, f32[8,2304]{1,0:T(8,128)S(1)}, u32[]{:S(2)}, u32[]{:S(2)}) collective-permute-start(f32[8,2304]{1,0:T(8,128)S(1)} %get-tuple-element.35), channel_id=1, source_target_pairs={{4,8},{12,16},{20,24},{28,0},{8,4},{16,12},{24,20},{0,28},{5,9},{1... | collective-permute-start | bytes 221192 | tf_op jit(solution)/shard_map/ppermute | solution.py:441
  18.2 0.2 collective-permute-start.10
  18.4 0.5 %collective-permute-done.7.near = f32[8,2304]{1,0:T(8,128)S(1)} collective-permute-done((f32[8,2304]{1,0:T(8,128)S(1)}, f32[8,2304]{1,0:T(8,128)S(1)}, u32[]{:S(2)}, u32[]{:S(2)}) %collective-permute-start.7) | collective-permute-done | bytes 73760 | tf_op jit(solution)/shard_map/ppermute | solution.py:441
  18.8 4.4 %collective-permute-start.11 = (f32[1,16,2048]{2,1,0:T(8,128)S(1)}, f32[1,16,2048]{2,1,0:T(8,128)S(1)}, u32[]{:S(2)}, u32[]{:S(2)}) collective-permute-start(f32[1,16,2048]{2,1,0:T(8,128)S(1)} %get-tuple-element.39), channel_id=1, source_target_pairs={{1,2},{2,1},{5,6},{6,5},{9,10},{10,9},{13,14},{14,13},{17,18},{18,... | collective-permute-start | bytes 393224 | tf_op jit(solution)/shard_map/ppermute | solution.py:441
  23.2 0.6 %own_spectra.3 = (f32[272,256]{1,0:T(8,128)S(1)}, f32[544,256]{1,0:T(8,128)S(1)}) custom-call(f32[8,2304]{1,0:T(8,128)S(1)} %collective-permute-done.7.near, f32[1,16,2048]{2,1,0:T(8,128)S(1)} %get-tuple-element.27.refs_8_.east, f32[2,16,2048]{2,1,0:T(8,128)S(1)} %get-tuple-element.33.rest, f32[34,128]{1,0:T(8,128)S(1)} %copy-done.3, ...), custom_call_target="tpu_custom_call" | custom-call | tf_op jit(solution)/shard_map/own_spectra/pallas_call | solution.py:474
  23.9 1.2 %eastward_wind.3 = (f32[1,16,2048]{2,1,0:T(8,128)S(1)}, f32[2,16,2048]{2,1,0:T(8,128)S(1)}) custom-call(f32[1,16,2048]{2,1,0:T(8,128)S(1)} %collective-permute-done.3.far_rows, f32[272,256]{1,0:T(8,128)S(1)} %get-tuple-element.34.spectrum, f32[1,16,2048]{2,1,0:T(8,128)S(1)} %get-tuple-element.27.refs_8_.east, f32[2,16,2048]{2,1,0:T(8,128)S(1)} %get-tuple-element.33.rest, ...), custom_call_target="tpu_custom_call" | custom-call | flops 2000000000 | bytes 6666666 | tf_op jit(solution)/shard_map/eastward_wind/pallas_call | solution.py:474
  25.1 0.2 collective-permute-done.9.far_rows
  25.4 1.3 %north_and_height.3.rest = f32[2,16,2048]{2,1,0:T(8,128)S(1)} custom-call(f32[2,16,2048]{2,1,0:T(8,128)S(1)} %collective-permute-done.9.far_rows, f32[544,256]{1,0:T(8,128)S(1)} %get-tuple-element.37.spectrum, f32[2,16,2048]{2,1,0:T(8,128)S(1)} %get-tuple-element.33.rest, f32[2,16,2048]{2,1,0:T(8,128)S(1)} %get-tuple-element.38.zonal_terms, ...), custom_call_target="tpu_custom_call" | custom-call | flops 2000000000 | bytes 6666666 | tf_op jit(solution)/shard_map/north_and_height/pallas_call | solution.py:474
  26.6 0.8 %level_term.1 = (f32[1,16,2048]{2,1,0:T(8,128)}, f32[2,16,2048]{2,1,0:T(8,128)}) custom-call(f32[1,16,2048]{2,1,0:T(8,128)S(1)} %get-tuple-element.36.east, f32[2,16,2048]{2,1,0:T(8,128)S(1)} %north_and_height.3.rest, f32[1,16,2048]{2,1,0:T(8,128)S(1)} %collective-permute-done.10.levels, f32[1,16,2048]{2,1,0:T(8,128)S(1)} %collective-permute-done.11.others), custom_call_target="tpu_custom_call" | custom-call | tf_op jit(solution)/shard_map/level_term/pallas_call | solution.py:474
  (19 shorter events, 0.0 us)
Async XLA Ops:
  0.6 11.8 %collective-permute-start = (f32[2,16,2048]{2,1,0:T(8,128)}, f32[2,16,2048]{2,1,0:T(8,128)S(1)}, u32[]{:S(2)}, u32[]{:S(2)}) collective-permute-start(f32[2,16,2048]{2,1,0:T(8,128)} %bitcast.4), channel_id=1, source_target_pairs={{0,16},{4,20},{8,24},{12,28},{16,0},{20,4},{24,8},{28,12},{1,17},{... | collective-permute-start | bytes 786440 | tf_op jit(solution)/shard_map/ppermute | solution.py:446
  2.2 7.9 %copy-start.8 = (f32[1,16,2048]{2,1,0:T(8,128)S(1)}, f32[1,16,2048]{2,1,0:T(8,128)}, u32[]{:S(2)}) copy-start(f32[1,16,2048]{2,1,0:T(8,128)} %param.10) | copy-start | bytes 393220
  3.3 8.4 %copy-start = (bf16[256,256]{1,0:T(8,128)(2,1)S(1)}, bf16[256,256]{1,0:T(8,128)(2,1)}, u32[]{:S(2)}) copy-start(bf16[256,256]{1,0:T(8,128)(2,1)} %constant.16.clone.high.refs_3_) | copy-start | bytes 393220
  3.3 8.4 %copy-start.1 = (bf16[256,256]{1,0:T(8,128)(2,1)S(1)}, bf16[256,256]{1,0:T(8,128)(2,1)}, u32[]{:S(2)}) copy-start(bf16[256,256]{1,0:T(8,128)(2,1)} %constant.17.clone.low.refs_4_) | copy-start | bytes 393220
  3.3 8.4 %copy-start.2 = (f32[51,256]{1,0:T(8,128)S(1)}, f32[51,256]{1,0:T(8,128)}, u32[]{:S(2)}) copy-start(f32[51,256]{1,0:T(8,128)} %constant.22.clone.masks.refs_2_) | copy-start | bytes 156676
  3.3 8.4 %copy-start.3 = (f32[34,128]{1,0:T(8,128)S(1)}, f32[34,128]{1,0:T(8,128)}, u32[]{:S(2)}) copy-start(f32[34,128]{1,0:T(8,128)} %constant.20.clone.twist.refs_0_) | copy-start | bytes 52228
  3.4 6.7 %collective-permute-start.1 = (f32[8,2304]{1,0:T(8,128)S(1)}, f32[8,2304]{1,0:T(8,128)S(1)}, u32[]{:S(2)}, u32[]{:S(2)}) collective-permute-start(f32[8,2304]{1,0:T(8,128)S(1)} %get-tuple-element.22), channel_id=1, source_target_pairs={{0,4},{8,12},{16,20},{24,28},{4,0},{12,8},{20,16},{28,24},{1,5},{9... | collective-permute-start | bytes 221192 | tf_op jit(solution)/shard_map/ppermute | solution.py:441
  3.5 8.9 %collective-permute-start.2 = (f32[8,2304]{1,0:T(8,128)S(1)}, f32[8,2304]{1,0:T(8,128)S(1)}, u32[]{:S(2)}, u32[]{:S(2)}) collective-permute-start(f32[8,2304]{1,0:T(8,128)S(1)} %get-tuple-element.26), channel_id=1, source_target_pairs={{4,8},{12,16},{20,24},{28,0},{8,4},{16,12},{24,20},{0,28},{5,9},{1... | collective-permute-start | bytes 221192 | tf_op jit(solution)/shard_map/ppermute | solution.py:441
  5.0 10.0 %collective-permute-start.5 = (f32[1,16,2048]{2,1,0:T(8,128)S(1)}, f32[1,16,2048]{2,1,0:T(8,128)S(1)}, u32[]{:S(2)}, u32[]{:S(2)}) collective-permute-start(f32[1,16,2048]{2,1,0:T(8,128)S(1)} %get-tuple-element.31), channel_id=1, source_target_pairs={{0,1},{2,3},{1,0},{3,2},{4,5},{6,7},{5,4},{7,6},{8,9},{10,11},{9,8... | collective-permute-start | bytes 393224 | tf_op jit(solution)/shard_map/ppermute | solution.py:441
  5.5 9.5 %collective-permute-start.6 = (f32[1,16,2048]{2,1,0:T(8,128)S(1)}, f32[1,16,2048]{2,1,0:T(8,128)S(1)}, u32[]{:S(2)}, u32[]{:S(2)}) collective-permute-start(f32[1,16,2048]{2,1,0:T(8,128)S(1)} %get-tuple-element.31), channel_id=1, source_target_pairs={{1,2},{2,1},{5,6},{6,5},{9,10},{10,9},{13,14},{14,13},{17,18},{18,... | collective-permute-start | bytes 393224 | tf_op jit(solution)/shard_map/ppermute | solution.py:441
  10.1 5.0 %collective-permute-start.4 = (f32[1,16,2048]{2,1,0:T(8,128)S(1)}, f32[1,16,2048]{2,1,0:T(8,128)S(1)}, u32[]{:S(2)}, u32[]{:S(2)}) collective-permute-start(f32[1,16,2048]{2,1,0:T(8,128)S(1)} %copy-done.8), channel_id=1, source_target_pairs={{0,16},{4,20},{8,24},{12,28},{16,0},{20,4},{24,8},{28,12},{1,17},{... | collective-permute-start | bytes 393224 | tf_op jit(solution)/shard_map/ppermute | solution.py:446
  11.7 1.0 %copy-start.4 = (bf16[256,512]{1,0:T(8,128)(2,1)S(1)}, bf16[256,512]{1,0:T(8,128)(2,1)}, u32[]{:S(2)}) copy-start(bf16[256,512]{1,0:T(8,128)(2,1)} %constant.18.clone.refs_5_) | copy-start | bytes 786436
  11.7 1.0 %copy-start.5 = (bf16[256,512]{1,0:T(8,128)(2,1)S(1)}, bf16[256,512]{1,0:T(8,128)(2,1)}, u32[]{:S(2)}) copy-start(bf16[256,512]{1,0:T(8,128)(2,1)} %constant.19.clone.refs_6_) | copy-start | bytes 786436
  11.7 1.0 %copy-start.6 = (f32[68,128]{1,0:T(8,128)S(1)}, f32[68,128]{1,0:T(8,128)}, u32[]{:S(2)}) copy-start(f32[68,128]{1,0:T(8,128)} %constant.21.clone.refs_1_) | copy-start | bytes 104452
  11.7 1.0 %copy-start.7 = (f32[2,2048]{1,0:T(2,128)S(1)}, f32[2,2048]{1,0:T(2,128)}, u32[]{:S(2)}) copy-start(f32[2,2048]{1,0:T(2,128)} %constant.23.clone.rows) | copy-start | bytes 49156
  14.4 9.5 %collective-permute-start.3 = (f32[1,16,2048]{2,1,0:T(8,128)S(1)}, f32[1,16,2048]{2,1,0:T(8,128)S(1)}, u32[]{:S(2)}, u32[]{:S(2)}) collective-permute-start(f32[1,16,2048]{2,1,0:T(8,128)S(1)} %get-tuple-element.27.refs_8_.east), channel_id=1, source_target_pairs={{0,16},{4,20},{8,24},{12,28},{16,0},{20,4},{24,8},{28,12},{1,17},{... | collective-permute-start | bytes 393224 | tf_op jit(solution)/shard_map/ppermute | solution.py:446
  16.0 9.3 %collective-permute-start.9 = (f32[2,16,2048]{2,1,0:T(8,128)S(1)}, f32[2,16,2048]{2,1,0:T(8,128)S(1)}, u32[]{:S(2)}, u32[]{:S(2)}) collective-permute-start(f32[2,16,2048]{2,1,0:T(8,128)S(1)} %get-tuple-element.33.rest), channel_id=1, source_target_pairs={{0,16},{4,20},{8,24},{12,28},{16,0},{20,4},{24,8},{28,12},{1,17},{... | collective-permute-start | bytes 786440 | tf_op jit(solution)/shard_map/ppermute | solution.py:446
  17.6 1.3 %collective-permute-start.7 = (f32[8,2304]{1,0:T(8,128)S(1)}, f32[8,2304]{1,0:T(8,128)S(1)}, u32[]{:S(2)}, u32[]{:S(2)}) collective-permute-start(f32[8,2304]{1,0:T(8,128)S(1)} %get-tuple-element.32), channel_id=1, source_target_pairs={{0,4},{8,12},{16,20},{24,28},{4,0},{12,8},{20,16},{28,24},{1,5},{9... | collective-permute-start | bytes 221192 | tf_op jit(solution)/shard_map/ppermute | solution.py:441
  17.6 6.3 %collective-permute-start.8 = (f32[8,2304]{1,0:T(8,128)S(1)}, f32[8,2304]{1,0:T(8,128)S(1)}, u32[]{:S(2)}, u32[]{:S(2)}) collective-permute-start(f32[8,2304]{1,0:T(8,128)S(1)} %get-tuple-element.35), channel_id=1, source_target_pairs={{4,8},{12,16},{20,24},{28,0},{8,4},{16,12},{24,20},{0,28},{5,9},{1... | collective-permute-start | bytes 221192 | tf_op jit(solution)/shard_map/ppermute | solution.py:441
  18.2 8.4 %collective-permute-start.10 = (f32[1,16,2048]{2,1,0:T(8,128)S(1)}, f32[1,16,2048]{2,1,0:T(8,128)S(1)}, u32[]{:S(2)}, u32[]{:S(2)}) collective-permute-start(f32[1,16,2048]{2,1,0:T(8,128)S(1)} %get-tuple-element.39), channel_id=1, source_target_pairs={{0,1},{2,3},{1,0},{3,2},{4,5},{6,7},{5,4},{7,6},{8,9},{10,11},{9,8... | collective-permute-start | bytes 393224 | tf_op jit(solution)/shard_map/ppermute | solution.py:441
  18.8 7.8 %collective-permute-start.11 = (f32[1,16,2048]{2,1,0:T(8,128)S(1)}, f32[1,16,2048]{2,1,0:T(8,128)S(1)}, u32[]{:S(2)}, u32[]{:S(2)}) collective-permute-start(f32[1,16,2048]{2,1,0:T(8,128)S(1)} %get-tuple-element.39), channel_id=1, source_target_pairs={{1,2},{2,1},{5,6},{6,5},{9,10},{10,9},{13,14},{14,13},{17,18},{18,... | collective-permute-start | bytes 393224 | tf_op jit(solution)/shard_map/ppermute | solution.py:441

commit v4 on v3

--- a/solution.py
+++ b/solution.py
@@ -18,8 +18,12 @@
 
 RADIX = 128
 ROWS = 8
-FIRST_COST = 2000000000
-SECOND_COST = 2000000000
+FIRST_COST = 2_000_000_000
+SECOND_COST = 2_000_000_000
+EAST_COST = 2_000_000_000
+REST_COST = 2_000_000_000
+ZONAL_COST = 2000000000
+LATE_ZONAL_COST = 1
 PIECES = 4
 HALO = 3
 
@@ -239,7 +243,7 @@
     pack_rows(far_pack, lat_count, field, index, jnp.where(odd, last, first))
 
 
-def gather_kernel(fields, east, rest, height, near_pack, far_pack):
+def gather_kernel(fields, east, rest, near_pack, far_pack):
     lat_count = fields.shape[-1]
     for index in range(lat_count // RADIX):
         at = tile(index)
@@ -247,13 +251,12 @@
         east[0, :, at] = eastward
         rest[0, :, at] = northward
         rest[1, :, at] = thickness
-        height[0, :, at] = thickness
         for field, rows in enumerate((eastward, northward, thickness)):
             pack_tile(field, index, rows, near_pack, far_pack, lat_count)
 
 
 def own_kernel(blocks, split_at, near, east, rest, twist, masks, high, low, *refs):
-    first, second, turned = refs
+    first, second, turned = refs[-3:]
     kept = blocks // 2 + 1
     lon_count = east.shape[1]
     groups = [(field, at) for field in range(3) for at in row_groups(lon_count)]
@@ -316,108 +319,129 @@
             slope[field, out, tile(m)] = value
 
 
-def first_kernel(blocks, with_north, far_rows, spectrum, east, rest, near, far, rows, *refs):
-    tables, refs = refs[:7], refs[7:]
+def zonal_parts(index, east, rest, near, far, rows):
     lon_count, lat_count = east.shape[1:]
     odd = odd_device()
-    east_next, zonal_terms = refs[:2]
-    if with_north:
-        north_terms, refs = refs[2], refs[3:]
-    else:
-        refs = refs[2:]
-    smooth, slope, *work = refs
-    count = far_rows.shape[0]
-    transform(blocks, (-1,) * count, far_rows, spectrum, tables, smooth, slope, work)
-    if with_north:
-        north_terms[0] = smooth[1]
-        north_terms[1] = slope[1]
-    for index in range(lat_count // RADIX):
-        here = [field_at(east, rest, field, slice(None), tile(index)) for field in range(3)]
-        secant, turning = rows[0:1, tile(index)], rows[1:2, tile(index)]
-        zonal = []
-        for field in range(3):
-            close = halo_rows(near, lat_count, field, index)
-            away = halo_rows(far, lat_count, field, index)
-            line = jnp.concatenate(
-                [jnp.where(odd, close, away), here[field], jnp.where(odd, away, close)], 0
-            )
-            at = [line[i : i + lon_count] for i in range(2 * HALO + 1)]
-            difference = (
-                (45.0 / 60.0) * (at[4] - at[2])
-                - (9.0 / 60.0) * (at[5] - at[1])
-                + (1.0 / 60.0) * (at[6] - at[0])
-            )
-            zonal.append(secant * difference)
-        eastward, northward, thick = here
-        tendency = (
-            turning * northward
-            - eastward * zonal[0]
-            - northward * slope[0, :, tile(index)]
-            - zonal[2]
-        )
-        east_next[0, :, tile(index)] = smooth[0, :, tile(index)] + courant * tendency
-        zonal_terms[0, :, tile(index)] = -eastward * zonal[1] - turning * eastward
-        zonal_terms[1, :, tile(index)] = -eastward * zonal[2] - thick * zonal[0]
+    here = [field_at(east, rest, field, slice(None), tile(index)) for field in range(3)]
+    secant, turning = rows[0:1, tile(index)], rows[1:2, tile(index)]
+    zonal = []
+    for field in range(3):
+        close = halo_rows(near, lat_count, field, index)
+        away = halo_rows(far, lat_count, field, index)
+        line = jnp.concatenate(
+            [jnp.where(odd, close, away), here[field], jnp.where(odd, away, close)], 0
+        )
+        at = [line[i : i + lon_count] for i in range(2 * HALO + 1)]
+        difference = (
+            (45.0 / 60.0) * (at[4] - at[2])
+            - (9.0 / 60.0) * (at[5] - at[1])
+            + (1.0 / 60.0) * (at[6] - at[0])
+        )
+        zonal.append(secant * difference)
+    eastward, northward, thick = here
+    return here, (
+        turning * northward - eastward * zonal[0] - zonal[2],
+        -eastward * zonal[1] - turning * eastward,
+        -eastward * zonal[2] - thick * zonal[0],
+    )
+
+
+def first_kernel(blocks, far_rows, spectrum, east, rest, zonal_terms, *refs):
+    tables, refs = refs[:7], refs[7:]
+    east_next, north_terms, smooth, slope, *work = refs
+    transform(blocks, (-1, -1), far_rows, spectrum, tables, smooth, slope, work)
+    north_terms[0] = smooth[1]
+    north_terms[1] = slope[1]
+    for index in range(east.shape[-1] // RADIX):
+        at = tile(index)
+        tendency = zonal_terms[0, :, at] - rest[0, :, at] * slope[0, :, at]
+        east_next[0, :, at] = smooth[0, :, at] + courant * tendency
 
 
 def second_kernel(
-    blocks, with_north, final, far_rows, spectrum, rest, zonal_terms, *refs
+    blocks, far_rows, spectrum, rest, zonal_terms, north_terms, east_next, levels, others, *refs
 ):
     tables, refs = refs[:7], refs[7:]
-    if with_north:
-        north_terms, refs = refs[0], refs[1:]
+    rest_next, height_next, near_pack, far_pack, smooth, slope, *work = refs
     lat_count = rest.shape[-1]
-    if final:
-        rest_next, *refs = refs
-    else:
-        (east_next, levels, others, rest_next, height_next, near_pack, far_pack, *refs) = refs
-    smooth, slope, *work = refs
-    parities = (1,) if with_north else (-1, 1)
-    transform(blocks, parities, far_rows, spectrum, tables, smooth, slope, work)
+    transform(blocks, (1,), far_rows, spectrum, tables, smooth, slope, work)
     for index in range(lat_count // RADIX):
         at = tile(index)
         northward, thick = rest[0, :, at], rest[1, :, at]
-        last = len(parities) - 1
-        thick_smooth, thick_slope = smooth[last, :, at], slope[last, :, at]
-        north_smooth = north_terms[0, :, at] if with_north else smooth[0, :, at]
-        north_slope = north_terms[1, :, at] if with_north else slope[0, :, at]
-        north_tendency = zonal_terms[0, :, at] - northward * north_slope - thick_slope
-        thick_tendency = zonal_terms[1, :, at] - northward * thick_slope - thick * north_slope
-        if final:
-            thick_tendency -= 2.0 * mixing * thick
-        else:
-            thick_tendency += mixing * (levels[0, :, at] + others[0, :, at] - 2.0 * thick)
+        north_slope, thick_slope = north_terms[1, :, at], slope[0, :, at]
+        vertical = levels[0, :, at] + others[0, :, at] - 2.0 * thick
+        north_tendency = zonal_terms[1, :, at] - northward * north_slope - thick_slope
+        thick_tendency = (
+            zonal_terms[2, :, at]
+            - northward * thick_slope
+            - thick * north_slope
+            + mixing * vertical
+        )
         values = (
-            north_smooth + courant * north_tendency,
-            thick_smooth + courant * thick_tendency,
+            north_terms[0, :, at] + courant * north_tendency,
+            smooth[0, :, at] + courant * thick_tendency,
         )
         for field in range(2):
             rest_next[field, :, at] = values[field]
-        if not final:
-            height_next[0, :, at] = values[1]
-            for field, moved in enumerate((east_next[0, :, at], *values)):
-                pack_tile(field, index, moved, near_pack, far_pack, lat_count)
-
-
-def last_kernel(east, rest, levels, others, height_out, wind_out, height, sems):
-    tiles = height.shape[-1] // RADIX
-    copies = [
-        pltpu.make_async_copy(east.at[0], wind_out.at[0], sems.at[0]),
-        pltpu.make_async_copy(rest.at[0], wind_out.at[1], sems.at[1]),
-    ]
-    for copy in copies:
-        copy.start()
+        height_next[0, :, at] = values[1]
+        for field, moved in enumerate((east_next[0, :, at], *values)):
+            pack_tile(field, index, moved, near_pack, far_pack, lat_count)
+
+
+def transform_kernel(blocks, parities, far_rows, spectrum, *refs):
+    tables, (smooth, slope, *work) = refs[:7], refs[7:]
+    transform(blocks, parities, far_rows, spectrum, tables, smooth, slope, work)
+
+
+def zonal_kernel(east, rest, near, far, rows, out):
+    for index in range(east.shape[-1] // RADIX):
+        _, terms = zonal_parts(index, east, rest, near, far, rows)
+        for field in range(3):
+            out[field, :, tile(index)] = terms[field]
+
+
+def last_kernel(
+    rest,
+    zonal_terms,
+    east_smooth,
+    east_slope,
+    rest_smooth,
+    rest_slope,
+    levels,
+    others,
+    height_out,
+    wind_out,
+    staged,
+    sems,
+):
+    tiles = rest.shape[-1] // RADIX
+    copies = []
     for piece in range(PIECES):
         for index in range(piece * tiles // PIECES, (piece + 1) * tiles // PIECES):
             at = tile(index)
-            height[:, at] = rest[1, :, at] + (courant * mixing) * (
-                levels[0, :, at] + others[0, :, at]
+            northward, thick = rest[0, :, at], rest[1, :, at]
+            north_slope, thick_slope = rest_slope[0, :, at], rest_slope[1, :, at]
+            vertical = levels[0, :, at] + others[0, :, at] - 2.0 * thick
+            tendencies = (
+                zonal_terms[0, :, at] - northward * east_slope[0, :, at],
+                zonal_terms[1, :, at] - northward * north_slope - thick_slope,
+                zonal_terms[2, :, at]
+                - northward * thick_slope
+                - thick * north_slope
+                + mixing * vertical,
             )
+            smooths = (east_smooth[0, :, at], rest_smooth[0, :, at], rest_smooth[1, :, at])
+            for field in range(3):
+                staged[field, :, at] = smooths[field] + courant * tendencies[field]
         span = pl.ds(piece * tiles // PIECES * RADIX, tiles // PIECES * RADIX)
-        copies.append(
-            pltpu.make_async_copy(height.at[:, span], height_out.at[0, :, span], sems.at[2 + piece])
-        )
-        copies[-1].start()
+        targets = (wind_out.at[0, :, span], wind_out.at[1, :, span], height_out.at[0, :, span])
+        for field, target in enumerate(targets):
+            copies.append(
+                pltpu.make_async_copy(
+                    staged.at[field, :, span], target, sems.at[3 * piece + field]
+                )
+            )
+            copies[-1].start()
     for copy in copies:
         copy.wait()
 
@@ -486,13 +510,13 @@
     winds = wind_field.reshape(2, lon_count, lat_count)
     far_first, far_second = from_antipode(winds), from_antipode(thickness)
     fields = jnp.concatenate([thickness, winds], 0)
-    east, rest, height, near_pack, far_pack = call(
-        gather_kernel, "gather_fields", [one, two, one, pack_shape, pack_shape], [], fields
-    )
+    east, rest, near_pack, far_pack = call(
+        gather_kernel, "gather_fields", [one, two, pack_shape, pack_shape], [], fields
+    )
+    height = thickness
     for step in range(STEPS):
         final = step == STEPS - 1
-        with_north = step == 0
-        counts = (2, 1) if with_north else (1, 2)
+        counts = (2, 1) if step == 0 else (1, 2)
         near = exchange(near_pack, "lon", 0)
         levels = [exchange(height, "lev", first) for first in (0, 1)]
         far = exchange(far_pack, "lon", 1)
@@ -507,54 +531,89 @@
             twist,
             masks,
             *forward_tables,
-            in_specs=anywhere(1) + vmem(6),
-        )
-        east_next, zonal_terms, *north_terms = call(
-            functools.partial(first_kernel, blocks, with_north),
-            "eastward_wind",
-            [one, two] + [two] * with_north,
-            working(counts[0]),
-            far_first,
-            spectra[0],
+            *inverse_tables,
+            back,
+            in_specs=anywhere(1) + vmem(9),
+        )
+        (zonal_terms,) = call(
+            zonal_kernel,
+            "zonal_terms",
+            [array(3, lon_count, lat_count)],
+            [],
             east,
             rest,
             near,
             far,
             rows,
+            cost=LATE_ZONAL_COST if final else ZONAL_COST,
+        )
+        if final:
+            break
+        east_next, north_terms = call(
+            functools.partial(first_kernel, blocks),
+            "eastward_wind",
+            [one, two],
+            working(2),
+            far_first,
+            spectra[0],
+            east,
+            rest,
+            zonal_terms,
             *tables,
             cost=FIRST_COST,
         )
-        if not final:
-            far_first = from_antipode(east_next)
-        args = (far_second, spectra[1], rest, zonal_terms, *tables, *north_terms)
-        kernel = functools.partial(second_kernel, blocks, with_north, final)
-        if final:
-            (rest_next,) = call(
-                kernel, "north_and_height", [two], working(counts[1]), *args, cost=SECOND_COST
-            )
-            height, winds = call(
-                last_kernel,
-                "level_term",
-                [one, two],
-                [scratch(lon_count, lat_count), pltpu.SemaphoreType.DMA((2 + PIECES,))],
-                east_next,
-                rest_next,
-                *levels,
-                out_specs=anywhere(2),
-            )
-            return height, winds.reshape(wind_field.shape)
+        far_first = from_antipode(east_next)
         rest, height, near_pack, far_pack = call(
-            kernel,
+            functools.partial(second_kernel, blocks),
             "north_and_height",
             [two, one, pack_shape, pack_shape],
-            working(counts[1]),
-            *args,
+            working(1),
+            far_second,
+            spectra[1],
+            rest,
+            zonal_terms,
+            north_terms,
             east_next,
             *levels,
+            *tables,
             cost=SECOND_COST,
         )
         east = east_next
         far_second = from_antipode(rest)
+
+    east_terms = call(
+        functools.partial(transform_kernel, blocks, (-1,)),
+        "transform_east",
+        [one, one],
+        working(1)[2:],
+        far_first,
+        spectra[0],
+        *tables,
+        cost=EAST_COST,
+    )
+    rest_terms = call(
+        functools.partial(transform_kernel, blocks, (-1, 1)),
+        "transform_rest",
+        [two, two],
+        working(2)[2:],
+        far_second,
+        spectra[1],
+        *tables,
+        cost=REST_COST,
+    )
+    height, winds = call(
+        last_kernel,
+        "last_update",
+        [one, two],
+        [scratch(3, lon_count, lat_count), pltpu.SemaphoreType.DMA((3 * PIECES,))],
+        rest,
+        zonal_terms,
+        *east_terms,
+        *rest_terms,
+        *levels,
+        out_specs=anywhere(2),
+    )
+    return height, winds.reshape(wind_field.shape)
 
 
 def solution(mesh):

time: 27.6 us -> 27.3 us (0.989)
    pallas_call x8 -> x10, Pallas kernels: 7.13 us -> 7.05 us  [call(): pl.pallas_call(kernel, out_shape=outs, in_specs=in_specs or vmem(len(args...]
  transfers between devices with their start and end apart: 12 -> 12, of which waited for: 3 -> 2; matrix products, arithmetic and copies ran while one was open for 4% -> 4% of each run, Pallas kernels for 23% -> 23%
where the time goes in v4:
time: 27.3 us; the launch traced here: 27.1 us
  starting transfers between devices  17.2 us (63%)
  Pallas kernels  7.05 us (26%)
  other arithmetic  1.07 us (4%)
  between operations  0.88 us (3%)
  waiting for transfers between devices  0.71 us (3%)
    ppermute x8, starting transfers between devices, exchange(): return lax.ppermute(value, axis, pairs + [(j, i) for i, j in pairs])  12 us
    pallas_call x10, Pallas kernels, call(): pl.pallas_call(kernel, out_shape=outs, in_specs=in_specs or vmem(len(args...  7.05 us
    ppermute x4, starting transfers between devices, from_antipode(): lax.ppermute(value, 'lon', [(i, (i + size // 2) % size) for i in range(si...  5.26 us
    concatenate x1, other arithmetic, body(): fields = jnp.concatenate([thickness, winds], 0)  1.07 us
  transfers between devices with their start and end apart: 12, of which 2 were waited for; matrix products, arithmetic and copies ran while one was open for 4% of the time, Pallas kernels for 23%

profile of v4, /device:TPU:8, one launch (start us, length us, event | category | flops | bytes accessed | tf_op | source)
XLA Modules:
  0.0 27.1 jit_solution(636413495476214229)
XLA Ops:
  0.6 1.6 %collective-permute-start.3 = (f32[2,16,2048]{2,1,0:T(8,128)}, f32[2,16,2048]{2,1,0:T(8,128)S(1)}, u32[]{:S(2)}, u32[]{:S(2)}) collective-permute-start(f32[2,16,2048]{2,1,0:T(8,128)} %bitcast.4), channel_id=1, source_target_pairs={{0,16},{4,20},{8,24},{12,28},{16,0},{20,4},{24,8},{28,12},{1,17},{... | collective-permute-start | bytes 786440 | tf_op jit(solution)/shard_map/ppermute | solution.py:470
  2.2 0.0 copy-start.5
  2.2 0.0 copy-start.6
  2.3 1.1 %pad_maximum_fusion.fields = f32[3,16,2048]{2,1,0:T(8,128)S(1)} fusion(f32[2,16,2048]{2,1,0:T(8,128)} %bitcast.5, f32[1,16,2048]{2,1,0:T(8,128)} %param.10), kind=kLoop, calls=%fused_computation | loop fusion | flops 98304 | bytes 786432 | tf_op jit(solution)/shard_map/concatenate | solution.py:512
  3.3 0.0 copy-start
  3.3 0.0 copy-start.2
  3.3 0.1 gather_fields.1
  3.4 0.1 collective-permute-start.1
  3.5 1.5 %collective-permute-start.2 = (f32[8,2304]{1,0:T(8,128)S(1)}, f32[8,2304]{1,0:T(8,128)S(1)}, u32[]{:S(2)}, u32[]{:S(2)}) collective-permute-start(f32[8,2304]{1,0:T(8,128)S(1)} %get-tuple-element.26), channel_id=1, source_target_pairs={{4,8},{12,16},{20,24},{28,0},{8,4},{16,12},{24,20},{0,28},{5,9},{1... | collective-permute-start | bytes 221192 | tf_op jit(solution)/shard_map/ppermute | solution.py:465
  5.0 1.5 %collective-permute-start = (f32[1,16,2048]{2,1,0:T(8,128)S(1)}, f32[1,16,2048]{2,1,0:T(8,128)S(1)}, u32[]{:S(2)}, u32[]{:S(2)}) collective-permute-start(f32[1,16,2048]{2,1,0:T(8,128)S(1)} %copy-done.8), channel_id=1, source_target_pairs={{0,16},{4,20},{8,24},{12,28},{16,0},{20,4},{24,8},{28,12},{1,17},{... | collective-permute-start | bytes 393224 | tf_op jit(solution)/shard_map/ppermute | solution.py:470
  6.6 0.4 %collective-permute-start.4 = (f32[1,16,2048]{2,1,0:T(8,128)S(1)}, f32[1,16,2048]{2,1,0:T(8,128)S(1)}, u32[]{:S(2)}, u32[]{:S(2)}) collective-permute-start(f32[1,16,2048]{2,1,0:T(8,128)S(1)} %copy-done.8), channel_id=1, source_target_pairs={{0,1},{2,3},{1,0},{3,2},{4,5},{6,7},{5,4},{7,6},{8,9},{10,11},{9,8... | collective-permute-start | bytes 393224 | tf_op jit(solution)/shard_map/ppermute | solution.py:465
  7.0 4.6 %collective-permute-start.5 = (f32[1,16,2048]{2,1,0:T(8,128)S(1)}, f32[1,16,2048]{2,1,0:T(8,128)S(1)}, u32[]{:S(2)}, u32[]{:S(2)}) collective-permute-start(f32[1,16,2048]{2,1,0:T(8,128)S(1)} %copy-done.8), channel_id=1, source_target_pairs={{1,2},{2,1},{5,6},{6,5},{9,10},{10,9},{13,14},{14,13},{17,18},{18,... | collective-permute-start | bytes 393224 | tf_op jit(solution)/shard_map/ppermute | solution.py:465
  11.7 0.0 copy-start.7
  11.7 0.6 %own_spectra.2 = (f32[544,256]{1,0:T(8,128)S(1)}, f32[272,256]{1,0:T(8,128)S(1)}) custom-call(f32[8,2304]{1,0:T(8,128)S(1)} %collective-permute-done.1.near, f32[1,16,2048]{2,1,0:T(8,128)S(1)} %get-tuple-element.23.east, f32[2,16,2048]{2,1,0:T(8,128)S(1)} %get-tuple-element.24.rest, f32[34,128]{1,0:T(8,128)S(1)} %copy-done.6, f32[51,256]{1,0:T(8,128)S(1)} %copy-done.4, ...), custom_call_target="tpu_custom_call" | custom-call | tf_op jit(solution)/shard_map/own_spectra/pallas_call | solution.py:498
  12.3 0.0 collective-permute-done.2.far
  12.4 0.1 copy-done.7
  12.4 0.5 %zonal_terms.2 = f32[3,16,2048]{2,1,0:T(8,128)S(1)} custom-call(f32[1,16,2048]{2,1,0:T(8,128)S(1)} %get-tuple-element.23.east, f32[2,16,2048]{2,1,0:T(8,128)S(1)} %get-tuple-element.24.rest, f32[8,2304]{1,0:T(8,128)S(1)} %collective-permute-done.1.near, f32[8,2304]{1,0:T(8,128)S(1)} %collective-permute-done.2.far, f32[2,2048]{1,0:T(2,128)S(1)} %copy-done.7), custom_call_target="tpu_custom_call" | custom-call | flops 2000000000 | bytes 6666666 | tf_op jit(solution)/shard_map/zonal_terms/pallas_call | solution.py:498
  12.9 1.2 %eastward_wind.1 = (f32[1,16,2048]{2,1,0:T(8,128)S(1)}, f32[2,16,2048]{2,1,0:T(8,128)S(1)}) custom-call(f32[2,16,2048]{2,1,0:T(8,128)S(1)} %collective-permute-done.3.far_rows, f32[544,256]{1,0:T(8,128)S(1)} %get-tuple-element.27.spectrum, f32[1,16,2048]{2,1,0:T(8,128)S(1)} %get-tuple-element.23.east, f32[2,16,2048]{2,1,0:T(8,128)S(1)} %get-tuple-element.24.rest, ...), custom_call_target="tpu_custom_call" | custom-call | flops 2000000000 | bytes 6666666 | tf_op jit(solution)/shard_map/eastward_wind/pallas_call | solution.py:498
  14.1 0.6 %collective-permute-start.8 = (f32[1,16,2048]{2,1,0:T(8,128)S(1)}, f32[1,16,2048]{2,1,0:T(8,128)S(1)}, u32[]{:S(2)}, u32[]{:S(2)}) collective-permute-start(f32[1,16,2048]{2,1,0:T(8,128)S(1)} %get-tuple-element.29.east_next.east), channel_id=1, source_target_pairs={{0,16},{4,20},{8,24},{12,28},{16,0},{20,4},{24,8},{28,12},{1,17},{... | collective-permute-start | bytes 393224 | tf_op jit(solution)/shard_map/ppermute | solution.py:470
  14.7 0.8 %north_and_height.1 = (f32[2,16,2048]{2,1,0:T(8,128)S(1)}, f32[1,16,2048]{2,1,0:T(8,128)S(1)}, f32[8,2304]{1,0:T(8,128)S(1)}, f32[8,2304]{1,0:T(8,128)S(1)}) custom-call(f32[1,16,2048]{2,1,0:T(8,128)S(1)} %collective-permute-done.far_rows, f32[272,256]{1,0:T(8,128)S(1)} %get-tuple-element.25.spectrum, f32[2,16,2048]{2,1,0:T(8,128)S(1)} %get-tuple-element.24.rest, ...), custom_call_target="tpu_custom_call" | custom-call | flops 2000000000 | bytes 6666666 | tf_op jit(solution)/shard_map/north_and_height/pallas_call | solution.py:498
  15.5 1.6 %collective-permute-start.9 = (f32[2,16,2048]{2,1,0:T(8,128)S(1)}, f32[2,16,2048]{2,1,0:T(8,128)S(1)}, u32[]{:S(2)}, u32[]{:S(2)}) collective-permute-start(f32[2,16,2048]{2,1,0:T(8,128)S(1)} %get-tuple-element.30.rest), channel_id=1, source_target_pairs={{0,16},{4,20},{8,24},{12,28},{16,0},{20,4},{24,8},{28,12},{1,17},{... | collective-permute-start | bytes 786440 | tf_op jit(solution)/shard_map/ppermute | solution.py:470
  17.1 0.7 %collective-permute-start.7 = (f32[8,2304]{1,0:T(8,128)S(1)}, f32[8,2304]{1,0:T(8,128)S(1)}, u32[]{:S(2)}, u32[]{:S(2)}) collective-permute-start(f32[8,2304]{1,0:T(8,128)S(1)} %get-tuple-element.32), channel_id=1, source_target_pairs={{4,8},{12,16},{20,24},{28,0},{8,4},{16,12},{24,20},{0,28},{5,9},{1... | collective-permute-start | bytes 221192 | tf_op jit(solution)/shard_map/ppermute | solution.py:465
  17.8 0.3 %collective-permute-start.10 = (f32[1,16,2048]{2,1,0:T(8,128)S(1)}, f32[1,16,2048]{2,1,0:T(8,128)S(1)}, u32[]{:S(2)}, u32[]{:S(2)}) collective-permute-start(f32[1,16,2048]{2,1,0:T(8,128)S(1)} %get-tuple-element.39), channel_id=1, source_target_pairs={{0,1},{2,3},{1,0},{3,2},{4,5},{6,7},{5,4},{7,6},{8,9},{10,11},{9,8... | collective-permute-start | bytes 393224 | tf_op jit(solution)/shard_map/ppermute | solution.py:465
  18.1 0.3 %collective-permute-done.6.near = f32[8,2304]{1,0:T(8,128)S(1)} collective-permute-done((f32[8,2304]{1,0:T(8,128)S(1)}, f32[8,2304]{1,0:T(8,128)S(1)}, u32[]{:S(2)}, u32[]{:S(2)}) %collective-permute-start.6) | collective-permute-done | bytes 73760 | tf_op jit(solution)/shard_map/ppermute | solution.py:465
  18.4 4.3 %collective-permute-start.11 = (f32[1,16,2048]{2,1,0:T(8,128)S(1)}, f32[1,16,2048]{2,1,0:T(8,128)S(1)}, u32[]{:S(2)}, u32[]{:S(2)}) collective-permute-start(f32[1,16,2048]{2,1,0:T(8,128)S(1)} %get-tuple-element.39), channel_id=1, source_target_pairs={{1,2},{2,1},{5,6},{6,5},{9,10},{10,9},{13,14},{14,13},{17,18},{18,... | collective-permute-start | bytes 393224 | tf_op jit(solution)/shard_map/ppermute | solution.py:465
  22.7 0.5 %zonal_terms.3 = f32[3,16,2048]{2,1,0:T(8,128)S(1)} custom-call(f32[1,16,2048]{2,1,0:T(8,128)S(1)} %get-tuple-element.29.east_next.east, f32[2,16,2048]{2,1,0:T(8,128)S(1)} %get-tuple-element.30.rest, f32[8,2304]{1,0:T(8,128)S(1)} %collective-permute-done.6.near, f32[8,2304]{1,0:T(8,128)S(1)} %collective-permute-done.7.far, f32[2,2048]{1,0:T(2,128)S(1)} %copy-done.7), custom_call_target="tpu_custom_call" | custom-call | flops 1 | tf_op jit(solution)/shard_map/zonal_terms/pallas_call | solution.py:498
  23.2 0.6 %own_spectra.3 = (f32[272,256]{1,0:T(8,128)S(1)}, f32[544,256]{1,0:T(8,128)S(1)}) custom-call(f32[8,2304]{1,0:T(8,128)S(1)} %collective-permute-done.6.near, f32[1,16,2048]{2,1,0:T(8,128)S(1)} %get-tuple-element.29.east_next.east, f32[2,16,2048]{2,1,0:T(8,128)S(1)} %get-tuple-element.30.rest, f32[34,128]{1,0:T(8,128)S(1)} %copy-done.6, ...), custom_call_target="tpu_custom_call" | custom-call | tf_op jit(solution)/shard_map/own_spectra/pallas_call | solution.py:498
  23.8 0.0 collective-permute-done.8.far_rows
  23.8 0.7 %transform_east.1 = (f32[1,16,2048]{2,1,0:T(8,128)S(1)}, f32[1,16,2048]{2,1,0:T(8,128)S(1)}) custom-call(f32[1,16,2048]{2,1,0:T(8,128)S(1)} %collective-permute-done.8.far_rows, f32[272,256]{1,0:T(8,128)S(1)} %get-tuple-element.33.spectrum, f32[34,128]{1,0:T(8,128)S(1)} %copy-done.6, f32[68,128]{1,0:T(8,128)S(1)} %copy-done.5, f32[51,256]{1,0:T(8,128)S(1)} %copy-done.4, ...), custom_call_target="tpu_custom_call" | custom-call | flops 2000000000 | bytes 6666666 | tf_op jit(solution)/shard_map/transform_east/pallas_call | solution.py:498
  24.6 0.4 %collective-permute-done.9.far_rows = f32[2,16,2048]{2,1,0:T(8,128)S(1)} collective-permute-done((f32[2,16,2048]{2,1,0:T(8,128)S(1)}, f32[2,16,2048]{2,1,0:T(8,128)S(1)}, u32[]{:S(2)}, u32[]{:S(2)}) %collective-permute-start.9) | collective-permute-done | bytes 262176 | tf_op jit(solution)/shard_map/ppermute | solution.py:470
  25.0 1.1 %transform_rest.1 = (f32[2,16,2048]{2,1,0:T(8,128)S(1)}, f32[2,16,2048]{2,1,0:T(8,128)S(1)}) custom-call(f32[2,16,2048]{2,1,0:T(8,128)S(1)} %collective-permute-done.9.far_rows, f32[544,256]{1,0:T(8,128)S(1)} %get-tuple-element.36.spectrum, f32[34,128]{1,0:T(8,128)S(1)} %copy-done.6, f32[68,128]{1,0:T(8,128)S(1)} %copy-done.5, f32[51,256]{1,0:T(8,128)S(1)} %copy-done.4, ...), custom_call_target="tpu_custom_call" | custom-call | flops 2000000000 | bytes 6666666 | tf_op jit(solution)/shard_map/transform_rest/pallas_call | solution.py:498
  26.2 0.9 %last_update.1 = (f32[1,16,2048]{2,1,0:T(8,128)}, f32[2,16,2048]{2,1,0:T(8,128)}) custom-call(f32[2,16,2048]{2,1,0:T(8,128)S(1)} %get-tuple-element.30.rest, f32[3,16,2048]{2,1,0:T(8,128)S(1)} %zonal_terms.3, f32[1,16,2048]{2,1,0:T(8,128)S(1)} %get-tuple-element.34.east_smooth, f32[1,16,2048]{2,1,0:T(8,128)S(1)} %get-tuple-element.35.east_slope, ...), custom_call_target="tpu_custom_call" | custom-call | tf_op jit(solution)/shard_map/last_update/pallas_call | solution.py:498
  (21 shorter events, 0.0 us)
Async XLA Ops:
  0.6 12.3 %collective-permute-start.3 = (f32[2,16,2048]{2,1,0:T(8,128)}, f32[2,16,2048]{2,1,0:T(8,128)S(1)}, u32[]{:S(2)}, u32[]{:S(2)}) collective-permute-start(f32[2,16,2048]{2,1,0:T(8,128)} %bitcast.4), channel_id=1, source_target_pairs={{0,16},{4,20},{8,24},{12,28},{16,0},{20,4},{24,8},{28,12},{1,17},{... | collective-permute-start | bytes 786440 | tf_op jit(solution)/shard_map/ppermute | solution.py:470
  2.2 2.8 %copy-start.8 = (f32[1,16,2048]{2,1,0:T(8,128)S(1)}, f32[1,16,2048]{2,1,0:T(8,128)}, u32[]{:S(2)}) copy-start(f32[1,16,2048]{2,1,0:T(8,128)} %param.10) | copy-start | bytes 393220
  2.2 9.4 %copy-start.1 = (bf16[256,512]{1,0:T(8,128)(2,1)S(1)}, bf16[256,512]{1,0:T(8,128)(2,1)}, u32[]{:S(2)}) copy-start(bf16[256,512]{1,0:T(8,128)(2,1)} %constant.19.clone.refs_1_.refs_6_) | copy-start | bytes 786436
  2.2 9.4 %copy-start.3 = (bf16[256,256]{1,0:T(8,128)(2,1)S(1)}, bf16[256,256]{1,0:T(8,128)(2,1)}, u32[]{:S(2)}) copy-start(bf16[256,256]{1,0:T(8,128)(2,1)} %constant.17.clone.low.refs_4_) | copy-start | bytes 393220
  2.2 9.4 %copy-start.4 = (f32[51,256]{1,0:T(8,128)S(1)}, f32[51,256]{1,0:T(8,128)}, u32[]{:S(2)}) copy-start(f32[51,256]{1,0:T(8,128)} %constant.22.clone.masks.refs_2_) | copy-start | bytes 156676
  2.2 9.4 %copy-start.5 = (f32[68,128]{1,0:T(8,128)S(1)}, f32[68,128]{1,0:T(8,128)}, u32[]{:S(2)}) copy-start(f32[68,128]{1,0:T(8,128)} %constant.21.clone.refs_2_.refs_1_) | copy-start | bytes 104452
  2.2 9.4 %copy-start.6 = (f32[34,128]{1,0:T(8,128)S(1)}, f32[34,128]{1,0:T(8,128)}, u32[]{:S(2)}) copy-start(f32[34,128]{1,0:T(8,128)} %constant.20.clone.twist.refs_0_) | copy-start | bytes 52228
  3.3 8.4 %copy-start = (bf16[256,512]{1,0:T(8,128)(2,1)S(1)}, bf16[256,512]{1,0:T(8,128)(2,1)}, u32[]{:S(2)}) copy-start(bf16[256,512]{1,0:T(8,128)(2,1)} %constant.18.clone.refs_0_.refs_5_) | copy-start | bytes 786436
  3.3 8.4 %copy-start.2 = (bf16[256,256]{1,0:T(8,128)(2,1)S(1)}, bf16[256,256]{1,0:T(8,128)(2,1)}, u32[]{:S(2)}) copy-start(bf16[256,256]{1,0:T(8,128)(2,1)} %constant.16.clone.high.refs_3_) | copy-start | bytes 393220
  3.4 3.6 %collective-permute-start.1 = (f32[8,2304]{1,0:T(8,128)S(1)}, f32[8,2304]{1,0:T(8,128)S(1)}, u32[]{:S(2)}, u32[]{:S(2)}) collective-permute-start(f32[8,2304]{1,0:T(8,128)S(1)} %get-tuple-element.22), channel_id=1, source_target_pairs={{0,4},{8,12},{16,20},{24,28},{4,0},{12,8},{20,16},{28,24},{1,5},{9... | collective-permute-start | bytes 221192 | tf_op jit(solution)/shard_map/ppermute | solution.py:465
  3.5 8.8 %collective-permute-start.2 = (f32[8,2304]{1,0:T(8,128)S(1)}, f32[8,2304]{1,0:T(8,128)S(1)}, u32[]{:S(2)}, u32[]{:S(2)}) collective-permute-start(f32[8,2304]{1,0:T(8,128)S(1)} %get-tuple-element.26), channel_id=1, source_target_pairs={{4,8},{12,16},{20,24},{28,0},{8,4},{16,12},{24,20},{0,28},{5,9},{1... | collective-permute-start | bytes 221192 | tf_op jit(solution)/shard_map/ppermute | solution.py:465
  5.0 9.6 %collective-permute-start = (f32[1,16,2048]{2,1,0:T(8,128)S(1)}, f32[1,16,2048]{2,1,0:T(8,128)S(1)}, u32[]{:S(2)}, u32[]{:S(2)}) collective-permute-start(f32[1,16,2048]{2,1,0:T(8,128)S(1)} %copy-done.8), channel_id=1, source_target_pairs={{0,16},{4,20},{8,24},{12,28},{16,0},{20,4},{24,8},{28,12},{1,17},{... | collective-permute-start | bytes 393224 | tf_op jit(solution)/shard_map/ppermute | solution.py:470
  6.6 8.1 %collective-permute-start.4 = (f32[1,16,2048]{2,1,0:T(8,128)S(1)}, f32[1,16,2048]{2,1,0:T(8,128)S(1)}, u32[]{:S(2)}, u32[]{:S(2)}) collective-permute-start(f32[1,16,2048]{2,1,0:T(8,128)S(1)} %copy-done.8), channel_id=1, source_target_pairs={{0,1},{2,3},{1,0},{3,2},{4,5},{6,7},{5,4},{7,6},{8,9},{10,11},{9,8... | collective-permute-start | bytes 393224 | tf_op jit(solution)/shard_map/ppermute | solution.py:465
  7.0 7.6 %collective-permute-start.5 = (f32[1,16,2048]{2,1,0:T(8,128)S(1)}, f32[1,16,2048]{2,1,0:T(8,128)S(1)}, u32[]{:S(2)}, u32[]{:S(2)}) collective-permute-start(f32[1,16,2048]{2,1,0:T(8,128)S(1)} %copy-done.8), channel_id=1, source_target_pairs={{1,2},{2,1},{5,6},{6,5},{9,10},{10,9},{13,14},{14,13},{17,18},{18,... | collective-permute-start | bytes 393224 | tf_op jit(solution)/shard_map/ppermute | solution.py:465
  11.7 0.7 %copy-start.7 = (f32[2,2048]{1,0:T(2,128)S(1)}, f32[2,2048]{1,0:T(2,128)}, u32[]{:S(2)}) copy-start(f32[2,2048]{1,0:T(2,128)} %constant.23.clone.rows) | copy-start | bytes 49156
  14.1 9.8 %collective-permute-start.8 = (f32[1,16,2048]{2,1,0:T(8,128)S(1)}, f32[1,16,2048]{2,1,0:T(8,128)S(1)}, u32[]{:S(2)}, u32[]{:S(2)}) collective-permute-start(f32[1,16,2048]{2,1,0:T(8,128)S(1)} %get-tuple-element.29.east_next.east), channel_id=1, source_target_pairs={{0,16},{4,20},{8,24},{12,28},{16,0},{20,4},{24,8},{28,12},{1,17},{... | collective-permute-start | bytes 393224 | tf_op jit(solution)/shard_map/ppermute | solution.py:470
  15.5 9.5 %collective-permute-start.9 = (f32[2,16,2048]{2,1,0:T(8,128)S(1)}, f32[2,16,2048]{2,1,0:T(8,128)S(1)}, u32[]{:S(2)}, u32[]{:S(2)}) collective-permute-start(f32[2,16,2048]{2,1,0:T(8,128)S(1)} %get-tuple-element.30.rest), channel_id=1, source_target_pairs={{0,16},{4,20},{8,24},{12,28},{16,0},{20,4},{24,8},{28,12},{1,17},{... | collective-permute-start | bytes 786440 | tf_op jit(solution)/shard_map/ppermute | solution.py:470
  17.1 1.3 %collective-permute-start.6 = (f32[8,2304]{1,0:T(8,128)S(1)}, f32[8,2304]{1,0:T(8,128)S(1)}, u32[]{:S(2)}, u32[]{:S(2)}) collective-permute-start(f32[8,2304]{1,0:T(8,128)S(1)} %get-tuple-element.31), channel_id=1, source_target_pairs={{0,4},{8,12},{16,20},{24,28},{4,0},{12,8},{20,16},{28,24},{1,5},{9... | collective-permute-start | bytes 221192 | tf_op jit(solution)/shard_map/ppermute | solution.py:465
  17.1 5.6 %collective-permute-start.7 = (f32[8,2304]{1,0:T(8,128)S(1)}, f32[8,2304]{1,0:T(8,128)S(1)}, u32[]{:S(2)}, u32[]{:S(2)}) collective-permute-start(f32[8,2304]{1,0:T(8,128)S(1)} %get-tuple-element.32), channel_id=1, source_target_pairs={{4,8},{12,16},{20,24},{28,0},{8,4},{16,12},{24,20},{0,28},{5,9},{1... | collective-permute-start | bytes 221192 | tf_op jit(solution)/shard_map/ppermute | solution.py:465
  17.8 8.3 %collective-permute-start.10 = (f32[1,16,2048]{2,1,0:T(8,128)S(1)}, f32[1,16,2048]{2,1,0:T(8,128)S(1)}, u32[]{:S(2)}, u32[]{:S(2)}) collective-permute-start(f32[1,16,2048]{2,1,0:T(8,128)S(1)} %get-tuple-element.39), channel_id=1, source_target_pairs={{0,1},{2,3},{1,0},{3,2},{4,5},{6,7},{5,4},{7,6},{8,9},{10,11},{9,8... | collective-permute-start | bytes 393224 | tf_op jit(solution)/shard_map/ppermute | solution.py:465
  18.4 7.8 %collective-permute-start.11 = (f32[1,16,2048]{2,1,0:T(8,128)S(1)}, f32[1,16,2048]{2,1,0:T(8,128)S(1)}, u32[]{:S(2)}, u32[]{:S(2)}) collective-permute-start(f32[1,16,2048]{2,1,0:T(8,128)S(1)} %get-tuple-element.39), channel_id=1, source_target_pairs={{1,2},{2,1},{5,6},{6,5},{9,10},{10,9},{13,14},{14,13},{17,18},{18,... | collective-permute-start | bytes 393224 | tf_op jit(solution)/shard_map/ppermute | solution.py:465

commit v5 on v4

--- a/solution.py
+++ b/solution.py
@@ -400,48 +400,41 @@
             out[field, :, tile(index)] = terms[field]
 
 
-def last_kernel(
-    rest,
-    zonal_terms,
-    east_smooth,
-    east_slope,
-    rest_smooth,
-    rest_slope,
-    levels,
-    others,
-    height_out,
-    wind_out,
-    staged,
-    sems,
+def rest_kernel(
+    blocks, far_rows, spectrum, rest, zonal_terms, east_smooth, east_slope, *refs
 ):
-    tiles = rest.shape[-1] // RADIX
-    copies = []
-    for piece in range(PIECES):
-        for index in range(piece * tiles // PIECES, (piece + 1) * tiles // PIECES):
-            at = tile(index)
-            northward, thick = rest[0, :, at], rest[1, :, at]
-            north_slope, thick_slope = rest_slope[0, :, at], rest_slope[1, :, at]
-            vertical = levels[0, :, at] + others[0, :, at] - 2.0 * thick
-            tendencies = (
-                zonal_terms[0, :, at] - northward * east_slope[0, :, at],
-                zonal_terms[1, :, at] - northward * north_slope - thick_slope,
-                zonal_terms[2, :, at]
-                - northward * thick_slope
-                - thick * north_slope
-                + mixing * vertical,
-            )
-            smooths = (east_smooth[0, :, at], rest_smooth[0, :, at], rest_smooth[1, :, at])
-            for field in range(3):
-                staged[field, :, at] = smooths[field] + courant * tendencies[field]
-        span = pl.ds(piece * tiles // PIECES * RADIX, tiles // PIECES * RADIX)
-        targets = (wind_out.at[0, :, span], wind_out.at[1, :, span], height_out.at[0, :, span])
-        for field, target in enumerate(targets):
-            copies.append(
-                pltpu.make_async_copy(
-                    staged.at[field, :, span], target, sems.at[3 * piece + field]
-                )
-            )
-            copies[-1].start()
+    tables, (out, smooth, slope, *work) = refs[:7], refs[7:]
+    transform(blocks, (-1, 1), far_rows, spectrum, tables, smooth, slope, work)
+    for index in range(rest.shape[-1] // RADIX):
+        at = tile(index)
+        northward, thick = rest[0, :, at], rest[1, :, at]
+        north_slope, thick_slope = slope[0, :, at], slope[1, :, at]
+        tendencies = (
+            zonal_terms[0, :, at] - northward * east_slope[0, :, at],
+            zonal_terms[1, :, at] - northward * north_slope - thick_slope,
+            zonal_terms[2, :, at]
+            - northward * thick_slope
+            - thick * north_slope
+            - 2.0 * mixing * thick,
+        )
+        smooths = (east_smooth[0, :, at], smooth[0, :, at], smooth[1, :, at])
+        for field in range(3):
+            out[field, :, at] = smooths[field] + courant * tendencies[field]
+
+
+def last_kernel(fields, levels, others, height_out, wind_out, height, sems):
+    copies = [
+        pltpu.make_async_copy(fields.at[0], wind_out.at[0], sems.at[0]),
+        pltpu.make_async_copy(fields.at[1], wind_out.at[1], sems.at[1]),
+        pltpu.make_async_copy(height, height_out.at[0], sems.at[2]),
+    ]
+    copies[0].start()
+    copies[1].start()
+    for index in range(height.shape[-1] // RADIX):
+        at = tile(index)
+        neighbours = levels[0, :, at] + others[0, :, at]
+        height[:, at] = fields[2, :, at] + (courant * mixing) * neighbours
+    copies[2].start()
     for copy in copies:
         copy.wait()
 
@@ -591,13 +584,16 @@
         *tables,
         cost=EAST_COST,
     )
-    rest_terms = call(
-        functools.partial(transform_kernel, blocks, (-1, 1)),
-        "transform_rest",
-        [two, two],
-        working(2)[2:],
+    (fields,) = call(
+        functools.partial(rest_kernel, blocks),
+        "rest_fields",
+        [array(3, lon_count, lat_count)],
+        working(2),
         far_second,
         spectra[1],
+        rest,
+        zonal_terms,
+        *east_terms,
         *tables,
         cost=REST_COST,
     )
@@ -605,11 +601,8 @@
         last_kernel,
         "last_update",
         [one, two],
-        [scratch(3, lon_count, lat_count), pltpu.SemaphoreType.DMA((3 * PIECES,))],
-        rest,
-        zonal_terms,
-        *east_terms,
-        *rest_terms,
+        [scratch(lon_count, lat_count), pltpu.SemaphoreType.DMA((3,))],
+        fields,
         *levels,
         out_specs=anywhere(2),
     )

time: 27.3 us -> 27.3 us (level)
  no operation moved by 1% of the time
where the time goes in v5:
time: 27.3 us; the launch traced here: 27 us
  starting transfers between devices  17.2 us (63%)
  Pallas kernels  7.02 us (26%)
  other arithmetic  1.07 us (4%)
  between operations  0.88 us (3%)
  waiting for transfers between devices  0.72 us (3%)
    ppermute x8, starting transfers between devices, exchange(): return lax.ppermute(value, axis, pairs + [(j, i) for i, j in pairs])  12 us
    pallas_call x10, Pallas kernels, call(): pl.pallas_call(kernel, out_shape=outs, in_specs=in_specs or vmem(len(args...  7.02 us
    ppermute x4, starting transfers between devices, from_antipode(): lax.ppermute(value, 'lon', [(i, (i + size // 2) % size) for i in range(si...  5.26 us
    concatenate x1, other arithmetic, body(): fields = jnp.concatenate([thickness, winds], 0)  1.07 us
  transfers between devices with their start and end apart: 12, of which 2 were waited for; matrix products, arithmetic and copies ran while one was open for 4% of the time, Pallas kernels for 23%

profile of v5, /device:TPU:8, one launch (start us, length us, event | category | flops | bytes accessed | tf_op | source)
XLA Modules:
  0.0 27.0 jit_solution(13376605888084183518)
XLA Ops:
  0.6 1.6 %collective-permute-start.3 = (f32[2,16,2048]{2,1,0:T(8,128)}, f32[2,16,2048]{2,1,0:T(8,128)S(1)}, u32[]{:S(2)}, u32[]{:S(2)}) collective-permute-start(f32[2,16,2048]{2,1,0:T(8,128)} %bitcast.4), channel_id=1, source_target_pairs={{0,16},{4,20},{8,24},{12,28},{16,0},{20,4},{24,8},{28,12},{1,17},{... | collective-permute-start | bytes 786440 | tf_op jit(solution)/shard_map/ppermute | solution.py:463
  2.2 0.0 copy-start.5
  2.2 0.0 copy-start.6
  2.3 1.1 %pad_maximum_fusion.fields = f32[3,16,2048]{2,1,0:T(8,128)S(1)} fusion(f32[2,16,2048]{2,1,0:T(8,128)} %bitcast.5, f32[1,16,2048]{2,1,0:T(8,128)} %param.10), kind=kLoop, calls=%fused_computation | loop fusion | flops 98304 | bytes 786432 | tf_op jit(solution)/shard_map/concatenate | solution.py:505
  3.3 0.0 copy-start
  3.3 0.0 copy-start.2
  3.3 0.1 gather_fields.1
  3.4 0.1 collective-permute-start.1
  3.5 1.5 %collective-permute-start.2 = (f32[8,2304]{1,0:T(8,128)S(1)}, f32[8,2304]{1,0:T(8,128)S(1)}, u32[]{:S(2)}, u32[]{:S(2)}) collective-permute-start(f32[8,2304]{1,0:T(8,128)S(1)} %get-tuple-element.24), channel_id=1, source_target_pairs={{4,8},{12,16},{20,24},{28,0},{8,4},{16,12},{24,20},{0,28},{5,9},{1... | collective-permute-start | bytes 221192 | tf_op jit(solution)/shard_map/ppermute | solution.py:458
  5.0 1.5 %collective-permute-start = (f32[1,16,2048]{2,1,0:T(8,128)S(1)}, f32[1,16,2048]{2,1,0:T(8,128)S(1)}, u32[]{:S(2)}, u32[]{:S(2)}) collective-permute-start(f32[1,16,2048]{2,1,0:T(8,128)S(1)} %copy-done.8), channel_id=1, source_target_pairs={{0,16},{4,20},{8,24},{12,28},{16,0},{20,4},{24,8},{28,12},{1,17},{... | collective-permute-start | bytes 393224 | tf_op jit(solution)/shard_map/ppermute | solution.py:463
  6.6 0.4 %collective-permute-start.4 = (f32[1,16,2048]{2,1,0:T(8,128)S(1)}, f32[1,16,2048]{2,1,0:T(8,128)S(1)}, u32[]{:S(2)}, u32[]{:S(2)}) collective-permute-start(f32[1,16,2048]{2,1,0:T(8,128)S(1)} %copy-done.8), channel_id=1, source_target_pairs={{0,1},{2,3},{1,0},{3,2},{4,5},{6,7},{5,4},{7,6},{8,9},{10,11},{9,8... | collective-permute-start | bytes 393224 | tf_op jit(solution)/shard_map/ppermute | solution.py:458
  7.0 0.0 collective-permute-done.1.near
  7.0 4.6 %collective-permute-start.5 = (f32[1,16,2048]{2,1,0:T(8,128)S(1)}, f32[1,16,2048]{2,1,0:T(8,128)S(1)}, u32[]{:S(2)}, u32[]{:S(2)}) collective-permute-start(f32[1,16,2048]{2,1,0:T(8,128)S(1)} %copy-done.8), channel_id=1, source_target_pairs={{1,2},{2,1},{5,6},{6,5},{9,10},{10,9},{13,14},{14,13},{17,18},{18,... | collective-permute-start | bytes 393224 | tf_op jit(solution)/shard_map/ppermute | solution.py:458
  11.7 0.0 copy-start.7
  11.7 0.6 %own_spectra.2 = (f32[544,256]{1,0:T(8,128)S(1)}, f32[272,256]{1,0:T(8,128)S(1)}) custom-call(f32[8,2304]{1,0:T(8,128)S(1)} %collective-permute-done.1.near, f32[1,16,2048]{2,1,0:T(8,128)S(1)} %get-tuple-element.21.east, f32[2,16,2048]{2,1,0:T(8,128)S(1)} %get-tuple-element.22.rest, f32[34,128]{1,0:T(8,128)S(1)} %copy-done.6, f32[51,256]{1,0:T(8,128)S(1)} %copy-done.4, ...), custom_call_target="tpu_custom_call" | custom-call | tf_op jit(solution)/shard_map/own_spectra/pallas_call | solution.py:491
  12.4 0.1 copy-done.7
  12.4 0.5 %zonal_terms.2 = f32[3,16,2048]{2,1,0:T(8,128)S(1)} custom-call(f32[1,16,2048]{2,1,0:T(8,128)S(1)} %get-tuple-element.21.east, f32[2,16,2048]{2,1,0:T(8,128)S(1)} %get-tuple-element.22.rest, f32[8,2304]{1,0:T(8,128)S(1)} %collective-permute-done.1.near, f32[8,2304]{1,0:T(8,128)S(1)} %collective-permute-done.2.far, f32[2,2048]{1,0:T(2,128)S(1)} %copy-done.7), custom_call_target="tpu_custom_call" | custom-call | flops 2000000000 | bytes 6666666 | tf_op jit(solution)/shard_map/zonal_terms/pallas_call | solution.py:491
  12.9 1.2 %eastward_wind.1 = (f32[1,16,2048]{2,1,0:T(8,128)S(1)}, f32[2,16,2048]{2,1,0:T(8,128)S(1)}) custom-call(f32[2,16,2048]{2,1,0:T(8,128)S(1)} %collective-permute-done.3.far_rows, f32[544,256]{1,0:T(8,128)S(1)} %get-tuple-element.25.spectrum, f32[1,16,2048]{2,1,0:T(8,128)S(1)} %get-tuple-element.21.east, f32[2,16,2048]{2,1,0:T(8,128)S(1)} %get-tuple-element.22.rest, ...), custom_call_target="tpu_custom_call" | custom-call | flops 2000000000 | bytes 6666666 | tf_op jit(solution)/shard_map/eastward_wind/pallas_call | solution.py:491
  14.1 0.6 %collective-permute-start.9 = (f32[1,16,2048]{2,1,0:T(8,128)S(1)}, f32[1,16,2048]{2,1,0:T(8,128)S(1)}, u32[]{:S(2)}, u32[]{:S(2)}) collective-permute-start(f32[1,16,2048]{2,1,0:T(8,128)S(1)} %get-tuple-element.27.east_next.east), channel_id=1, source_target_pairs={{0,16},{4,20},{8,24},{12,28},{16,0},{20,4},{24,8},{28,12},{1,17},{... | collective-permute-start | bytes 393224 | tf_op jit(solution)/shard_map/ppermute | solution.py:463
  14.6 0.0 collective-permute-done.far_rows
  14.7 0.9 %north_and_height.1 = (f32[2,16,2048]{2,1,0:T(8,128)S(1)}, f32[1,16,2048]{2,1,0:T(8,128)S(1)}, f32[8,2304]{1,0:T(8,128)S(1)}, f32[8,2304]{1,0:T(8,128)S(1)}) custom-call(f32[1,16,2048]{2,1,0:T(8,128)S(1)} %collective-permute-done.far_rows, f32[272,256]{1,0:T(8,128)S(1)} %get-tuple-element.23.spectrum, f32[2,16,2048]{2,1,0:T(8,128)S(1)} %get-tuple-element.22.rest, ...), custom_call_target="tpu_custom_call" | custom-call | flops 2000000000 | bytes 6666666 | tf_op jit(solution)/shard_map/north_and_height/pallas_call | solution.py:491
  15.5 1.6 %collective-permute-start.6 = (f32[2,16,2048]{2,1,0:T(8,128)S(1)}, f32[2,16,2048]{2,1,0:T(8,128)S(1)}, u32[]{:S(2)}, u32[]{:S(2)}) collective-permute-start(f32[2,16,2048]{2,1,0:T(8,128)S(1)} %get-tuple-element.28.rest), channel_id=1, source_target_pairs={{0,16},{4,20},{8,24},{12,28},{16,0},{20,4},{24,8},{28,12},{1,17},{... | collective-permute-start | bytes 786440 | tf_op jit(solution)/shard_map/ppermute | solution.py:463
  17.1 0.7 %collective-permute-start.8 = (f32[8,2304]{1,0:T(8,128)S(1)}, f32[8,2304]{1,0:T(8,128)S(1)}, u32[]{:S(2)}, u32[]{:S(2)}) collective-permute-start(f32[8,2304]{1,0:T(8,128)S(1)} %get-tuple-element.31), channel_id=1, source_target_pairs={{4,8},{12,16},{20,24},{28,0},{8,4},{16,12},{24,20},{0,28},{5,9},{1... | collective-permute-start | bytes 221192 | tf_op jit(solution)/shard_map/ppermute | solution.py:458
  17.8 0.3 %collective-permute-start.10 = (f32[1,16,2048]{2,1,0:T(8,128)S(1)}, f32[1,16,2048]{2,1,0:T(8,128)S(1)}, u32[]{:S(2)}, u32[]{:S(2)}) collective-permute-start(f32[1,16,2048]{2,1,0:T(8,128)S(1)} %get-tuple-element.35), channel_id=1, source_target_pairs={{0,1},{2,3},{1,0},{3,2},{4,5},{6,7},{5,4},{7,6},{8,9},{10,11},{9,8... | collective-permute-start | bytes 393224 | tf_op jit(solution)/shard_map/ppermute | solution.py:458
  18.1 0.3 %collective-permute-done.7.near = f32[8,2304]{1,0:T(8,128)S(1)} collective-permute-done((f32[8,2304]{1,0:T(8,128)S(1)}, f32[8,2304]{1,0:T(8,128)S(1)}, u32[]{:S(2)}, u32[]{:S(2)}) %collective-permute-start.7) | collective-permute-done | bytes 73760 | tf_op jit(solution)/shard_map/ppermute | solution.py:458
  18.4 4.3 %collective-permute-start.11 = (f32[1,16,2048]{2,1,0:T(8,128)S(1)}, f32[1,16,2048]{2,1,0:T(8,128)S(1)}, u32[]{:S(2)}, u32[]{:S(2)}) collective-permute-start(f32[1,16,2048]{2,1,0:T(8,128)S(1)} %get-tuple-element.35), channel_id=1, source_target_pairs={{1,2},{2,1},{5,6},{6,5},{9,10},{10,9},{13,14},{14,13},{17,18},{18,... | collective-permute-start | bytes 393224 | tf_op jit(solution)/shard_map/ppermute | solution.py:458
  22.7 0.5 %zonal_terms.3 = f32[3,16,2048]{2,1,0:T(8,128)S(1)} custom-call(f32[1,16,2048]{2,1,0:T(8,128)S(1)} %get-tuple-element.27.east_next.east, f32[2,16,2048]{2,1,0:T(8,128)S(1)} %get-tuple-element.28.rest, f32[8,2304]{1,0:T(8,128)S(1)} %collective-permute-done.7.near, f32[8,2304]{1,0:T(8,128)S(1)} %collective-permute-done.8.far, f32[2,2048]{1,0:T(2,128)S(1)} %copy-done.7), custom_call_target="tpu_custom_call" | custom-call | flops 1 | tf_op jit(solution)/shard_map/zonal_terms/pallas_call | solution.py:491
  23.2 0.6 %own_spectra.3 = (f32[272,256]{1,0:T(8,128)S(1)}, f32[544,256]{1,0:T(8,128)S(1)}) custom-call(f32[8,2304]{1,0:T(8,128)S(1)} %collective-permute-done.7.near, f32[1,16,2048]{2,1,0:T(8,128)S(1)} %get-tuple-element.27.east_next.east, f32[2,16,2048]{2,1,0:T(8,128)S(1)} %get-tuple-element.28.rest, f32[34,128]{1,0:T(8,128)S(1)} %copy-done.6, ...), custom_call_target="tpu_custom_call" | custom-call | tf_op jit(solution)/shard_map/own_spectra/pallas_call | solution.py:491
  23.8 0.7 %transform_east.1 = (f32[1,16,2048]{2,1,0:T(8,128)S(1)}, f32[1,16,2048]{2,1,0:T(8,128)S(1)}) custom-call(f32[1,16,2048]{2,1,0:T(8,128)S(1)} %collective-permute-done.9.far_rows, f32[272,256]{1,0:T(8,128)S(1)} %get-tuple-element.32.spectrum, f32[34,128]{1,0:T(8,128)S(1)} %copy-done.6, f32[68,128]{1,0:T(8,128)S(1)} %copy-done.5, f32[51,256]{1,0:T(8,128)S(1)} %copy-done.4, ...), custom_call_target="tpu_custom_call" | custom-call | flops 2000000000 | bytes 6666666 | tf_op jit(solution)/shard_map/transform_east/pallas_call | solution.py:491
  24.6 0.4 %collective-permute-done.6.far_rows = f32[2,16,2048]{2,1,0:T(8,128)S(1)} collective-permute-done((f32[2,16,2048]{2,1,0:T(8,128)S(1)}, f32[2,16,2048]{2,1,0:T(8,128)S(1)}, u32[]{:S(2)}, u32[]{:S(2)}) %collective-permute-start.6) | collective-permute-done | bytes 262176 | tf_op jit(solution)/shard_map/ppermute | solution.py:463
  25.0 1.2 %rest_fields.1.fields = f32[3,16,2048]{2,1,0:T(8,128)S(1)} custom-call(f32[2,16,2048]{2,1,0:T(8,128)S(1)} %collective-permute-done.6.far_rows, f32[544,256]{1,0:T(8,128)S(1)} %get-tuple-element.30.spectrum, f32[2,16,2048]{2,1,0:T(8,128)S(1)} %get-tuple-element.28.rest, f32[3,16,2048]{2,1,0:T(8,128)S(1)} %zonal_terms.3, ...), custom_call_target="tpu_custom_call" | custom-call | flops 2000000000 | bytes 6666666 | tf_op jit(solution)/shard_map/rest_fields/pallas_call | solution.py:491
  26.3 0.8 %last_update.1 = (f32[1,16,2048]{2,1,0:T(8,128)}, f32[2,16,2048]{2,1,0:T(8,128)}) custom-call(f32[3,16,2048]{2,1,0:T(8,128)S(1)} %rest_fields.1.fields, f32[1,16,2048]{2,1,0:T(8,128)S(1)} %collective-permute-done.10.levels, f32[1,16,2048]{2,1,0:T(8,128)S(1)} %collective-permute-done.11.others), custom_call_target="tpu_custom_call" | custom-call | tf_op jit(solution)/shard_map/last_update/pallas_call | solution.py:491
  (21 shorter events, 0.0 us)
Async XLA Ops:
  0.6 12.3 %collective-permute-start.3 = (f32[2,16,2048]{2,1,0:T(8,128)}, f32[2,16,2048]{2,1,0:T(8,128)S(1)}, u32[]{:S(2)}, u32[]{:S(2)}) collective-permute-start(f32[2,16,2048]{2,1,0:T(8,128)} %bitcast.4), channel_id=1, source_target_pairs={{0,16},{4,20},{8,24},{12,28},{16,0},{20,4},{24,8},{28,12},{1,17},{... | collective-permute-start | bytes 786440 | tf_op jit(solution)/shard_map/ppermute | solution.py:463
  2.2 2.8 %copy-start.8 = (f32[1,16,2048]{2,1,0:T(8,128)S(1)}, f32[1,16,2048]{2,1,0:T(8,128)}, u32[]{:S(2)}) copy-start(f32[1,16,2048]{2,1,0:T(8,128)} %param.10) | copy-start | bytes 393220
  2.2 9.4 %copy-start.1 = (bf16[256,512]{1,0:T(8,128)(2,1)S(1)}, bf16[256,512]{1,0:T(8,128)(2,1)}, u32[]{:S(2)}) copy-start(bf16[256,512]{1,0:T(8,128)(2,1)} %constant.19.clone.refs_1_.refs_6_) | copy-start | bytes 786436
  2.2 9.4 %copy-start.3 = (bf16[256,256]{1,0:T(8,128)(2,1)S(1)}, bf16[256,256]{1,0:T(8,128)(2,1)}, u32[]{:S(2)}) copy-start(bf16[256,256]{1,0:T(8,128)(2,1)} %constant.17.clone.low.refs_4_) | copy-start | bytes 393220
  2.2 9.4 %copy-start.4 = (f32[51,256]{1,0:T(8,128)S(1)}, f32[51,256]{1,0:T(8,128)}, u32[]{:S(2)}) copy-start(f32[51,256]{1,0:T(8,128)} %constant.22.clone.masks.refs_2_) | copy-start | bytes 156676
  2.2 9.4 %copy-start.5 = (f32[68,128]{1,0:T(8,128)S(1)}, f32[68,128]{1,0:T(8,128)}, u32[]{:S(2)}) copy-start(f32[68,128]{1,0:T(8,128)} %constant.21.clone.refs_2_.refs_1_) | copy-start | bytes 104452
  2.2 9.4 %copy-start.6 = (f32[34,128]{1,0:T(8,128)S(1)}, f32[34,128]{1,0:T(8,128)}, u32[]{:S(2)}) copy-start(f32[34,128]{1,0:T(8,128)} %constant.20.clone.twist.refs_0_) | copy-start | bytes 52228
  3.3 8.4 %copy-start = (bf16[256,512]{1,0:T(8,128)(2,1)S(1)}, bf16[256,512]{1,0:T(8,128)(2,1)}, u32[]{:S(2)}) copy-start(bf16[256,512]{1,0:T(8,128)(2,1)} %constant.18.clone.refs_0_.refs_5_) | copy-start | bytes 786436
  3.3 8.4 %copy-start.2 = (bf16[256,256]{1,0:T(8,128)(2,1)S(1)}, bf16[256,256]{1,0:T(8,128)(2,1)}, u32[]{:S(2)}) copy-start(bf16[256,256]{1,0:T(8,128)(2,1)} %constant.16.clone.high.refs_3_) | copy-start | bytes 393220
  3.4 3.6 %collective-permute-start.1 = (f32[8,2304]{1,0:T(8,128)S(1)}, f32[8,2304]{1,0:T(8,128)S(1)}, u32[]{:S(2)}, u32[]{:S(2)}) collective-permute-start(f32[8,2304]{1,0:T(8,128)S(1)} %get-tuple-element.20), channel_id=1, source_target_pairs={{0,4},{8,12},{16,20},{24,28},{4,0},{12,8},{20,16},{28,24},{1,5},{9... | collective-permute-start | bytes 221192 | tf_op jit(solution)/shard_map/ppermute | solution.py:458
  3.5 8.8 %collective-permute-start.2 = (f32[8,2304]{1,0:T(8,128)S(1)}, f32[8,2304]{1,0:T(8,128)S(1)}, u32[]{:S(2)}, u32[]{:S(2)}) collective-permute-start(f32[8,2304]{1,0:T(8,128)S(1)} %get-tuple-element.24), channel_id=1, source_target_pairs={{4,8},{12,16},{20,24},{28,0},{8,4},{16,12},{24,20},{0,28},{5,9},{1... | collective-permute-start | bytes 221192 | tf_op jit(solution)/shard_map/ppermute | solution.py:458
  5.0 9.6 %collective-permute-start = (f32[1,16,2048]{2,1,0:T(8,128)S(1)}, f32[1,16,2048]{2,1,0:T(8,128)S(1)}, u32[]{:S(2)}, u32[]{:S(2)}) collective-permute-start(f32[1,16,2048]{2,1,0:T(8,128)S(1)} %copy-done.8), channel_id=1, source_target_pairs={{0,16},{4,20},{8,24},{12,28},{16,0},{20,4},{24,8},{28,12},{1,17},{... | collective-permute-start | bytes 393224 | tf_op jit(solution)/shard_map/ppermute | solution.py:463
  6.6 8.1 %collective-permute-start.4 = (f32[1,16,2048]{2,1,0:T(8,128)S(1)}, f32[1,16,2048]{2,1,0:T(8,128)S(1)}, u32[]{:S(2)}, u32[]{:S(2)}) collective-permute-start(f32[1,16,2048]{2,1,0:T(8,128)S(1)} %copy-done.8), channel_id=1, source_target_pairs={{0,1},{2,3},{1,0},{3,2},{4,5},{6,7},{5,4},{7,6},{8,9},{10,11},{9,8... | collective-permute-start | bytes 393224 | tf_op jit(solution)/shard_map/ppermute | solution.py:458
  7.0 7.6 %collective-permute-start.5 = (f32[1,16,2048]{2,1,0:T(8,128)S(1)}, f32[1,16,2048]{2,1,0:T(8,128)S(1)}, u32[]{:S(2)}, u32[]{:S(2)}) collective-permute-start(f32[1,16,2048]{2,1,0:T(8,128)S(1)} %copy-done.8), channel_id=1, source_target_pairs={{1,2},{2,1},{5,6},{6,5},{9,10},{10,9},{13,14},{14,13},{17,18},{18,... | collective-permute-start | bytes 393224 | tf_op jit(solution)/shard_map/ppermute | solution.py:458
  11.7 0.7 %copy-start.7 = (f32[2,2048]{1,0:T(2,128)S(1)}, f32[2,2048]{1,0:T(2,128)}, u32[]{:S(2)}) copy-start(f32[2,2048]{1,0:T(2,128)} %constant.23.clone.rows) | copy-start | bytes 49156
  14.1 9.8 %collective-permute-start.9 = (f32[1,16,2048]{2,1,0:T(8,128)S(1)}, f32[1,16,2048]{2,1,0:T(8,128)S(1)}, u32[]{:S(2)}, u32[]{:S(2)}) collective-permute-start(f32[1,16,2048]{2,1,0:T(8,128)S(1)} %get-tuple-element.27.east_next.east), channel_id=1, source_target_pairs={{0,16},{4,20},{8,24},{12,28},{16,0},{20,4},{24,8},{28,12},{1,17},{... | collective-permute-start | bytes 393224 | tf_op jit(solution)/shard_map/ppermute | solution.py:463
  15.5 9.5 %collective-permute-start.6 = (f32[2,16,2048]{2,1,0:T(8,128)S(1)}, f32[2,16,2048]{2,1,0:T(8,128)S(1)}, u32[]{:S(2)}, u32[]{:S(2)}) collective-permute-start(f32[2,16,2048]{2,1,0:T(8,128)S(1)} %get-tuple-element.28.rest), channel_id=1, source_target_pairs={{0,16},{4,20},{8,24},{12,28},{16,0},{20,4},{24,8},{28,12},{1,17},{... | collective-permute-start | bytes 786440 | tf_op jit(solution)/shard_map/ppermute | solution.py:463
  17.1 1.3 %collective-permute-start.7 = (f32[8,2304]{1,0:T(8,128)S(1)}, f32[8,2304]{1,0:T(8,128)S(1)}, u32[]{:S(2)}, u32[]{:S(2)}) collective-permute-start(f32[8,2304]{1,0:T(8,128)S(1)} %get-tuple-element.29), channel_id=1, source_target_pairs={{0,4},{8,12},{16,20},{24,28},{4,0},{12,8},{20,16},{28,24},{1,5},{9... | collective-permute-start | bytes 221192 | tf_op jit(solution)/shard_map/ppermute | solution.py:458
  17.1 5.6 %collective-permute-start.8 = (f32[8,2304]{1,0:T(8,128)S(1)}, f32[8,2304]{1,0:T(8,128)S(1)}, u32[]{:S(2)}, u32[]{:S(2)}) collective-permute-start(f32[8,2304]{1,0:T(8,128)S(1)} %get-tuple-element.31), channel_id=1, source_target_pairs={{4,8},{12,16},{20,24},{28,0},{8,4},{16,12},{24,20},{0,28},{5,9},{1... | collective-permute-start | bytes 221192 | tf_op jit(solution)/shard_map/ppermute | solution.py:458
  17.8 8.4 %collective-permute-start.10 = (f32[1,16,2048]{2,1,0:T(8,128)S(1)}, f32[1,16,2048]{2,1,0:T(8,128)S(1)}, u32[]{:S(2)}, u32[]{:S(2)}) collective-permute-start(f32[1,16,2048]{2,1,0:T(8,128)S(1)} %get-tuple-element.35), channel_id=1, source_target_pairs={{0,1},{2,3},{1,0},{3,2},{4,5},{6,7},{5,4},{7,6},{8,9},{10,11},{9,8... | collective-permute-start | bytes 393224 | tf_op jit(solution)/shard_map/ppermute | solution.py:458
  18.4 7.9 %collective-permute-start.11 = (f32[1,16,2048]{2,1,0:T(8,128)S(1)}, f32[1,16,2048]{2,1,0:T(8,128)S(1)}, u32[]{:S(2)}, u32[]{:S(2)}) collective-permute-start(f32[1,16,2048]{2,1,0:T(8,128)S(1)} %get-tuple-element.35), channel_id=1, source_target_pairs={{1,2},{2,1},{5,6},{6,5},{9,10},{10,9},{13,14},{14,13},{17,18},{18,... | collective-permute-start | bytes 393224 | tf_op jit(solution)/shard_map/ppermute | solution.py:458

commit v6 on v5

--- a/solution.py
+++ b/solution.py
@@ -20,8 +20,8 @@
 ROWS = 8
 FIRST_COST = 2_000_000_000
 SECOND_COST = 2_000_000_000
-EAST_COST = 2_000_000_000
-REST_COST = 2_000_000_000
+EAST_COST = 1_500_000_000
+REST_COST = 2_500_000_000
 ZONAL_COST = 2000000000
 LATE_ZONAL_COST = 1
 PIECES = 4

time: 27.3 us -> 27.3 us (level)
  no operation moved by 1% of the time
where the time goes in v6:
time: 27.3 us; the launch traced here: 27 us
  starting transfers between devices  17.2 us (63%)
  Pallas kernels  7.02 us (26%)
  other arithmetic  1.07 us (4%)
  between operations  0.88 us (3%)
  waiting for transfers between devices  0.72 us (3%)
    ppermute x8, starting transfers between devices, exchange(): return lax.ppermute(value, axis, pairs + [(j, i) for i, j in pairs])  12 us
    pallas_call x10, Pallas kernels, call(): pl.pallas_call(kernel, out_shape=outs, in_specs=in_specs or vmem(len(args...  7.02 us
    ppermute x4, starting transfers between devices, from_antipode(): lax.ppermute(value, 'lon', [(i, (i + size // 2) % size) for i in range(si...  5.26 us
    concatenate x1, other arithmetic, body(): fields = jnp.concatenate([thickness, winds], 0)  1.07 us
  transfers between devices with their start and end apart: 12, of which 2 were waited for; matrix products, arithmetic and copies ran while one was open for 4% of the time, Pallas kernels for 23%

profile of v6, /device:TPU:8, one launch (start us, length us, event | category | flops | bytes accessed | tf_op | source)
XLA Modules:
  0.0 27.0 jit_solution(13376605888084183518)
XLA Ops:
  0.6 1.6 %collective-permute-start.3 = (f32[2,16,2048]{2,1,0:T(8,128)}, f32[2,16,2048]{2,1,0:T(8,128)S(1)}, u32[]{:S(2)}, u32[]{:S(2)}) collective-permute-start(f32[2,16,2048]{2,1,0:T(8,128)} %bitcast.4), channel_id=1, source_target_pairs={{0,16},{4,20},{8,24},{12,28},{16,0},{20,4},{24,8},{28,12},{1,17},{... | collective-permute-start | bytes 786440 | tf_op jit(solution)/shard_map/ppermute | solution.py:463
  2.2 0.0 copy-start.5
  2.2 0.0 copy-start.6
  2.3 1.1 %pad_maximum_fusion.fields = f32[3,16,2048]{2,1,0:T(8,128)S(1)} fusion(f32[2,16,2048]{2,1,0:T(8,128)} %bitcast.5, f32[1,16,2048]{2,1,0:T(8,128)} %param.10), kind=kLoop, calls=%fused_computation | loop fusion | flops 98304 | bytes 786432 | tf_op jit(solution)/shard_map/concatenate | solution.py:505
  3.3 0.0 copy-start
  3.3 0.0 copy-start.2
  3.3 0.1 gather_fields.1
  3.4 0.1 collective-permute-start.1
  3.5 1.5 %collective-permute-start.2 = (f32[8,2304]{1,0:T(8,128)S(1)}, f32[8,2304]{1,0:T(8,128)S(1)}, u32[]{:S(2)}, u32[]{:S(2)}) collective-permute-start(f32[8,2304]{1,0:T(8,128)S(1)} %get-tuple-element.24), channel_id=1, source_target_pairs={{4,8},{12,16},{20,24},{28,0},{8,4},{16,12},{24,20},{0,28},{5,9},{1... | collective-permute-start | bytes 221192 | tf_op jit(solution)/shard_map/ppermute | solution.py:458
  5.0 1.5 %collective-permute-start = (f32[1,16,2048]{2,1,0:T(8,128)S(1)}, f32[1,16,2048]{2,1,0:T(8,128)S(1)}, u32[]{:S(2)}, u32[]{:S(2)}) collective-permute-start(f32[1,16,2048]{2,1,0:T(8,128)S(1)} %copy-done.8), channel_id=1, source_target_pairs={{0,16},{4,20},{8,24},{12,28},{16,0},{20,4},{24,8},{28,12},{1,17},{... | collective-permute-start | bytes 393224 | tf_op jit(solution)/shard_map/ppermute | solution.py:463
  6.6 0.4 %collective-permute-start.4 = (f32[1,16,2048]{2,1,0:T(8,128)S(1)}, f32[1,16,2048]{2,1,0:T(8,128)S(1)}, u32[]{:S(2)}, u32[]{:S(2)}) collective-permute-start(f32[1,16,2048]{2,1,0:T(8,128)S(1)} %copy-done.8), channel_id=1, source_target_pairs={{0,1},{2,3},{1,0},{3,2},{4,5},{6,7},{5,4},{7,6},{8,9},{10,11},{9,8... | collective-permute-start | bytes 393224 | tf_op jit(solution)/shard_map/ppermute | solution.py:458
  7.0 0.0 collective-permute-done.1.near
  7.0 4.6 %collective-permute-start.5 = (f32[1,16,2048]{2,1,0:T(8,128)S(1)}, f32[1,16,2048]{2,1,0:T(8,128)S(1)}, u32[]{:S(2)}, u32[]{:S(2)}) collective-permute-start(f32[1,16,2048]{2,1,0:T(8,128)S(1)} %copy-done.8), channel_id=1, source_target_pairs={{1,2},{2,1},{5,6},{6,5},{9,10},{10,9},{13,14},{14,13},{17,18},{18,... | collective-permute-start | bytes 393224 | tf_op jit(solution)/shard_map/ppermute | solution.py:458
  11.7 0.0 copy-start.7
  11.7 0.6 %own_spectra.2 = (f32[544,256]{1,0:T(8,128)S(1)}, f32[272,256]{1,0:T(8,128)S(1)}) custom-call(f32[8,2304]{1,0:T(8,128)S(1)} %collective-permute-done.1.near, f32[1,16,2048]{2,1,0:T(8,128)S(1)} %get-tuple-element.21.east, f32[2,16,2048]{2,1,0:T(8,128)S(1)} %get-tuple-element.22.rest, f32[34,128]{1,0:T(8,128)S(1)} %copy-done.6, f32[51,256]{1,0:T(8,128)S(1)} %copy-done.4, ...), custom_call_target="tpu_custom_call" | custom-call | tf_op jit(solution)/shard_map/own_spectra/pallas_call | solution.py:491
  12.4 0.1 copy-done.7
  12.4 0.5 %zonal_terms.2 = f32[3,16,2048]{2,1,0:T(8,128)S(1)} custom-call(f32[1,16,2048]{2,1,0:T(8,128)S(1)} %get-tuple-element.21.east, f32[2,16,2048]{2,1,0:T(8,128)S(1)} %get-tuple-element.22.rest, f32[8,2304]{1,0:T(8,128)S(1)} %collective-permute-done.1.near, f32[8,2304]{1,0:T(8,128)S(1)} %collective-permute-done.2.far, f32[2,2048]{1,0:T(2,128)S(1)} %copy-done.7), custom_call_target="tpu_custom_call" | custom-call | flops 2000000000 | bytes 6666666 | tf_op jit(solution)/shard_map/zonal_terms/pallas_call | solution.py:491
  12.9 1.2 %eastward_wind.1 = (f32[1,16,2048]{2,1,0:T(8,128)S(1)}, f32[2,16,2048]{2,1,0:T(8,128)S(1)}) custom-call(f32[2,16,2048]{2,1,0:T(8,128)S(1)} %collective-permute-done.3.far_rows, f32[544,256]{1,0:T(8,128)S(1)} %get-tuple-element.25.spectrum, f32[1,16,2048]{2,1,0:T(8,128)S(1)} %get-tuple-element.21.east, f32[2,16,2048]{2,1,0:T(8,128)S(1)} %get-tuple-element.22.rest, ...), custom_call_target="tpu_custom_call" | custom-call | flops 2000000000 | bytes 6666666 | tf_op jit(solution)/shard_map/eastward_wind/pallas_call | solution.py:491
  14.1 0.6 %collective-permute-start.9 = (f32[1,16,2048]{2,1,0:T(8,128)S(1)}, f32[1,16,2048]{2,1,0:T(8,128)S(1)}, u32[]{:S(2)}, u32[]{:S(2)}) collective-permute-start(f32[1,16,2048]{2,1,0:T(8,128)S(1)} %get-tuple-element.27.east_next.east), channel_id=1, source_target_pairs={{0,16},{4,20},{8,24},{12,28},{16,0},{20,4},{24,8},{28,12},{1,17},{... | collective-permute-start | bytes 393224 | tf_op jit(solution)/shard_map/ppermute | solution.py:463
  14.6 0.0 collective-permute-done.far_rows
  14.7 0.9 %north_and_height.1 = (f32[2,16,2048]{2,1,0:T(8,128)S(1)}, f32[1,16,2048]{2,1,0:T(8,128)S(1)}, f32[8,2304]{1,0:T(8,128)S(1)}, f32[8,2304]{1,0:T(8,128)S(1)}) custom-call(f32[1,16,2048]{2,1,0:T(8,128)S(1)} %collective-permute-done.far_rows, f32[272,256]{1,0:T(8,128)S(1)} %get-tuple-element.23.spectrum, f32[2,16,2048]{2,1,0:T(8,128)S(1)} %get-tuple-element.22.rest, ...), custom_call_target="tpu_custom_call" | custom-call | flops 2000000000 | bytes 6666666 | tf_op jit(solution)/shard_map/north_and_height/pallas_call | solution.py:491
  15.5 1.6 %collective-permute-start.6 = (f32[2,16,2048]{2,1,0:T(8,128)S(1)}, f32[2,16,2048]{2,1,0:T(8,128)S(1)}, u32[]{:S(2)}, u32[]{:S(2)}) collective-permute-start(f32[2,16,2048]{2,1,0:T(8,128)S(1)} %get-tuple-element.28.rest), channel_id=1, source_target_pairs={{0,16},{4,20},{8,24},{12,28},{16,0},{20,4},{24,8},{28,12},{1,17},{... | collective-permute-start | bytes 786440 | tf_op jit(solution)/shard_map/ppermute | solution.py:463
  17.1 0.7 %collective-permute-start.8 = (f32[8,2304]{1,0:T(8,128)S(1)}, f32[8,2304]{1,0:T(8,128)S(1)}, u32[]{:S(2)}, u32[]{:S(2)}) collective-permute-start(f32[8,2304]{1,0:T(8,128)S(1)} %get-tuple-element.31), channel_id=1, source_target_pairs={{4,8},{12,16},{20,24},{28,0},{8,4},{16,12},{24,20},{0,28},{5,9},{1... | collective-permute-start | bytes 221192 | tf_op jit(solution)/shard_map/ppermute | solution.py:458
  17.8 0.3 %collective-permute-start.10 = (f32[1,16,2048]{2,1,0:T(8,128)S(1)}, f32[1,16,2048]{2,1,0:T(8,128)S(1)}, u32[]{:S(2)}, u32[]{:S(2)}) collective-permute-start(f32[1,16,2048]{2,1,0:T(8,128)S(1)} %get-tuple-element.35), channel_id=1, source_target_pairs={{0,1},{2,3},{1,0},{3,2},{4,5},{6,7},{5,4},{7,6},{8,9},{10,11},{9,8... | collective-permute-start | bytes 393224 | tf_op jit(solution)/shard_map/ppermute | solution.py:458
  18.1 0.3 %collective-permute-done.7.near = f32[8,2304]{1,0:T(8,128)S(1)} collective-permute-done((f32[8,2304]{1,0:T(8,128)S(1)}, f32[8,2304]{1,0:T(8,128)S(1)}, u32[]{:S(2)}, u32[]{:S(2)}) %collective-permute-start.7) | collective-permute-done | bytes 73760 | tf_op jit(solution)/shard_map/ppermute | solution.py:458
  18.4 4.3 %collective-permute-start.11 = (f32[1,16,2048]{2,1,0:T(8,128)S(1)}, f32[1,16,2048]{2,1,0:T(8,128)S(1)}, u32[]{:S(2)}, u32[]{:S(2)}) collective-permute-start(f32[1,16,2048]{2,1,0:T(8,128)S(1)} %get-tuple-element.35), channel_id=1, source_target_pairs={{1,2},{2,1},{5,6},{6,5},{9,10},{10,9},{13,14},{14,13},{17,18},{18,... | collective-permute-start | bytes 393224 | tf_op jit(solution)/shard_map/ppermute | solution.py:458
  22.7 0.5 %zonal_terms.3 = f32[3,16,2048]{2,1,0:T(8,128)S(1)} custom-call(f32[1,16,2048]{2,1,0:T(8,128)S(1)} %get-tuple-element.27.east_next.east, f32[2,16,2048]{2,1,0:T(8,128)S(1)} %get-tuple-element.28.rest, f32[8,2304]{1,0:T(8,128)S(1)} %collective-permute-done.7.near, f32[8,2304]{1,0:T(8,128)S(1)} %collective-permute-done.8.far, f32[2,2048]{1,0:T(2,128)S(1)} %copy-done.7), custom_call_target="tpu_custom_call" | custom-call | flops 1 | tf_op jit(solution)/shard_map/zonal_terms/pallas_call | solution.py:491
  23.2 0.6 %own_spectra.3 = (f32[272,256]{1,0:T(8,128)S(1)}, f32[544,256]{1,0:T(8,128)S(1)}) custom-call(f32[8,2304]{1,0:T(8,128)S(1)} %collective-permute-done.7.near, f32[1,16,2048]{2,1,0:T(8,128)S(1)} %get-tuple-element.27.east_next.east, f32[2,16,2048]{2,1,0:T(8,128)S(1)} %get-tuple-element.28.rest, f32[34,128]{1,0:T(8,128)S(1)} %copy-done.6, ...), custom_call_target="tpu_custom_call" | custom-call | tf_op jit(solution)/shard_map/own_spectra/pallas_call | solution.py:491
  23.8 0.7 %transform_east.1 = (f32[1,16,2048]{2,1,0:T(8,128)S(1)}, f32[1,16,2048]{2,1,0:T(8,128)S(1)}) custom-call(f32[1,16,2048]{2,1,0:T(8,128)S(1)} %collective-permute-done.9.far_rows, f32[272,256]{1,0:T(8,128)S(1)} %get-tuple-element.32.spectrum, f32[34,128]{1,0:T(8,128)S(1)} %copy-done.6, f32[68,128]{1,0:T(8,128)S(1)} %copy-done.5, f32[51,256]{1,0:T(8,128)S(1)} %copy-done.4, ...), custom_call_target="tpu_custom_call" | custom-call | flops 1500000000 | bytes 5000000 | tf_op jit(solution)/shard_map/transform_east/pallas_call | solution.py:491
  24.6 0.4 %collective-permute-done.6.far_rows = f32[2,16,2048]{2,1,0:T(8,128)S(1)} collective-permute-done((f32[2,16,2048]{2,1,0:T(8,128)S(1)}, f32[2,16,2048]{2,1,0:T(8,128)S(1)}, u32[]{:S(2)}, u32[]{:S(2)}) %collective-permute-start.6) | collective-permute-done | bytes 262176 | tf_op jit(solution)/shard_map/ppermute | solution.py:463
  25.0 1.2 %rest_fields.1.fields = f32[3,16,2048]{2,1,0:T(8,128)S(1)} custom-call(f32[2,16,2048]{2,1,0:T(8,128)S(1)} %collective-permute-done.6.far_rows, f32[544,256]{1,0:T(8,128)S(1)} %get-tuple-element.30.spectrum, f32[2,16,2048]{2,1,0:T(8,128)S(1)} %get-tuple-element.28.rest, f32[3,16,2048]{2,1,0:T(8,128)S(1)} %zonal_terms.3, ...), custom_call_target="tpu_custom_call" | custom-call | flops 2500000000 | bytes 8333333 | tf_op jit(solution)/shard_map/rest_fields/pallas_call | solution.py:491
  26.3 0.8 %last_update.1 = (f32[1,16,2048]{2,1,0:T(8,128)}, f32[2,16,2048]{2,1,0:T(8,128)}) custom-call(f32[3,16,2048]{2,1,0:T(8,128)S(1)} %rest_fields.1.fields, f32[1,16,2048]{2,1,0:T(8,128)S(1)} %collective-permute-done.10.levels, f32[1,16,2048]{2,1,0:T(8,128)S(1)} %collective-permute-done.11.others), custom_call_target="tpu_custom_call" | custom-call | tf_op jit(solution)/shard_map/last_update/pallas_call | solution.py:491
  (21 shorter events, 0.0 us)
Async XLA Ops:
  0.6 12.3 %collective-permute-start.3 = (f32[2,16,2048]{2,1,0:T(8,128)}, f32[2,16,2048]{2,1,0:T(8,128)S(1)}, u32[]{:S(2)}, u32[]{:S(2)}) collective-permute-start(f32[2,16,2048]{2,1,0:T(8,128)} %bitcast.4), channel_id=1, source_target_pairs={{0,16},{4,20},{8,24},{12,28},{16,0},{20,4},{24,8},{28,12},{1,17},{... | collective-permute-start | bytes 786440 | tf_op jit(solution)/shard_map/ppermute | solution.py:463
  2.2 2.8 %copy-start.8 = (f32[1,16,2048]{2,1,0:T(8,128)S(1)}, f32[1,16,2048]{2,1,0:T(8,128)}, u32[]{:S(2)}) copy-start(f32[1,16,2048]{2,1,0:T(8,128)} %param.10) | copy-start | bytes 393220
  2.2 9.4 %copy-start.1 = (bf16[256,512]{1,0:T(8,128)(2,1)S(1)}, bf16[256,512]{1,0:T(8,128)(2,1)}, u32[]{:S(2)}) copy-start(bf16[256,512]{1,0:T(8,128)(2,1)} %constant.19.clone.refs_1_.refs_6_) | copy-start | bytes 786436
  2.2 9.4 %copy-start.3 = (bf16[256,256]{1,0:T(8,128)(2,1)S(1)}, bf16[256,256]{1,0:T(8,128)(2,1)}, u32[]{:S(2)}) copy-start(bf16[256,256]{1,0:T(8,128)(2,1)} %constant.17.clone.low.refs_4_) | copy-start | bytes 393220
  2.2 9.4 %copy-start.4 = (f32[51,256]{1,0:T(8,128)S(1)}, f32[51,256]{1,0:T(8,128)}, u32[]{:S(2)}) copy-start(f32[51,256]{1,0:T(8,128)} %constant.22.clone.masks.refs_2_) | copy-start | bytes 156676
  2.2 9.4 %copy-start.5 = (f32[68,128]{1,0:T(8,128)S(1)}, f32[68,128]{1,0:T(8,128)}, u32[]{:S(2)}) copy-start(f32[68,128]{1,0:T(8,128)} %constant.21.clone.refs_2_.refs_1_) | copy-start | bytes 104452
  2.2 9.4 %copy-start.6 = (f32[34,128]{1,0:T(8,128)S(1)}, f32[34,128]{1,0:T(8,128)}, u32[]{:S(2)}) copy-start(f32[34,128]{1,0:T(8,128)} %constant.20.clone.twist.refs_0_) | copy-start | bytes 52228
  3.3 8.4 %copy-start = (bf16[256,512]{1,0:T(8,128)(2,1)S(1)}, bf16[256,512]{1,0:T(8,128)(2,1)}, u32[]{:S(2)}) copy-start(bf16[256,512]{1,0:T(8,128)(2,1)} %constant.18.clone.refs_0_.refs_5_) | copy-start | bytes 786436
  3.3 8.4 %copy-start.2 = (bf16[256,256]{1,0:T(8,128)(2,1)S(1)}, bf16[256,256]{1,0:T(8,128)(2,1)}, u32[]{:S(2)}) copy-start(bf16[256,256]{1,0:T(8,128)(2,1)} %constant.16.clone.high.refs_3_) | copy-start | bytes 393220
  3.4 3.6 %collective-permute-start.1 = (f32[8,2304]{1,0:T(8,128)S(1)}, f32[8,2304]{1,0:T(8,128)S(1)}, u32[]{:S(2)}, u32[]{:S(2)}) collective-permute-start(f32[8,2304]{1,0:T(8,128)S(1)} %get-tuple-element.20), channel_id=1, source_target_pairs={{0,4},{8,12},{16,20},{24,28},{4,0},{12,8},{20,16},{28,24},{1,5},{9... | collective-permute-start | bytes 221192 | tf_op jit(solution)/shard_map/ppermute | solution.py:458
  3.5 8.8 %collective-permute-start.2 = (f32[8,2304]{1,0:T(8,128)S(1)}, f32[8,2304]{1,0:T(8,128)S(1)}, u32[]{:S(2)}, u32[]{:S(2)}) collective-permute-start(f32[8,2304]{1,0:T(8,128)S(1)} %get-tuple-element.24), channel_id=1, source_target_pairs={{4,8},{12,16},{20,24},{28,0},{8,4},{16,12},{24,20},{0,28},{5,9},{1... | collective-permute-start | bytes 221192 | tf_op jit(solution)/shard_map/ppermute | solution.py:458
  5.0 9.6 %collective-permute-start = (f32[1,16,2048]{2,1,0:T(8,128)S(1)}, f32[1,16,2048]{2,1,0:T(8,128)S(1)}, u32[]{:S(2)}, u32[]{:S(2)}) collective-permute-start(f32[1,16,2048]{2,1,0:T(8,128)S(1)} %copy-done.8), channel_id=1, source_target_pairs={{0,16},{4,20},{8,24},{12,28},{16,0},{20,4},{24,8},{28,12},{1,17},{... | collective-permute-start | bytes 393224 | tf_op jit(solution)/shard_map/ppermute | solution.py:463
  6.6 8.1 %collective-permute-start.4 = (f32[1,16,2048]{2,1,0:T(8,128)S(1)}, f32[1,16,2048]{2,1,0:T(8,128)S(1)}, u32[]{:S(2)}, u32[]{:S(2)}) collective-permute-start(f32[1,16,2048]{2,1,0:T(8,128)S(1)} %copy-done.8), channel_id=1, source_target_pairs={{0,1},{2,3},{1,0},{3,2},{4,5},{6,7},{5,4},{7,6},{8,9},{10,11},{9,8... | collective-permute-start | bytes 393224 | tf_op jit(solution)/shard_map/ppermute | solution.py:458
  7.0 7.6 %collective-permute-start.5 = (f32[1,16,2048]{2,1,0:T(8,128)S(1)}, f32[1,16,2048]{2,1,0:T(8,128)S(1)}, u32[]{:S(2)}, u32[]{:S(2)}) collective-permute-start(f32[1,16,2048]{2,1,0:T(8,128)S(1)} %copy-done.8), channel_id=1, source_target_pairs={{1,2},{2,1},{5,6},{6,5},{9,10},{10,9},{13,14},{14,13},{17,18},{18,... | collective-permute-start | bytes 393224 | tf_op jit(solution)/shard_map/ppermute | solution.py:458
  11.7 0.7 %copy-start.7 = (f32[2,2048]{1,0:T(2,128)S(1)}, f32[2,2048]{1,0:T(2,128)}, u32[]{:S(2)}) copy-start(f32[2,2048]{1,0:T(2,128)} %constant.23.clone.rows) | copy-start | bytes 49156
  14.1 9.8 %collective-permute-start.9 = (f32[1,16,2048]{2,1,0:T(8,128)S(1)}, f32[1,16,2048]{2,1,0:T(8,128)S(1)}, u32[]{:S(2)}, u32[]{:S(2)}) collective-permute-start(f32[1,16,2048]{2,1,0:T(8,128)S(1)} %get-tuple-element.27.east_next.east), channel_id=1, source_target_pairs={{0,16},{4,20},{8,24},{12,28},{16,0},{20,4},{24,8},{28,12},{1,17},{... | collective-permute-start | bytes 393224 | tf_op jit(solution)/shard_map/ppermute | solution.py:463
  15.5 9.5 %collective-permute-start.6 = (f32[2,16,2048]{2,1,0:T(8,128)S(1)}, f32[2,16,2048]{2,1,0:T(8,128)S(1)}, u32[]{:S(2)}, u32[]{:S(2)}) collective-permute-start(f32[2,16,2048]{2,1,0:T(8,128)S(1)} %get-tuple-element.28.rest), channel_id=1, source_target_pairs={{0,16},{4,20},{8,24},{12,28},{16,0},{20,4},{24,8},{28,12},{1,17},{... | collective-permute-start | bytes 786440 | tf_op jit(solution)/shard_map/ppermute | solution.py:463
  17.1 1.3 %collective-permute-start.7 = (f32[8,2304]{1,0:T(8,128)S(1)}, f32[8,2304]{1,0:T(8,128)S(1)}, u32[]{:S(2)}, u32[]{:S(2)}) collective-permute-start(f32[8,2304]{1,0:T(8,128)S(1)} %get-tuple-element.29), channel_id=1, source_target_pairs={{0,4},{8,12},{16,20},{24,28},{4,0},{12,8},{20,16},{28,24},{1,5},{9... | collective-permute-start | bytes 221192 | tf_op jit(solution)/shard_map/ppermute | solution.py:458
  17.1 5.6 %collective-permute-start.8 = (f32[8,2304]{1,0:T(8,128)S(1)}, f32[8,2304]{1,0:T(8,128)S(1)}, u32[]{:S(2)}, u32[]{:S(2)}) collective-permute-start(f32[8,2304]{1,0:T(8,128)S(1)} %get-tuple-element.31), channel_id=1, source_target_pairs={{4,8},{12,16},{20,24},{28,0},{8,4},{16,12},{24,20},{0,28},{5,9},{1... | collective-permute-start | bytes 221192 | tf_op jit(solution)/shard_map/ppermute | solution.py:458
  17.8 8.4 %collective-permute-start.10 = (f32[1,16,2048]{2,1,0:T(8,128)S(1)}, f32[1,16,2048]{2,1,0:T(8,128)S(1)}, u32[]{:S(2)}, u32[]{:S(2)}) collective-permute-start(f32[1,16,2048]{2,1,0:T(8,128)S(1)} %get-tuple-element.35), channel_id=1, source_target_pairs={{0,1},{2,3},{1,0},{3,2},{4,5},{6,7},{5,4},{7,6},{8,9},{10,11},{9,8... | collective-permute-start | bytes 393224 | tf_op jit(solution)/shard_map/ppermute | solution.py:458
  18.4 7.9 %collective-permute-start.11 = (f32[1,16,2048]{2,1,0:T(8,128)S(1)}, f32[1,16,2048]{2,1,0:T(8,128)S(1)}, u32[]{:S(2)}, u32[]{:S(2)}) collective-permute-start(f32[1,16,2048]{2,1,0:T(8,128)S(1)} %get-tuple-element.35), channel_id=1, source_target_pairs={{1,2},{2,1},{5,6},{6,5},{9,10},{10,9},{13,14},{14,13},{17,18},{18,... | collective-permute-start | bytes 393224 | tf_op jit(solution)/shard_map/ppermute | solution.py:458
